TPU v7x, 32 devices: a whole 2x2x4 slice. The times are simulated.
32 devices in a mesh: sx: 8 (over y, x, core), sy: 4 (over z).
Axes of the slice: x: 2, y: 2, z: 4, core: 2. Of those that a mesh axis runs over, the one named last changes fastest.
Arguments:
- force: float32 [3, 64, 32, 256], P(None, 'sx', 'sy'), may hold values from -7.2 to 7.2
- load_mask: int32 [64, 32, 256], P('sx', 'sy'), may hold values 0 or 1
- support_mask: int32 [64, 32, 256], P('sx', 'sy'), may hold values 0 or 1
- start_field: float32 [3, 64, 32, 256], P(None, 'sx', 'sy'), may hold values from -7.2 to 7.2
- density: float32 [32, 16, 128], P('sx', 'sy'), may hold values from 0.1 to 1
- passive_mask: int32 [32, 16, 128], P('sx', 'sy'), may hold values 0 or 1
Outputs:
- displacement: float32 [3, 64, 32, 256], P(None, 'sx', 'sy')
- filtered: float32 [32, 16, 128], P('sx', 'sy')
- compliance: float32 [], replicated
All inputs are finite; a program needn't handle non-finite values. No bound on the sum of `load_mask` or of `support_mask` or of `passive_mask` on one device may be relied on, other than what follows from the above.
Results may differ from a plain program's by a relative error of at most 0.0003.
Values sent between devices are 32-bit elements; how exact they have to be, the bound alone decides.
No kernel may reach another device: no remote copies, remote signals or barrier semaphores. Data moves between devices by JAX's collectives and lax.ppermute only.
A program may use at most 128 MiB of HBM per device.

v0:
```python
import math

import jax
import jax.numpy as jnp
import numpy as np
from jax import lax
from jax.sharding import PartitionSpec as P

SWEEPS = 4


EMIN = 0.001
RADIUS = 1.5


def shifted(value, axis, steps):
    count = lax.axis_size(axis)
    first, last = (max(0, -steps), min(count, count - steps))
    return lax.ppermute(value, axis, [(source, source + steps) for source in range(first, last)])


def extended(x, sides, width):
    for axis, dim in sides:
        devices, length = (lax.axis_size(axis), x.shape[dim])
        up = [(i, (i + 1) % devices) for i in range(devices - 1)]
        down = [(j, i) for i, j in up]
        last = lax.slice_in_dim(x, length - width, length, axis=dim)
        first = lax.slice_in_dim(x, 0, width, axis=dim)
        before = lax.ppermute(last, axis, up)
        after = lax.ppermute(first, axis, down)
        x = jnp.concatenate([before, x, after], axis=dim)
    return x


def element_matrix():
    poisson = 0.3
    lame_first = poisson / ((1.0 + poisson) * (1.0 - 2.0 * poisson))
    shear = 1.0 / (2.0 * (1.0 + poisson))
    elastic = np.zeros((6, 6))
    elastic[:3, :3] = lame_first
    for entry in range(3):
        elastic[entry, entry] += 2.0 * shear
        elastic[entry + 3, entry + 3] = shear
    points = [-math.sqrt(0.6), 0.0, math.sqrt(0.6)]
    weights = [5.0 / 9.0, 8.0 / 9.0, 5.0 / 9.0]

    def values(point):
        return np.array(
            [point * (point - 1.0) / 2.0, 1.0 - point * point, point * (point + 1.0) / 2.0]
        )

    def slopes(point):
        return np.array([point - 0.5, -2.0 * point, point + 0.5])

    stiff = np.zeros((81, 81))
    for first in range(3):
        for second in range(3):
            for third in range(3):
                val_x, val_y, val_z = (
                    values(points[first]),
                    values(points[second]),
                    values(points[third]),
                )
                der_x, der_y, der_z = (
                    slopes(points[first]),
                    slopes(points[second]),
                    slopes(points[third]),
                )
                strain = np.zeros((6, 81))
                for node_a in range(3):
                    for node_b in range(3):
                        for node_c in range(3):
                            node = node_a * 9 + node_b * 3 + node_c
                            grad_x = 2.0 * der_x[node_a] * val_y[node_b] * val_z[node_c]
                            grad_y = 2.0 * val_x[node_a] * der_y[node_b] * val_z[node_c]
                            grad_z = 2.0 * val_x[node_a] * val_y[node_b] * der_z[node_c]
                            strain[0, node] = grad_x
                            strain[1, 27 + node] = grad_y
                            strain[2, 54 + node] = grad_z
                            strain[3, node] = grad_y
                            strain[3, 27 + node] = grad_x
                            strain[4, 27 + node] = grad_z
                            strain[4, 54 + node] = grad_y
                            strain[5, node] = grad_z
                            strain[5, 54 + node] = grad_x
                factor = weights[first] * weights[second] * weights[third] * 0.125
                stiff = stiff + factor * strain.T @ elastic @ strain
    return jnp.asarray(stiff.astype(np.float32))


def filter_weights():
    table = []
    for first in range(3):
        for second in range(3):
            for third in range(3):
                distance = math.sqrt((first - 1) ** 2 + (second - 1) ** 2 + (third - 1) ** 2)
                table.append(max(0.0, RADIUS - distance))
    return table


def split_parity(nodes, count_x, count_y, count_z):
    extra_x = 2 * count_x + 2 - nodes.shape[1]
    extra_y = 2 * count_y + 2 - nodes.shape[2]
    extra_z = 2 * count_z + 2 - nodes.shape[3]
    padded = jnp.pad(nodes, ((0, 0), (0, extra_x), (0, extra_y), (0, extra_z)))
    shaped = padded.reshape(3, count_x + 1, 2, count_y + 1, 2, count_z + 1, 2)
    return jnp.transpose(shaped, (0, 2, 4, 6, 1, 3, 5))


def element_vectors(nodes, count_x, count_y, count_z):
    planes = split_parity(nodes, count_x, count_y, count_z)
    pieces = []
    for comp in range(3):
        for node_a in range(3):
            for node_b in range(3):
                for node_c in range(3):
                    shift_a, shift_b, shift_c = (node_a // 2, node_b // 2, node_c // 2)
                    plane = planes[comp, node_a % 2, node_b % 2, node_c % 2]
                    pieces.append(
                        plane[
                            shift_a : shift_a + count_x,
                            shift_b : shift_b + count_y,
                            shift_c : shift_c + count_z,
                        ]
                    )
    return jnp.stack(pieces)


def element_scatter(products, count_x, count_y, count_z):
    sums = {}
    index = 0
    for comp in range(3):
        for node_a in range(3):
            for node_b in range(3):
                for node_c in range(3):
                    shift_a, shift_b, shift_c = (node_a // 2, node_b // 2, node_c // 2)
                    placed = jnp.pad(
                        products[index],
                        ((shift_a, 1 - shift_a), (shift_b, 1 - shift_b), (shift_c, 1 - shift_c)),
                    )
                    label = (comp, node_a % 2, node_b % 2, node_c % 2)
                    if label in sums:
                        sums[label] = sums[label] + placed
                    else:
                        sums[label] = placed
                    index += 1
    stacked = jnp.stack(
        [
            jnp.stack(
                [
                    jnp.stack(
                        [jnp.stack([sums[comp, pa, pb, pc] for pc in range(2)]) for pb in range(2)]
                    )
                    for pa in range(2)
                ]
            )
            for comp in range(3)
        ]
    )
    moved = jnp.transpose(stacked, (0, 4, 1, 5, 2, 6, 3))
    whole = moved.reshape(3, 2 * count_x + 2, 2 * count_y + 2, 2 * count_z + 2)
    return whole[:, : 2 * count_x + 1, : 2 * count_y + 1, : 2 * count_z + 1]


def multiply(stiff, vectors):
    return jnp.einsum("ij,jxyz->ixyz", stiff, vectors, precision=lax.Precision.HIGHEST)


def body(force, load_mask, support_mask, start_field, density, passive_mask):
    stiff = element_matrix()
    stiff_diag = jnp.diagonal(stiff)
    count_x, count_y, count_z = density.shape
    rho = jnp.where(passive_mask == 1, jnp.float32(1.0), density)
    young = EMIN + (1.0 - EMIN) * rho**3
    free = (1 - support_mask).astype(jnp.float32)[None]
    load = free * load_mask.astype(jnp.float32)[None] * force

    def fetch(field):
        upper_x = shifted(field[:, :1], "sx", -1)
        wider = jnp.concatenate([field, upper_x], 1)
        upper_y = shifted(wider[:, :, :1], "sy", -1)
        return jnp.concatenate([wider, upper_y], 2)

    def send_back(parts):
        parts = parts[:, :, :, : 2 * count_z]
        top_y = shifted(parts[:, :, 2 * count_y :], "sy", 1)
        parts = parts[:, :, : 2 * count_y].at[:, :, :1].add(top_y)
        top_x = shifted(parts[:, 2 * count_x :], "sx", 1)
        return parts[:, : 2 * count_x].at[:, :1].add(top_x)

    def stiff_apply(field):
        vectors = element_vectors(fetch(field), count_x, count_y, count_z)
        products = multiply(stiff, vectors) * young[None]
        return send_back(element_scatter(products, count_x, count_y, count_z))

    raw_diag = send_back(
        element_scatter(stiff_diag[:, None, None, None] * young[None], count_x, count_y, count_z)
    )
    diagonal = free * raw_diag + (1.0 - free)

    def operator(field):
        return free * stiff_apply(free * field) + (1.0 - free) * field

    displacement = free * start_field
    residual = load - operator(displacement)
    for sweep in range(SWEEPS):
        step = residual / diagonal
        image = operator(step)
        inner_ri, inner_ii = lax.psum(
            (jnp.sum(residual * image), jnp.sum(image * image)), ("sx", "sy")
        )
        omega = inner_ri / inner_ii
        displacement = displacement + omega * step
        residual = residual - omega * image
    vectors = element_vectors(fetch(displacement), count_x, count_y, count_z)
    energy = jnp.sum(vectors * multiply(stiff, vectors), axis=0)
    compliance = lax.psum(jnp.sum(young * energy), ("sx", "sy"))
    sens = jnp.where(passive_mask == 1, jnp.float32(0.0), -3.0 * (1.0 - EMIN) * rho**2 * energy)
    rim = extended(sens, (("sx", 0), ("sy", 1)), 1)
    rim = jnp.pad(rim, ((0, 0), (0, 0), (1, 1)))
    index_x = lax.axis_index("sx")
    index_y = lax.axis_index("sy")
    last_x = lax.axis_size("sx") - 1
    last_y = lax.axis_size("sy") - 1
    place_x = jnp.arange(count_x + 2, dtype=jnp.int32)
    place_y = jnp.arange(count_y + 2, dtype=jnp.int32)
    valid_x = jnp.logical_not(
        (index_x == 0) & (place_x == 0) | (index_x == last_x) & (place_x == count_x + 1)
    ).astype(jnp.float32)
    valid_y = jnp.logical_not(
        (index_y == 0) & (place_y == 0) | (index_y == last_y) & (place_y == count_y + 1)
    ).astype(jnp.float32)
    covered = (
        valid_x[:, None, None] * valid_y[None, :, None] * jnp.ones((1, 1, count_z), jnp.float32)
    )
    covered = jnp.pad(covered, ((0, 0), (0, 0), (1, 1)))
    table = filter_weights()
    upper = jnp.zeros_like(sens)
    lower = jnp.zeros_like(sens)
    index = 0
    for first in range(3):
        for second in range(3):
            for third in range(3):
                if table[index] > 0.0:
                    upper = (
                        upper
                        + table[index]
                        * rim[
                            first : first + count_x,
                            second : second + count_y,
                            third : third + count_z,
                        ]
                    )
                    lower = (
                        lower
                        + table[index]
                        * covered[
                            first : first + count_x,
                            second : second + count_y,
                            third : third + count_z,
                        ]
                    )
                index += 1
    return (displacement, upper / lower, compliance)


def solution(mesh):
    in_specs = (
        P(None, "sx", "sy", None),
        P("sx", "sy", None),
        P("sx", "sy", None),
        P(None, "sx", "sy", None),
        P("sx", "sy", None),
        P("sx", "sy", None),
    )
    out_specs = (P(None, "sx", "sy", None), P("sx", "sy", None), P())
    return jax.shard_map(body, mesh=mesh, in_specs=in_specs, out_specs=out_specs, check_vma=False)
```

profile of v0, /device:TPU:0, one launch (start us, length us, event | category | flops | bytes accessed | tf_op | source)
XLA Modules:
  0.0 742.5 jit_solution(14915022687178406251)
XLA Ops:
  9.5 11.8 %copy.1059 = f32[3,5,2,5,2,129,2]{6,5,0,4,3,2,1:T(8,128)} copy(f32[3,5,2,5,2,129,2]{5,3,1,6,4,2,0:T(8,128)S(1)} %maximum_bitcast_fusion.1) | data formatting | bytes 619200 | tf_op jit(solution)/shard_map/transpose | solution.py:160
  21.3 13.3 %reshape.506 = f32[3,10,10,258]{3,0,2,1:T(4,128)S(1)} reshape(f32[3,5,2,5,2,129,2]{6,5,0,4,3,2,1:T(8,128)} %copy.1059) | data formatting | bytes 619200 | tf_op jit(solution)/shard_map/reshape | solution.py:161
  34.6 4.9 collective-permute-start.4
  41.0 4.7 collective-permute-done.1
  45.8 11.3 %reshape.504 = f32[3,5,2,5,2,129,2]{6,5,0,4,3,2,1:T(8,128)} reshape(f32[3,10,10,258]{3,0,2,1:T(4,128)S(1)} %select_maximum_fusion.10) | data formatting | bytes 619200 | tf_op jit(solution)/shard_map/reshape | solution.py:106
  57.1 23.4 %copy.897 = f32[3,5,2,5,2,129,2]{5,3,1,6,4,2,0:T(8,128)S(1)} copy(f32[3,5,2,5,2,129,2]{6,5,0,4,3,2,1:T(8,128)} %reshape.504) | data formatting | bytes 619200 | tf_op jit(solution)/shard_map/reshape | solution.py:106
  85.9 11.8 %copy.1058 = f32[3,5,2,5,2,129,2]{6,5,0,4,3,2,1:T(8,128)} copy(f32[3,5,2,5,2,129,2]{5,3,1,6,4,2,0:T(8,128)S(1)} %maximum_bitcast_fusion) | data formatting | bytes 619200 | tf_op jit(solution)/shard_map/transpose | solution.py:160
  97.7 13.3 %reshape.505 = f32[3,10,10,258]{3,0,2,1:T(4,128)S(1)} reshape(f32[3,5,2,5,2,129,2]{6,5,0,4,3,2,1:T(8,128)} %copy.1058) | data formatting | bytes 619200 | tf_op jit(solution)/shard_map/reshape | solution.py:161
  126.4 4.6 collective-permute-done.7
  131.0 11.3 %reshape.507 = f32[3,5,2,5,2,129,2]{6,5,0,4,3,2,1:T(8,128)} reshape(f32[3,10,10,258]{3,0,2,1:T(4,128)S(1)} %select_maximum_fusion.8) | data formatting | bytes 619200 | tf_op jit(solution)/shard_map/reshape | solution.py:106
  142.3 23.4 %copy.1060 = f32[3,5,2,5,2,129,2]{5,3,1,6,4,2,0:T(8,128)S(1)} copy(f32[3,5,2,5,2,129,2]{6,5,0,4,3,2,1:T(8,128)} %reshape.507) | data formatting | bytes 619200 | tf_op jit(solution)/shard_map/reshape | solution.py:106
  171.2 11.8 %copy.1221 = f32[3,5,2,5,2,129,2]{6,5,0,4,3,2,1:T(8,128)} copy(f32[3,5,2,5,2,129,2]{5,3,1,6,4,2,0:T(8,128)S(1)} %maximum_bitcast_fusion.2) | data formatting | bytes 619200 | tf_op jit(solution)/shard_map/transpose | solution.py:160
  183.0 13.3 %reshape.508 = f32[3,10,10,258]{3,0,2,1:T(4,128)S(1)} reshape(f32[3,5,2,5,2,129,2]{6,5,0,4,3,2,1:T(8,128)} %copy.1221) | data formatting | bytes 619200 | tf_op jit(solution)/shard_map/reshape | solution.py:161
  206.3 45.6 %all-reduce.497 = (f32[]{:T(128)}, f32[]{:T(128)}) all-reduce(f32[]{:T(128)} %get-tuple-element.157, f32[]{:T(128)} %get-tuple-element.156), channel_id=1, replica_groups=mesh['sx'=8,'sy'=4] {'sx','sy'}, use_global_device_ids=true, to_apply=%region_1.2 | all-reduce | flops 2 | bytes 16 | tf_op jit(solution)/shard_map/psum | solution.py:209
  262.5 11.3 %reshape.509 = f32[3,5,2,5,2,129,2]{6,5,0,4,3,2,1:T(8,128)} reshape(f32[3,10,10,258]{3,0,2,1:T(4,128)S(1)} %select_maximum_fusion.6) | data formatting | bytes 619200 | tf_op jit(solution)/shard_map/reshape | solution.py:106
  273.7 23.4 %copy.1222 = f32[3,5,2,5,2,129,2]{5,3,1,6,4,2,0:T(8,128)S(1)} copy(f32[3,5,2,5,2,129,2]{6,5,0,4,3,2,1:T(8,128)} %reshape.509) | data formatting | bytes 619200 | tf_op jit(solution)/shard_map/reshape | solution.py:106
  302.7 11.8 %copy.1383 = f32[3,5,2,5,2,129,2]{6,5,0,4,3,2,1:T(8,128)} copy(f32[3,5,2,5,2,129,2]{5,3,1,6,4,2,0:T(8,128)S(1)} %maximum_bitcast_fusion.3) | data formatting | bytes 619200 | tf_op jit(solution)/shard_map/transpose | solution.py:160
  314.5 13.3 %reshape.510 = f32[3,10,10,258]{3,0,2,1:T(4,128)S(1)} reshape(f32[3,5,2,5,2,129,2]{6,5,0,4,3,2,1:T(8,128)} %copy.1383) | data formatting | bytes 619200 | tf_op jit(solution)/shard_map/reshape | solution.py:161
  335.8 44.8 %all-reduce.496 = (f32[]{:T(128)}, f32[]{:T(128)}) all-reduce(f32[]{:T(128)} %get-tuple-element.155, f32[]{:T(128)} %get-tuple-element.154), channel_id=1, replica_groups=mesh['sx'=8,'sy'=4] {'sx','sy'}, use_global_device_ids=true, to_apply=%region_5.6 | all-reduce | flops 2 | bytes 16 | tf_op jit(solution)/shard_map/psum | solution.py:209
  391.2 11.3 %reshape.511 = f32[3,5,2,5,2,129,2]{6,5,0,4,3,2,1:T(8,128)} reshape(f32[3,10,10,258]{3,0,2,1:T(4,128)S(1)} %select_maximum_fusion.4) | data formatting | bytes 619200 | tf_op jit(solution)/shard_map/reshape | solution.py:106
  402.5 23.4 %copy.1384 = f32[3,5,2,5,2,129,2]{5,3,1,6,4,2,0:T(8,128)S(1)} copy(f32[3,5,2,5,2,129,2]{6,5,0,4,3,2,1:T(8,128)} %reshape.511) | data formatting | bytes 619200 | tf_op jit(solution)/shard_map/reshape | solution.py:106
  431.4 11.8 %copy.1545 = f32[3,5,2,5,2,129,2]{6,5,0,4,3,2,1:T(8,128)} copy(f32[3,5,2,5,2,129,2]{5,3,1,6,4,2,0:T(8,128)S(1)} %maximum_bitcast_fusion.4) | data formatting | bytes 619200 | tf_op jit(solution)/shard_map/transpose | solution.py:160
  443.2 13.3 %reshape.512 = f32[3,10,10,258]{3,0,2,1:T(4,128)S(1)} reshape(f32[3,5,2,5,2,129,2]{6,5,0,4,3,2,1:T(8,128)} %copy.1545) | data formatting | bytes 619200 | tf_op jit(solution)/shard_map/reshape | solution.py:161
  464.6 44.4 %all-reduce.495 = (f32[]{:T(128)}, f32[]{:T(128)}) all-reduce(f32[]{:T(128)} %get-tuple-element.153, f32[]{:T(128)} %get-tuple-element.152), channel_id=1, replica_groups=mesh['sx'=8,'sy'=4] {'sx','sy'}, use_global_device_ids=true, to_apply=%region_9.10 | all-reduce | flops 2 | bytes 16 | tf_op jit(solution)/shard_map/psum | solution.py:209
  519.6 11.3 %reshape.513 = f32[3,5,2,5,2,129,2]{6,5,0,4,3,2,1:T(8,128)} reshape(f32[3,10,10,258]{3,0,2,1:T(4,128)S(1)} %select_maximum_fusion.2) | data formatting | bytes 619200 | tf_op jit(solution)/shard_map/reshape | solution.py:106
  530.9 23.4 %copy.1546 = f32[3,5,2,5,2,129,2]{5,3,1,6,4,2,0:T(8,128)S(1)} copy(f32[3,5,2,5,2,129,2]{6,5,0,4,3,2,1:T(8,128)} %reshape.513) | data formatting | bytes 619200 | tf_op jit(solution)/shard_map/reshape | solution.py:106
  559.8 11.8 %copy.1707 = f32[3,5,2,5,2,129,2]{6,5,0,4,3,2,1:T(8,128)} copy(f32[3,5,2,5,2,129,2]{5,3,1,6,4,2,0:T(8,128)S(1)} %maximum_bitcast_fusion.5) | data formatting | bytes 619200 | tf_op jit(solution)/shard_map/transpose | solution.py:160
  571.6 13.3 %reshape.514 = f32[3,10,10,258]{3,0,2,1:T(4,128)S(1)} reshape(f32[3,5,2,5,2,129,2]{6,5,0,4,3,2,1:T(8,128)} %copy.1707) | data formatting | bytes 619200 | tf_op jit(solution)/shard_map/reshape | solution.py:161
  592.9 44.4 %all-reduce.494 = (f32[]{:T(128)}, f32[]{:T(128)}) all-reduce(f32[]{:T(128)} %get-tuple-element.151, f32[]{:T(128)} %get-tuple-element.150), channel_id=1, replica_groups=mesh['sx'=8,'sy'=4] {'sx','sy'}, use_global_device_ids=true, to_apply=%region_13.14 | all-reduce | flops 2 | bytes 16 | tf_op jit(solution)/shard_map/psum | solution.py:209
  648.1 11.3 %reshape.515 = f32[3,5,2,5,2,129,2]{6,5,0,4,3,2,1:T(8,128)} reshape(f32[3,10,10,258]{3,0,2,1:T(4,128)S(1)} %select_maximum_fusion) | data formatting | bytes 619200 | tf_op jit(solution)/shard_map/reshape | solution.py:106
  659.4 23.4 %copy.1708 = f32[3,5,2,5,2,129,2]{5,3,1,6,4,2,0:T(8,128)S(1)} copy(f32[3,5,2,5,2,129,2]{6,5,0,4,3,2,1:T(8,128)} %reshape.515) | data formatting | bytes 619200 | tf_op jit(solution)/shard_map/reshape | solution.py:106
  696.7 44.6 %psum.71 = f32[]{:T(128)} all-reduce(f32[]{:T(128)} %get-tuple-element.1286), channel_id=1, replica_groups=mesh['sx'=8,'sy'=4] {'sx','sy'}, use_global_device_ids=true, to_apply=%region_18.19 | all-reduce | flops 1 | bytes 8 | tf_op jit(solution)/shard_map/psum | solution.py:217
  (601 shorter events, 135.8 us)
Async XLA Ops:
  2.6 37.0 %collective-permute-start = (f32[3,1,8,256]{3,0,2,1:T(4,128)S(1)}, f32[3,1,8,256]{3,0,2,1:T(4,128)S(1)}, u32[]{:S(2)}, u32[]{:S(2)}) collective-permute-start(f32[3,1,8,256]{3,0,2,1:T(4,128)S(1)} %slice.5557), channel_id=1, source_target_pairs={{4,0},{8,4},{12,8},{16,12},{20,16},{24,20},{28,24},{5,1},{9,5},{13... | collective-permute-start | bytes 73736 | tf_op jit(solution)/shard_map/ppermute | solution.py:19
  34.6 79.9 %collective-permute-start.4 = (f32[3,9,1,256]{3,0,2,1:T(4,128)S(1)}, f32[3,9,1,256]{3,0,2,1:T(4,128)S(1)}, u32[]{:S(2)}, u32[]{:S(2)}) collective-permute-start(f32[3,9,1,256]{3,0,2,1:T(4,128)S(1)} %slice.5833), channel_id=1, source_target_pairs={{0,1},{1,2},{2,3},{4,5},{5,6},{6,7},{8,9},{9,10},{10,11},{12,13},{... | collective-permute-start | bytes 82952 | tf_op jit(solution)/shard_map/ppermute | solution.py:19
  39.6 6.1 collective-permute-start.1
  45.8 36.8 %copy-start.1 = (f32[81,81,1,1]{1,0,3,2:T(8,128)S(1)}, f32[81,81,1,1]{1,0,3,2:T(8,128)}, u32[]{:S(2)}) copy-start(f32[81,81,1,1]{1,0,3,2:T(8,128)} %constant.1301) | copy-start | bytes 78736
  85.9 35.5 %copy-start = (f32[3,8,8,256]{3,2,1,0:T(8,128)S(1)}, f32[3,8,8,256]{3,2,1,0:T(8,128)}, u32[]{:S(2)}) copy-start(f32[3,8,8,256]{3,2,1,0:T(8,128)} %param.34) | copy-start | bytes 589828
  111.1 5.3 collective-permute-start.2
  114.7 6.1 collective-permute-start.5
  116.4 5.0 collective-permute-start.3
  121.9 3.1 collective-permute-start.6
  125.1 5.9 collective-permute-start.7
  196.4 5.1 collective-permute-start.8
  201.5 3.9 collective-permute-start.9
  253.4 3.1 collective-permute-start.10
  256.5 5.9 collective-permute-start.11
  327.8 3.5 collective-permute-start.12
  331.4 3.5 collective-permute-start.13
  382.2 3.1 collective-permute-start.14
  385.3 5.9 collective-permute-start.15
  456.6 3.5 collective-permute-start.16
  460.1 3.5 collective-permute-start.17
  510.5 3.1 collective-permute-start.18
  513.6 5.9 collective-permute-start.19
  584.9 3.5 collective-permute-start.20
  588.5 3.5 collective-permute-start.21
  639.0 3.1 collective-permute-start.22
  642.1 5.9 collective-permute-start.23
  648.1 37.7 %copy-start.5 = (f32[4,4,128]{2,1,0:T(4,128)S(1)}, f32[4,4,128]{2,1,0:T(4,128)}, u32[]{:S(2)}) copy-start(f32[4,4,128]{2,1,0:T(4,128)} %param.35) | copy-start | bytes 24580
  648.1 37.7 %copy-start.6 = (pred[4,4,128]{2,1,0:T(4,128)(4,1)S(1)}, pred[4,4,128]{2,1,0:T(4,128)(4,1)}, u32[]{:S(2)}) copy-start(pred[4,4,128]{2,1,0:T(4,128)(4,1)} %get-tuple-element.181) | copy-start | bytes 6148
  686.4 5.5 collective-permute-start.25
  687.7 5.0 collective-permute-start.24
  692.7 48.6 %collective-permute-start.26 = (f32[6,1,128]{2,1,0:T(1,128)S(1)}, f32[6,1,128]{2,1,0:T(1,128)S(1)}, u32[]{:S(2)}, u32[]{:S(2)}) collective-permute-start(f32[6,1,128]{2,1,0:T(1,128)S(1)} %get-tuple-element.1284), channel_id=1, source_target_pairs={{0,1},{1,2},{2,3},{4,5},{5,6},{6,7},{8,9},{9,10},{10,11},{12,13},{... | collective-permute-start | bytes 9224 | tf_op jit(solution)/shard_map/ppermute | solution.py:29
  694.6 46.7 %collective-permute-start.27 = (f32[6,1,128]{2,1,0:T(1,128)S(1)}, f32[6,1,128]{2,1,0:T(1,128)S(1)}, u32[]{:S(2)}, u32[]{:S(2)}) collective-permute-start(f32[6,1,128]{2,1,0:T(1,128)S(1)} %get-tuple-element.1285), channel_id=1, source_target_pairs={{1,0},{2,1},{3,2},{5,4},{6,5},{7,6},{9,8},{10,9},{11,10},{13,12},{... | collective-permute-start | bytes 9224 | tf_op jit(solution)/shard_map/ppermute | solution.py:30
  (3 other events, 98.4 us)
where the time goes:
time: 753 us; the launch traced here: 743 us
  local copies, waits for them, and re-layouts  378 us (50%)
  blocking collectives  224 us (30%)
  starting transfers between devices  59.8 us (8%)
  waiting for transfers between devices  46.1 us (6%)
  other arithmetic  20.3 us (3%)
  between operations  9.75 us (1%)
    reshape x12, local copies, waits for them, and re-layouts, split_parity(): shaped = padded.reshape(3, count_x + 1, 2, count_y + 1, 2, count_z + 1, 2)  208 us
    psum x4, blocking collectives, body(): lax.psum((jnp.sum(residual * image), jnp.sum(image * image)), ('sx', 'sy'))  179 us
    reshape x6, local copies, waits for them, and re-layouts, element_scatter(): whole = moved.reshape(3, 2 * count_x + 2, 2 * count_y + 2, 2 * count_z + 2)  80 us
    transpose x6, local copies, waits for them, and re-layouts, element_scatter(): moved = jnp.transpose(stacked, (0, 4, 1, 5, 2, 6, 3))  70.7 us
    ppermute x24, starting transfers between devices, shifted(): lax.ppermute(value, axis, [(source, source + steps) for source in range(f...  51.2 us
    ppermute x24, waiting for transfers between devices, shifted(): lax.ppermute(value, axis, [(source, source + steps) for source in range(f...  45.4 us
    psum x1, blocking collectives, body(): compliance = lax.psum(jnp.sum(young * energy), ('sx', 'sy'))  44.6 us
  transfers between devices with their start and end apart: 28, of which 21 were waited for; matrix products, arithmetic and copies ran while one was open for 13% of the time, Pallas kernels for 0%

commit v1 on v0

v1 whole, which is shorter than its diff:
```python
import functools
import math

import jax
import jax.numpy as jnp
import numpy as np
from jax import lax
from jax.experimental import pallas as pl
from jax.experimental.pallas import tpu as pltpu
from jax.sharding import PartitionSpec as P

SWEEPS = 4
EMIN = 0.001
RADIUS = 1.5

OWN = 8
ELEMS = OWN // 2
HALO_U = 5
HALO_F = 3
HALO_Z = 7
PARTS = [
    (0, None),
    (1, None),
    (None, 0),
    (None, 1),
    (0, 0),
    (0, 1),
    (1, 0),
    (1, 1),
]
UP_X, UP_Y, LOW_X, HIGH_X, LOW_Y, HIGH_Y = range(6)
F32 = jnp.float32
BF16 = jnp.bfloat16


def element_matrix():
    poisson = 0.3
    lame_first = poisson / ((1.0 + poisson) * (1.0 - 2.0 * poisson))
    shear = 1.0 / (2.0 * (1.0 + poisson))
    elastic = np.zeros((6, 6))
    elastic[:3, :3] = lame_first
    for entry in range(3):
        elastic[entry, entry] += 2.0 * shear
        elastic[entry + 3, entry + 3] = shear
    points = [-math.sqrt(0.6), 0.0, math.sqrt(0.6)]
    weights = [5.0 / 9.0, 8.0 / 9.0, 5.0 / 9.0]

    def values(point):
        return np.array(
            [point * (point - 1.0) / 2.0, 1.0 - point * point, point * (point + 1.0) / 2.0]
        )

    def slopes(point):
        return np.array([point - 0.5, -2.0 * point, point + 0.5])

    stiff = np.zeros((81, 81))
    for first in range(3):
        for second in range(3):
            for third in range(3):
                val_x, val_y, val_z = (
                    values(points[first]),
                    values(points[second]),
                    values(points[third]),
                )
                der_x, der_y, der_z = (
                    slopes(points[first]),
                    slopes(points[second]),
                    slopes(points[third]),
                )
                strain = np.zeros((6, 81))
                for node_a in range(3):
                    for node_b in range(3):
                        for node_c in range(3):
                            node = node_a * 9 + node_b * 3 + node_c
                            grad_x = 2.0 * der_x[node_a] * val_y[node_b] * val_z[node_c]
                            grad_y = 2.0 * val_x[node_a] * der_y[node_b] * val_z[node_c]
                            grad_z = 2.0 * val_x[node_a] * val_y[node_b] * der_z[node_c]
                            strain[0, node] = grad_x
                            strain[1, 27 + node] = grad_y
                            strain[2, 54 + node] = grad_z
                            strain[3, node] = grad_y
                            strain[3, 27 + node] = grad_x
                            strain[4, 27 + node] = grad_z
                            strain[4, 54 + node] = grad_y
                            strain[5, node] = grad_z
                            strain[5, 54 + node] = grad_x
                factor = weights[first] * weights[second] * weights[third] * 0.125
                stiff = stiff + factor * strain.T @ elastic @ strain
    return stiff.astype(np.float32)


def operator_matrix(stiff):
    hi = stiff.astype(BF16).astype(np.float32)
    parts = (hi, stiff - hi)
    out = np.zeros((2, 120, 256), np.float32)

    def out_row(comp, a, b, c):
        if c < 2:
            return (a * 3 + b) * 8 + c * 3 + comp
        return 72 + (a * 2 + b // 2) * 8 + (b % 2) * 3 + comp

    def in_row(comp, a, b, c, low):
        if c < 2:
            return (a * 3 + b) * 16 + low * 8 + c * 3 + comp
        return 144 + (a * 2 + b // 2) * 16 + (b % 2) * 8 + low * 3 + comp

    index = [(p, a, b, c) for p in range(3) for a in range(3) for b in range(3) for c in range(3)]
    for i, first in enumerate(index):
        for j, second in enumerate(index):
            row = out_row(*first)
            out[0, row, in_row(*second, 0)] = parts[0][i, j]
            out[0, row, in_row(*second, 1)] = parts[0][i, j]
            out[1, row, in_row(*second, 0)] = parts[1][i, j]
    return out.reshape(240, 256).astype(BF16)


def diagonal_columns(stiff):
    out = np.zeros((4, 8, 128), np.float32)
    for pa in range(2):
        for pb in range(2):
            for c in range(2):
                for comp in range(3):
                    dof = comp * 27 + pa * 9 + pb * 3 + c
                    out[pa * 2 + pb, c * 3 + comp] = stiff[dof, dof]
    return out


def iota(shape, dim):
    return lax.broadcasted_iota(jnp.int32, shape, dim)


def parity_matrix(transposed):
    node = iota((256, 256), 1 if transposed else 0)
    place = iota((256, 256), 0 if transposed else 1)
    return (node == 2 * (place % 128) + place // 128).astype(F32).astype(BF16)


def exact_product(rows, matrix):
    first = rows.astype(BF16)
    left = rows - first.astype(F32)
    second = left.astype(BF16)
    third = (left - second.astype(F32)).astype(BF16)
    stacked = jnp.concatenate([first, second, third], axis=0)
    out = jnp.dot(stacked, matrix, preferred_element_type=F32)
    count = rows.shape[0]
    return out[:count] + out[count : 2 * count] + out[2 * count :]


def span(k, up, width):
    if k is None:
        return 0, OWN
    upward = up if k == 0 else 1 - up
    return upward * (OWN - width), width


def landing(k, up, width):
    if k is None:
        return width, OWN
    upward = up if k == 0 else 1 - up
    return upward * (OWN + width), width


def rows8(start):
    return pl.multiple_of(start * 8, 8) if not isinstance(start, int) else start * 8


def part_shape(part, width):
    return [OWN if k is None else width for k in part]


def take(ref, part, flags, width):
    sx, nx = span(part[0], flags[UP_X], width)
    sy, ny = span(part[1], flags[UP_Y], width)
    return ref[pl.ds(sx, nx), pl.ds(rows8(sy), ny * 8), :].reshape(nx * ny * 8, 128)


def place(ref, value, part, flags, width):
    dx, nx = landing(part[0], flags[UP_X], width)
    dy, ny = landing(part[1], flags[UP_Y], width)
    valid = present(part[0], flags, 0) * present(part[1], flags, 1)
    value = value * valid.astype(F32) if not isinstance(valid, int) else value
    ref[pl.ds(dx, nx), pl.ds(rows8(dy), ny * 8), :] = value.reshape(nx, ny * 8, 128)


def present(k, flags, dim):
    if k is None:
        return 1
    up, low, high = flags[(UP_X, UP_Y)[dim]], flags[(LOW_X, LOW_Y)[dim]], flags[(HIGH_X, HIGH_Y)[dim]]
    upward = up if k == 0 else 1 - up
    return upward * high + (1 - upward) * low


def young_place(e):
    return (e if e <= 2 else 7 if e == 3 else e + 4) + HALO_F


def split_store(z, x, s_ref, t_ref):
    count = z.shape[0]
    hi = z.astype(BF16).astype(F32)
    lo = z - hi
    s_ref[x, : count * 16, :] = jnp.concatenate([hi, lo], axis=1).astype(BF16).reshape(count * 16, 128)
    row = iota(z.shape, 1)
    nxt = next_even(jnp.where(row < 3, hi, pltpu.roll(lo, 3, 1)))
    if count % 2:
        nxt = jnp.concatenate([nxt, nxt[count - 1 :]], axis=0)
        count += 1
    t_ref[x, : count * 8, :] = nxt.reshape(count // 2, 16, 128).astype(BF16).reshape(count * 8, 128)


def next_even(z):
    count = z.shape[0]
    moved = pltpu.roll(z.reshape(count * 8, 128), 127, 1)
    return jnp.where(iota(moved.shape, 1) < 127, moved, 0.0).reshape(count, 8, 128)


def element_operand(s_ref, t_ref, x, y, pair):
    pieces = [s_ref[x + a, pl.ds(y * 16, 48), :] for a in range(3)]
    pieces += [t_ref[x + a, pl.ds(pair * 16, 32), :] for a in range(3)]
    pieces.append(jnp.zeros((16, 128), BF16))
    return jnp.concatenate(pieces, axis=0)


def products(matrix_ref, s_ref, t_ref, x, j):
    operand = jnp.concatenate(
        [element_operand(s_ref, t_ref, x, 2 * e, e) for e in (j, j + 1)], axis=1
    )
    out = jnp.dot(matrix_ref[...], operand, preferred_element_type=F32)
    out = out[:120] + out[120:]
    return out[:, :128], out[:, 128:]


def apply(matrix_ref, s_ref, t_ref, young_ref, w_ref, o_ref, count_x, pairs_y, young_at):
    w_ref[: 2 * count_x + 1] = jnp.zeros((2 * count_x + 1,) + w_ref.shape[1:], F32)
    o_ref[: 2 * count_x + 1] = jnp.zeros((2 * count_x + 1,) + o_ref.shape[1:], F32)

    def row(i, carry):
        for j in range(0, 2 * pairs_y, 2):
            both = products(matrix_ref, s_ref, t_ref, 2 * i, j)
            for e in range(2):
                k = j + e
                out = both[e] * young_ref[i + young_at, k + young_at : k + young_at + 1, :]
                for a in range(3):
                    w_ref[2 * i + a, 16 * k : 16 * k + 24, :] += out[24 * a : 24 * a + 24]
                    o_ref[2 * i + a, 8 * k : 8 * k + 16, :] += out[72 + 16 * a : 88 + 16 * a]
        return carry

    lax.fori_loop(0, count_x, row, 0)


def collect(w_ref, o_ref, x, low, count):
    half = (count + 1) // 2
    moved = pltpu.roll(o_ref[x, 4 * low : 4 * low + 8 * half, :], 1, 1)
    moved = jnp.where(iota(moved.shape, 1) > 0, moved, 0.0).reshape(half, 8, 128)
    row = iota(moved.shape, 1)
    even = jnp.where(row < 3, moved, 0.0)
    odd = jnp.where(row < 3, pltpu.roll(moved, 5, 1), 0.0)
    both = jnp.stack([even, odd], axis=1).reshape(2 * half, 8, 128)[:count]
    return w_ref[x, 8 * low : 8 * (low + count), :].reshape(count, 8, 128) + both


def load_columns(ref, x, low, count):
    return ref[x, 8 * low : 8 * (low + count), :].reshape(count, 8, 128)


def store_columns(ref, x, value):
    ref[x, : 8 * value.shape[0], :] = value.reshape(8 * value.shape[0], 128)


def prepare_kernel(flags, force, load_mask, support, start, density, passive, u_ref, f_ref, *sends):
    matrix = parity_matrix(False)
    rho = jnp.where(passive[...] == 1, 1.0, density[...])
    young = EMIN + (1.0 - EMIN) * rho * rho * rho
    factor = jnp.where(passive[...] == 1, 0.0, -3.0 * (1.0 - EMIN) * rho * rho)
    for x in range(OWN):
        free = (1 - support[x]).astype(F32)
        loaded = free * load_mask[x].astype(F32)
        rows = [free * start[c, x] for c in range(3)] + [loaded * force[c, x] for c in range(3)] + [free]
        split = exact_product(jnp.concatenate(rows, axis=0), matrix)
        for index in range(7):
            ref, row = ((u_ref, index), (f_ref, index - 3), (u_ref, 6))[index // 3]
            step = 1 if index == 6 else 3
            for parity in range(2):
                ref[x, pl.ds(row + parity * step, 8, stride=8), :] = split[
                    8 * index : 8 * index + 8, 128 * parity : 128 * parity + 128
                ]
        element = {0: 0, 1: 1, 2: 2, 5: 1, 6: 2, 7: 3}.get(x)
        for row, values in ((6, young), (7, factor)):
            if element is None:
                column = jnp.zeros((8, 128), F32)
            else:
                column = jnp.concatenate(
                    [values[element, :3], jnp.zeros((2, 128), F32), values[element, 1:]], axis=0
                )
            f_ref[x, pl.ds(row, 8, stride=8), :] = column
    for part, send in zip(PARTS, sends):
        first = take(u_ref, part, flags, HALO_U)
        send[: first.shape[0], :] = first
        send[first.shape[0] :, :] = take(f_ref, part, flags, HALO_F)


def first_kernel(flags, matrix, diag, u_own, f_own, *rest):
    received, rest = rest[:8], rest[8:]
    (z0_ref, u_ref, dinv, young, factor, w0_ref, w1_ref, z1_ref), rest = rest[:8], rest[8:]
    sends, (u_reg, f_reg, s_ref, t_ref, w_ref, o_ref) = rest[:8], rest[8:]
    u_reg[HALO_U : HALO_U + OWN, 8 * HALO_U : 8 * (HALO_U + OWN), :] = u_own[...]
    f_reg[HALO_F : HALO_F + OWN, 8 * HALO_F : 8 * (HALO_F + OWN), :] = f_own[...]
    for part, value in zip(PARTS, received):
        nx, ny = part_shape(part, HALO_U)
        place(u_reg, value[: nx * ny * 8, :], part, flags, HALO_U)
        place(f_reg, value[nx * ny * 8 :, :], part, flags, HALO_F)
    zero = jnp.zeros((1, 128), F32)
    for e in range(-3, 7):
        rows = [f_reg[young_place(e), 8 * young_place(f) + 6 : 8 * young_place(f) + 7, :] for f in range(-3, 7)]
        young[e + 3] = jnp.concatenate(rows + [zero] * 6, axis=0)
    for e in range(-1, 5):
        rows = [f_reg[young_place(e), 8 * young_place(f) + 7 : 8 * young_place(f) + 8, :] for f in range(-1, 5)]
        factor[e + 1] = jnp.concatenate(rows + [zero] * 2, axis=0)

    def inverse(x, pa, near):
        free = load_columns(u_reg, x + 1, 1, 17)
        below = jnp.concatenate([jnp.zeros((1, 128), F32), near[:15]], axis=0)
        sums = (near + below, near)
        cols = []
        for y in range(17):
            pb, f = y % 2, y // 2 + 1
            total = jnp.broadcast_to(sums[pb][f : f + 1], (8, 128))
            before = jnp.where(iota((8, 128), 1) > 0, pltpu.roll(total, 1, 1), 0.0)
            row = iota((8, 128), 0)
            held = jnp.where(row < 3, total + before, total) * diag[pa * 2 + pb]
            even = jnp.broadcast_to(free[y, 6:7], (8, 128))
            odd = jnp.broadcast_to(free[y, 7:8], (8, 128))
            open_ = jnp.where(row < 3, even, jnp.where(row < 6, odd, 0.0))
            cols.append(open_ / (open_ * held + (1.0 - open_)))
        dinv[x] = jnp.concatenate(cols, axis=0)

    def pair(e, carry):
        inverse(2 * e, 0, young[e] + young[e + 1])

        @pl.when(e < 8)
        def _():
            inverse(2 * e + 1, 1, young[e + 1])

        return carry

    lax.fori_loop(0, 9, pair, 0)

    def operand(x, carry):
        split_store(load_columns(u_reg, x + 1, 1, 17), x, s_ref, t_ref)
        return carry

    lax.fori_loop(0, 17, operand, 0)
    apply(matrix, s_ref, t_ref, young, w_ref, o_ref, 8, 4, 1)

    def residual(x, carry):
        image = collect(w_ref, o_ref, x + 2, 2, 13)
        inv = load_columns(dinv, x + 2, 2, 13)
        res = load_columns(f_reg, x + 1, 1, 13) - image
        z0 = inv * res
        store_columns(z0_ref, x, z0)
        store_columns(u_ref, x, load_columns(u_reg, x + 3, 3, 13))

        @pl.when(jnp.logical_and(x >= 2, x < 10))
        def _():
            store_columns(w0_ref, x - 2, jnp.where(inv > 0.0, res, 0.0)[2:10])

        return carry

    lax.fori_loop(0, 13, residual, 0)

    def operand_0(x, carry):
        split_store(load_columns(z0_ref, x, 0, 13), x, s_ref, t_ref)
        return carry

    lax.fori_loop(0, 13, operand_0, 0)
    apply(matrix, s_ref, t_ref, young, w_ref, o_ref, 5, 3, 2)

    def image_1(x, carry):
        image = collect(w_ref, o_ref, x + 2, 2, 8)
        inv = load_columns(dinv, x + 4, 4, 8)
        store_columns(w1_ref, x, jnp.where(inv > 0.0, image, 0.0))
        store_columns(z1_ref, x, inv * image)
        return carry

    lax.fori_loop(0, OWN, image_1, 0)
    for part, send in zip(PARTS, sends):
        send[...] = take(z1_ref, part, flags, HALO_Z)


def second_kernel(flags, matrix, z1_own, dinv, young, w0_ref, w1_ref, z0_ref, u_ref, f_own, *rest):
    received, rest = rest[:8], rest[8:]
    (z1_ref, z2_ref, z3_ref, sums_ref), rest = rest[:4], rest[4:]
    z_reg, z2_reg, s_ref, t_ref, w_ref, o_ref, w2_ref, w3_ref, w4_ref, table = rest
    z_reg[HALO_Z : HALO_Z + OWN, 8 * HALO_Z : 8 * (HALO_Z + OWN), :] = z1_own[...]
    for part, value in zip(PARTS, received):
        place(z_reg, value[...], part, flags, HALO_Z)

    def operand_1(x, carry):
        split_store(load_columns(z_reg, x + 1, 1, 21), x, s_ref, t_ref)
        return carry

    lax.fori_loop(0, 21, operand_1, 0)

    def keep(x, carry):
        store_columns(z1_ref, x, load_columns(z_reg, x + 5, 5, 13))
        return carry

    lax.fori_loop(0, 13, keep, 0)
    apply(matrix, s_ref, t_ref, young, w_ref, o_ref, 10, 5, 0)

    def image_2(x, carry):
        image = collect(w_ref, o_ref, x + 2, 2, 17)
        inv = load_columns(dinv, x, 0, 17)
        z2 = inv * image
        split_store(z2, x, s_ref, t_ref)

        @pl.when(jnp.logical_and(x >= 2, x < 15))
        def _():
            store_columns(z2_ref, x - 2, z2[2:15])

        @pl.when(jnp.logical_and(x >= 4, x < 12))
        def _():
            store_columns(w2_ref, x - 4, jnp.where(inv > 0.0, image, 0.0)[4:12])

        return carry

    lax.fori_loop(0, 17, image_2, 0)
    apply(matrix, s_ref, t_ref, young, w_ref, o_ref, 8, 4, 1)

    def image_3(x, carry):
        image = collect(w_ref, o_ref, x + 2, 2, 13)
        inv = load_columns(dinv, x + 2, 2, 13)
        z3 = inv * image
        split_store(z3, x, s_ref, t_ref)
        store_columns(z3_ref, x, z3)

        @pl.when(jnp.logical_and(x >= 2, x < 10))
        def _():
            store_columns(w3_ref, x - 2, jnp.where(inv > 0.0, image, 0.0)[2:10])

        return carry

    lax.fori_loop(0, 13, image_3, 0)
    apply(matrix, s_ref, t_ref, young, w_ref, o_ref, 5, 3, 2)
    table[...] = jnp.zeros(table.shape, F32)

    def dots(x, carry):
        inv = load_columns(dinv, x + 4, 4, 8)
        w4 = jnp.where(inv > 0.0, collect(w_ref, o_ref, x + 2, 2, 8), 0.0)
        w = [load_columns(ref, x, 0, 8) for ref in (w0_ref, w1_ref, w2_ref, w3_ref)] + [w4]
        z = [inv * value for value in w[:4]]
        load = jnp.where(inv > 0.0, load_columns(f_own, x, 0, 8), 0.0)
        u = load_columns(u_ref, x + 2, 2, 8)
        for index, (first, second) in enumerate(dot_list()):
            first = u if first is None else (w if first[0] == "w" else z)[first[1]]
            second = load if second is None else w[second[1]]
            table[index : index + 1, :] += jnp.sum(
                jnp.sum(first * second, axis=0), axis=0, keepdims=True
            )
        return carry

    lax.fori_loop(0, OWN, dots, 0)
    totals = jnp.sum(table[...], axis=1, keepdims=True)
    shape = table.shape
    line = jnp.sum(
        jnp.where(iota(shape, 0) == iota(shape, 1), jnp.broadcast_to(totals, shape), 0.0),
        axis=0,
        keepdims=True,
    )
    sums_ref[...] = jnp.broadcast_to(line, sums_ref.shape)


def dot_list():
    out = [(("w", i), ("w", j)) for i in range(5) for j in range(i, 5)]
    out += [(None, None)] + [(("z", i), None) for i in range(4)]
    out += [(None, ("w", j)) for j in range(5)]
    out += [(("z", i), ("w", j)) for i in range(4) for j in range(5)]
    return out


def step_sizes(total):
    place_of = {pair: index for index, pair in enumerate(dot_list())}

    def gram(i, j):
        return total(place_of[("w", min(i, j)), ("w", max(i, j))])

    one = jnp.ones((1, 128), F32)
    poly = [one]
    coef = [jnp.zeros((1, 128), F32)] * SWEEPS
    for sweep in range(SWEEPS):
        top = sum(poly[i] * poly[j] * gram(i, j + 1) for i in range(sweep + 1) for j in range(sweep + 1))
        bottom = sum(
            poly[i] * poly[j] * gram(i + 1, j + 1) for i in range(sweep + 1) for j in range(sweep + 1)
        )
        omega = top / bottom
        for i in range(sweep + 1):
            coef[i] = coef[i] + omega * poly[i]
        poly = [
            (poly[i] if i <= sweep else 0.0) - (omega * poly[i - 1] if i else 0.0)
            for i in range(sweep + 2)
        ]
    work = total(place_of[None, None])
    for i in range(SWEEPS):
        work = work + coef[i] * total(place_of[("z", i), None])
    for j in range(SWEEPS + 1):
        part = total(place_of[None, ("w", j)])
        for i in range(SWEEPS):
            part = part + coef[i] * total(place_of[("z", i), ("w", j)])
        work = work - poly[j] * part
    return coef, work


def last_kernel(flags, matrix, sums, u_ref, z0_ref, z1_ref, z2_ref, z3_ref, factor, *rest):
    (out_u, out_f, out_c), (own, s_ref, t_ref, uf_ref, tf_ref, sens_ref) = rest[:3], rest[3:]
    line = jnp.sum(sums[...], axis=0, keepdims=True)
    shape = (48, 128)
    spread = jnp.where(iota(shape, 0) == iota(shape, 1), jnp.broadcast_to(line, shape), 0.0)
    spread = jnp.broadcast_to(jnp.sum(spread, axis=1, keepdims=True), shape)
    coef, work = step_sizes(lambda index: spread[index : index + 1])
    out_c[...] = work

    def combine(x, carry):
        value = load_columns(u_ref, x, 0, 13)
        for index, ref in enumerate((z0_ref, z1_ref, z2_ref, z3_ref)):
            value = value + coef[index] * load_columns(ref, x, 0, 13)
        store_columns(uf_ref, x, value)
        split_store(value, x, s_ref, t_ref)
        row = iota((7, 8, 128), 1)
        even = jnp.concatenate([value[y : y + 1] for y in range(0, 13, 2)], axis=0)
        odd = jnp.concatenate([value[min(y, 12) : min(y, 12) + 1] for y in range(1, 14, 2)], axis=0)
        nxt = next_even(jnp.where(row < 3, even, pltpu.roll(odd, 3, 1)))
        store_columns(tf_ref, x, nxt)

        @pl.when(jnp.logical_and(x >= 2, x < 10))
        def _():
            store_columns(own, x - 2, value[2:10])

        return carry

    lax.fori_loop(0, 13, combine, 0)

    def energies(i, carry):
        for j in range(0, 6, 2):
            both = products(matrix, s_ref, t_ref, 2 * i, j)
            for e in range(2):
                k = j + e
                acc = jnp.zeros((8, 128), F32)
                for a in range(3):
                    left = uf_ref[2 * i + a, 16 * k : 16 * k + 24, :] * both[e][24 * a : 24 * a + 24]
                    right = tf_ref[2 * i + a, 8 * k : 8 * k + 16, :] * both[e][72 + 16 * a : 88 + 16 * a]
                    acc = acc + left[:8] + left[8:16] + left[16:] + right[:8] + right[8:]
                sens_ref[i, k : k + 1, :] = jnp.sum(acc, axis=0, keepdims=True)
        sens_ref[i, 6:8, :] = jnp.zeros((2, 128), F32)
        return carry

    lax.fori_loop(0, 6, energies, 0)
    edge = RADIUS - 1.0
    corner = RADIUS - math.sqrt(2.0)
    row = iota((8, 128), 0)
    lane = iota((8, 128), 1)
    sens = [sens_ref[x] * factor[x] for x in range(6)]
    low, high = flags[LOW_Y].astype(F32), flags[HIGH_Y].astype(F32)
    inside = jnp.where(row == 0, low, jnp.where(row < 5, 1.0, jnp.where(row == 5, high, 0.0)))
    inside_x = [flags[LOW_X].astype(F32)] + [1.0] * 4 + [flags[HIGH_X].astype(F32)]
    covered = [inside * value for value in inside_x]

    def along_y(v):
        return pltpu.roll(v, 1, 0) + pltpu.roll(v, 7, 0)

    def along_z(v):
        return jnp.where(lane > 0, pltpu.roll(v, 1, 1), 0.0) + jnp.where(lane < 127, pltpu.roll(v, 127, 1), 0.0)

    def gathered(layers, x):
        here, sides = layers[x], layers[x - 1] + layers[x + 1]
        ys = along_y(here)
        return (
            RADIUS * here
            + edge * (ys + along_z(here) + sides)
            + corner * (along_z(ys) + along_y(sides) + along_z(sides))
        )

    for x in range(ELEMS):
        out_f[x] = (gathered(sens, x + 1) / gathered(covered, x + 1))[1:5]
    merge = parity_matrix(True)
    for x in range(OWN):
        rows = [
            jnp.concatenate(
                [own[x, pl.ds(comp + 3 * parity, 8, stride=8), :] for parity in range(2)], axis=1
            )
            for comp in range(3)
        ]
        joined = exact_product(jnp.concatenate(rows, axis=0), merge)
        for comp in range(3):
            out_u[comp, x] = joined[8 * comp : 8 * comp + 8]


def partners(part, count_x, count_y):
    def other(i, k, count):
        if k is None:
            return i
        if k == 0:
            return i ^ 1
        return ((i + 1) ^ 1) - 1 if 0 < i < count - 1 else None

    out = []
    for x in range(count_x):
        for y in range(count_y):
            px, py = other(x, part[0], count_x), other(y, part[1], count_y)
            if px is None and py is None:
                px, py = count_x - 1 - x, y
            elif px is None:
                px, py = x, (y ^ 1 if part[1] is None else py)
            elif py is None:
                px, py = (x ^ 1 if part[0] is None else px), y
            out.append((x * count_y + y, px * count_y + py))
    return out


def shapes(*items):
    return [jax.ShapeDtypeStruct(item, F32) for item in items]


def call(kernel, out_shape, scratch, operands):
    spec = pl.BlockSpec(memory_space=pltpu.VMEM)
    return pl.pallas_call(
        kernel,
        out_shape=out_shape,
        in_specs=[pl.BlockSpec(memory_space=pltpu.SMEM)] + [spec] * (len(operands) - 1),
        out_specs=[spec] * len(out_shape),
        scratch_shapes=scratch,
        compiler_params=pltpu.CompilerParams(vmem_limit_bytes=48 * 1024 * 1024),
    )(*operands)


def body(force, load_mask, support_mask, start_field, density, passive_mask):
    count_x, count_y = lax.axis_size("sx"), lax.axis_size("sy")
    devices = count_x * count_y
    index_x, index_y = lax.axis_index("sx"), lax.axis_index("sy")
    flags = jnp.stack(
        [
            1 - index_x % 2,
            1 - index_y % 2,
            jnp.minimum(index_x, 1),
            jnp.minimum(count_x - 1 - index_x, 1),
            jnp.minimum(index_y, 1),
            jnp.minimum(count_y - 1 - index_y, 1),
        ]
    ).astype(jnp.int32)
    stiff = element_matrix()
    matrix = jnp.asarray(operator_matrix(stiff))
    diag = jnp.asarray(diagonal_columns(stiff))

    def swap(values):
        return [
            lax.ppermute(value, ("sx", "sy"), partners(part, count_x, count_y))
            for part, value in zip(PARTS, values)
        ]

    def sizes(width):
        return [math.prod(part_shape(part, width)) * 8 for part in PARTS]

    own = (OWN, OWN * 8, 128)
    middle = (13, 13 * 8, 128)
    first = call(
        prepare_kernel,
        shapes(own, own, *((a + b, 128) for a, b in zip(sizes(HALO_U), sizes(HALO_F)))),
        [],
        [flags, force, load_mask, support_mask, start_field, density, passive_mask],
    )
    u_own, f_own = first[:2]
    second = call(
        first_kernel,
        shapes(
            middle,
            middle,
            (17, 17 * 8, 128),
            (10, 16, 128),
            (6, 8, 128),
            own,
            own,
            own,
            *((a, 128) for a in sizes(HALO_Z)),
        ),
        [
            pltpu.VMEM((18, 18 * 8, 128), F32),
            pltpu.VMEM((14, 14 * 8, 128), F32),
            pltpu.VMEM((17, 17 * 16, 128), BF16),
            pltpu.VMEM((17, 9 * 16, 128), BF16),
            pltpu.VMEM((17, 17 * 8, 128), F32),
            pltpu.VMEM((17, 9 * 8, 128), F32),
        ],
        [flags, matrix, diag, u_own, f_own, *swap(first[2:])],
    )
    z0, u0, dinv, young, factor, w0, w1, z1 = second[:8]
    z1, z2, z3, sums = call(
        second_kernel,
        shapes(middle, middle, middle, (devices, 128)),
        [
            pltpu.VMEM((22, 22 * 8, 128), F32),
            pltpu.VMEM((8, 128), F32),
            pltpu.VMEM((21, 21 * 16, 128), BF16),
            pltpu.VMEM((21, 11 * 16, 128), BF16),
            pltpu.VMEM((21, 21 * 8, 128), F32),
            pltpu.VMEM((21, 11 * 8, 128), F32),
            pltpu.VMEM(own, F32),
            pltpu.VMEM(own, F32),
            pltpu.VMEM(own, F32),
            pltpu.VMEM((48, 128), F32),
        ],
        [flags, matrix, z1, dinv, young, w0, w1, z0, u0, f_own, *swap(second[8:])],
    )
    sums = lax.all_to_all(sums, ("sx", "sy"), 0, 0, tiled=True)
    displacement, filtered, compliance = call(
        last_kernel,
        shapes(start_field.shape, density.shape, (1, 128)),
        [
            pltpu.VMEM(own, F32),
            pltpu.VMEM((13, 13 * 16, 128), BF16),
            pltpu.VMEM((13, 7 * 16, 128), BF16),
            pltpu.VMEM(middle, F32),
            pltpu.VMEM((13, 7 * 8, 128), F32),
            pltpu.VMEM((6, 8, 128), F32),
        ],
        [flags, matrix, sums, u0, z0, z1, z2, z3, factor],
    )
    return displacement, filtered, compliance[0, 0]


def solution(mesh):
    in_specs = (
        P(None, "sx", "sy", None),
        P("sx", "sy", None),
        P("sx", "sy", None),
        P(None, "sx", "sy", None),
        P("sx", "sy", None),
        P("sx", "sy", None),
    )
    out_specs = (P(None, "sx", "sy", None), P("sx", "sy", None), P())
    return jax.shard_map(body, mesh=mesh, in_specs=in_specs, out_specs=out_specs, check_vma=False)
```

time: 753 us -> 94.8 us (0.13); the launches traced: 743 us -> 94.4 us
  local copies, waits for them, and re-layouts: 378 us -> 6.64 us
  blocking collectives: 224 us -> 12.1 us
  starting transfers between devices: 59.8 us -> 20 us
  Pallas kernels: 0 us -> 35.5 us
  waiting for transfers between devices: 46.1 us -> 19.5 us
  other arithmetic: 20.3 us -> 0 us
  between operations: 9.75 us -> 0.72 us
    reshape x18 -> x0, local copies, waits for them, and re-layouts: 288 us -> none  [the longest x12 208 us: split_parity(): shaped = padded.reshape(3, count_x + 1, 2, count_y + 1, 2, count_z + 1, 2)]
    psum x5 -> x0, blocking collectives: 224 us -> none  [the longest x4 179 us: body(): lax.psum((jnp.sum(residual * image), jnp.sum(image * image)), ('sx', 'sy'))]
    transpose x6 -> x0, local copies, waits for them, and re-layouts: 70.7 us -> none  [element_scatter(): moved = jnp.transpose(stacked, (0, 4, 1, 5, 2, 6, 3))]
    ppermute x28 -> x16, starting transfers between devices: 59.8 us -> 20 us  [swap(): lax.ppermute(value, ('sx', 'sy'), partners(part, count_x, count_y))]
    pallas_call x0 -> x4, Pallas kernels: none -> 35.5 us  [call(): pl.pallas_call(kernel, out_shape=out_shape, in_specs=[pl.BlockSpec(memory...]
    ppermute x28 -> x16, waiting for transfers between devices: 46.1 us -> 19.5 us  [swap(): lax.ppermute(value, ('sx', 'sy'), partners(part, count_x, count_y))]
    all_to_all x0 -> x1, blocking collectives: none -> 12.1 us  [body(): sums = lax.all_to_all(sums, ('sx', 'sy'), 0, 0, tiled=True)]
    slice x190 -> x0, local copies, waits for them, and re-layouts: 8.98 us -> none  [the longest x134 5.78 us: element_vectors(): plane[shift_a:shift_a + count_x, shift_b:shift_b + count_y, shift_c:shift...]
  transfers between devices with their start and end apart: 28 -> 16, of which waited for: 21 -> 6; matrix products, arithmetic and copies ran while one was open for 13% -> 0% of each run, Pallas kernels for 0% -> 0%
where the time goes in v1:
time: 94.8 us; the launch traced here: 94.4 us
  Pallas kernels  35.5 us (37%)
  starting transfers between devices  20 us (21%)
  waiting for transfers between devices  19.5 us (21%)
  blocking collectives  12.1 us (13%)
  local copies, waits for them, and re-layouts  6.64 us (7%)
    pallas_call x4, Pallas kernels, call(): pl.pallas_call(kernel, out_shape=out_shape, in_specs=[pl.BlockSpec(memory...  35.5 us
    ppermute x16, starting transfers between devices, swap(): lax.ppermute(value, ('sx', 'sy'), partners(part, count_x, count_y))  20 us
    ppermute x16, waiting for transfers between devices, swap(): lax.ppermute(value, ('sx', 'sy'), partners(part, count_x, count_y))  19.5 us
    all_to_all x1, blocking collectives, body(): sums = lax.all_to_all(sums, ('sx', 'sy'), 0, 0, tiled=True)  12.1 us
    unnamed x20, local copies, waits for them, and re-layouts  6.55 us
  transfers between devices with their start and end apart: 16, of which 6 were waited for; matrix products, arithmetic and copies ran while one was open for 0% of the time, Pallas kernels for 0%

profile of v1, /device:TPU:0, one launch (start us, length us, event | category | flops | bytes accessed | tf_op | source)
XLA Modules:
  0.0 94.4 jit_solution(4852566910828003124)
XLA Ops:
  0.7 0.9 copy-done.3
  1.7 0.9 copy-done.4
  2.6 0.8 copy-done.5
  3.4 0.8 copy-done.6
  4.3 0.7 copy-done.8
  5.0 0.7 copy-done.9
  5.7 1.0 %shard_map.103 = (f32[8,64,128]{2,1,0:T(8,128)S(1)}, f32[8,64,128]{2,1,0:T(8,128)S(1)}, f32[512,128]{1,0:T(8,128)S(1)}, f32[512,128]{1,0:T(8,128)S(1)}, f32[512,...) custom-call(s32[6]{0:T(128)S(1)} %stack.27.flags, ...), custom_call_target="tpu_custom_call" | custom-call | tf_op jit(solution)/shard_map/pallas_call | solution.py:624
  6.7 2.5 %collective-permute-start.4 = (f32[272,128]{1,0:T(8,128)S(1)}, f32[272,128]{1,0:T(8,128)S(1)}, u32[]{:S(2)}, u32[]{:S(2)}) collective-permute-start(f32[272,128]{1,0:T(8,128)S(1)} %get-tuple-element.42), channel_id=1, source_target_pairs={{0,5},{1,4},{2,7},{3,6},{4,1},{5,0},{6,3},{7,2},{8,13},{9,12},{10,... | collective-permute-start | bytes 417800 | tf_op jit(solution)/shard_map/ppermute | solution.py:654
  9.2 0.7 collective-permute-start.5
  9.9 2.8 %collective-permute-start.6 = (f32[272,128]{1,0:T(8,128)S(1)}, f32[272,128]{1,0:T(8,128)S(1)}, u32[]{:S(2)}, u32[]{:S(2)}) collective-permute-start(f32[272,128]{1,0:T(8,128)S(1)} %get-tuple-element.44), channel_id=1, source_target_pairs={{0,1},{1,0},{2,3},{3,2},{4,9},{5,8},{6,11},{7,10},{8,5},{9,4},{10,... | collective-permute-start | bytes 417800 | tf_op jit(solution)/shard_map/ppermute | solution.py:654
  12.7 1.0 %collective-permute-start = (f32[512,128]{1,0:T(8,128)S(1)}, f32[512,128]{1,0:T(8,128)S(1)}, u32[]{:S(2)}, u32[]{:S(2)}) collective-permute-start(f32[512,128]{1,0:T(8,128)S(1)} %get-tuple-element.38), channel_id=1, source_target_pairs={{0,4},{1,5},{2,6},{3,7},{4,0},{5,1},{6,2},{7,3},{8,12},{9,13},{10,... | collective-permute-start | bytes 786440 | tf_op jit(solution)/shard_map/ppermute | solution.py:654
  13.7 2.0 %collective-permute-start.2 = (f32[512,128]{1,0:T(8,128)S(1)}, f32[512,128]{1,0:T(8,128)S(1)}, u32[]{:S(2)}, u32[]{:S(2)}) collective-permute-start(f32[512,128]{1,0:T(8,128)S(1)} %get-tuple-element.40), channel_id=1, source_target_pairs={{0,1},{1,0},{2,3},{3,2},{4,5},{5,4},{6,7},{7,6},{8,9},{9,8},{10,11... | collective-permute-start | bytes 786440 | tf_op jit(solution)/shard_map/ppermute | solution.py:654
  15.8 1.1 %collective-permute-done.6.rest_6_ = f32[272,128]{1,0:T(8,128)S(1)} collective-permute-done((f32[272,128]{1,0:T(8,128)S(1)}, f32[272,128]{1,0:T(8,128)S(1)}, u32[]{:S(2)}, u32[]{:S(2)}) %collective-permute-start.6) | collective-permute-done | bytes 139296 | tf_op jit(solution)/shard_map/ppermute | solution.py:654
  16.8 2.4 %collective-permute-start.7 = (f32[272,128]{1,0:T(8,128)S(1)}, f32[272,128]{1,0:T(8,128)S(1)}, u32[]{:S(2)}, u32[]{:S(2)}) collective-permute-start(f32[272,128]{1,0:T(8,128)S(1)} %get-tuple-element.45), channel_id=1, source_target_pairs={{0,28},{1,2},{2,1},{3,31},{4,8},{5,10},{6,9},{7,11},{8,4},{9,6},{1... | collective-permute-start | bytes 417800 | tf_op jit(solution)/shard_map/ppermute | solution.py:654
  19.2 3.9 %collective-permute-done.7.rest_7_ = f32[272,128]{1,0:T(8,128)S(1)} collective-permute-done((f32[272,128]{1,0:T(8,128)S(1)}, f32[272,128]{1,0:T(8,128)S(1)}, u32[]{:S(2)}, u32[]{:S(2)}) %collective-permute-start.7) | collective-permute-done | bytes 139296 | tf_op jit(solution)/shard_map/ppermute | solution.py:654
  23.1 2.6 %collective-permute-done.2.rest_2_ = f32[512,128]{1,0:T(8,128)S(1)} collective-permute-done((f32[512,128]{1,0:T(8,128)S(1)}, f32[512,128]{1,0:T(8,128)S(1)}, u32[]{:S(2)}, u32[]{:S(2)}) %collective-permute-start.2) | collective-permute-done | bytes 262176 | tf_op jit(solution)/shard_map/ppermute | solution.py:654
  25.7 0.9 copy-done.1
  26.6 0.7 copy-done.7
  27.3 12.0 %shard_map.104 = (f32[13,104,128]{2,1,0:T(8,128)S(1)}, f32[13,104,128]{2,1,0:T(8,128)}, f32[17,136,128]{2,1,0:T(8,128)}, f32[10,16,128]{2,1,0:T(8,128)S(1)}, f32...) custom-call(s32[6]{0:T(128)S(1)} %stack.27.flags, ...), custom_call_target="tpu_custom_call" | custom-call | tf_op jit(solution)/shard_map/pallas_call | solution.py:624
  39.3 2.9 %collective-permute-start.12 = (f32[392,128]{1,0:T(8,128)S(1)}, f32[392,128]{1,0:T(8,128)S(1)}, u32[]{:S(2)}, u32[]{:S(2)}) collective-permute-start(f32[392,128]{1,0:T(8,128)S(1)} %get-tuple-element.57), channel_id=1, source_target_pairs={{0,5},{1,4},{2,7},{3,6},{4,1},{5,0},{6,3},{7,2},{8,13},{9,12},{10,... | collective-permute-start | bytes 602120 | tf_op jit(solution)/shard_map/ppermute | solution.py:654
  42.3 1.7 %collective-permute-start.14 = (f32[392,128]{1,0:T(8,128)S(1)}, f32[392,128]{1,0:T(8,128)S(1)}, u32[]{:S(2)}, u32[]{:S(2)}) collective-permute-start(f32[392,128]{1,0:T(8,128)S(1)} %get-tuple-element.59), channel_id=1, source_target_pairs={{0,1},{1,0},{2,3},{3,2},{4,9},{5,8},{6,11},{7,10},{8,5},{9,4},{10,... | collective-permute-start | bytes 602120 | tf_op jit(solution)/shard_map/ppermute | solution.py:654
  44.0 1.0 %collective-permute-start.8 = (f32[448,128]{1,0:T(8,128)S(1)}, f32[448,128]{1,0:T(8,128)S(1)}, u32[]{:S(2)}, u32[]{:S(2)}) collective-permute-start(f32[448,128]{1,0:T(8,128)S(1)} %get-tuple-element.53), channel_id=1, source_target_pairs={{0,4},{1,5},{2,6},{3,7},{4,0},{5,1},{6,2},{7,3},{8,12},{9,13},{10,... | collective-permute-start | bytes 688136 | tf_op jit(solution)/shard_map/ppermute | solution.py:654
  45.0 0.3 collective-permute-start.9
  45.3 2.6 %collective-permute-done.12.rest_4_ = f32[392,128]{1,0:T(8,128)S(1)} collective-permute-done((f32[392,128]{1,0:T(8,128)S(1)}, f32[392,128]{1,0:T(8,128)S(1)}, u32[]{:S(2)}, u32[]{:S(2)}) %collective-permute-start.12) | collective-permute-done | bytes 200736 | tf_op jit(solution)/shard_map/ppermute | solution.py:654
  47.8 0.5 collective-permute-start.10
  48.3 1.4 %collective-permute-start.11 = (f32[448,128]{1,0:T(8,128)S(1)}, f32[448,128]{1,0:T(8,128)S(1)}, u32[]{:S(2)}, u32[]{:S(2)}) collective-permute-start(f32[448,128]{1,0:T(8,128)S(1)} %get-tuple-element.56), channel_id=1, source_target_pairs={{0,4},{1,2},{2,1},{3,7},{4,0},{5,6},{6,5},{7,3},{8,12},{9,10},{10,... | collective-permute-start | bytes 688136 | tf_op jit(solution)/shard_map/ppermute | solution.py:654
  49.7 2.3 %collective-permute-done.14.rest_6_ = f32[392,128]{1,0:T(8,128)S(1)} collective-permute-done((f32[392,128]{1,0:T(8,128)S(1)}, f32[392,128]{1,0:T(8,128)S(1)}, u32[]{:S(2)}, u32[]{:S(2)}) %collective-permute-start.14) | collective-permute-done | bytes 200736 | tf_op jit(solution)/shard_map/ppermute | solution.py:654
  52.0 0.8 collective-permute-start.15
  52.7 7.0 %collective-permute-done.15.rest_7_ = f32[392,128]{1,0:T(8,128)S(1)} collective-permute-done((f32[392,128]{1,0:T(8,128)S(1)}, f32[392,128]{1,0:T(8,128)S(1)}, u32[]{:S(2)}, u32[]{:S(2)}) %collective-permute-start.15) | collective-permute-done | bytes 200736 | tf_op jit(solution)/shard_map/ppermute | solution.py:654
  59.8 17.7 %shard_map.105 = (f32[13,104,128]{2,1,0:T(8,128)S(1)}, f32[13,104,128]{2,1,0:T(8,128)S(1)}, f32[13,104,128]{2,1,0:T(8,128)S(1)}, f32[32,128]{1,0:T(8,128)S(1)}) custom-call(s32[6]{0:T(128)S(1)} %stack.27.flags, bf16[240,256]{1,0:T(8,128)(2,1)S(1)} %copy-done.2, f32[8,64,128]{2,1,0:T(8,128)S(1)} %get-tuple-element.46.z1_own, ...), custom_call_target="tpu_custom_call" | custom-call | tf_op jit(solution)/shard_map/pallas_call | solution.py:624
  77.5 12.1 %all_to_all.11 = f32[32,1,128]{2,1,0:T(1,128)S(1)} all-to-all(f32[32,1,128]{2,1,0:T(1,128)S(1)} %bitcast.13), channel_id=1, replica_groups=mesh['sx'=8,'sy'=4] {'sx','sy'}, dimensions={0} | all-to-all | bytes 32768 | tf_op jit(solution)/shard_map/all_to_all | solution.py:711
  89.6 4.8 %shard_map.106 = (f32[3,8,8,256]{3,2,1,0:T(8,128)}, f32[4,4,128]{2,1,0:T(4,128)}, f32[1,128]{1,0:T(1,128)}) custom-call(s32[6]{0:T(128)S(1)} %stack.27.flags, bf16[240,256]{1,0:T(8,128)(2,1)S(1)} %copy-done.2, f32[32,128]{1,0:T(8,128)S(1)} %bitcast.12, f32[13,104,128]{2,1,0:T(8,128)S(1)} %copy-done, f32[13,104,128]{2,1,0:T(8,128)S(1)} %get-tuple-element.51.z0_ref, ...), custom_call_target="tpu_custom_call" | custom-call | tf_op jit(solution)/shard_map/pallas_call | solution.py:624
  (26 shorter events, 0.1 us)
Async XLA Ops:
  0.7 0.9 copy-start.3
  1.7 0.9 copy-start.4
  2.6 0.8 copy-start.5
  3.4 0.8 copy-start.6
  4.3 0.7 copy-start.8
  5.0 0.7 copy-start.9
  5.7 54.1 %copy-start.2 = (bf16[240,256]{1,0:T(8,128)(2,1)S(1)}, bf16[240,256]{1,0:T(8,128)(2,1)}, u32[]{:S(2)}) copy-start(bf16[240,256]{1,0:T(8,128)(2,1)} %constant.35.clone.matrix) | copy-start | bytes 368644
  6.7 7.0 %collective-permute-start.4 = (f32[272,128]{1,0:T(8,128)S(1)}, f32[272,128]{1,0:T(8,128)S(1)}, u32[]{:S(2)}, u32[]{:S(2)}) collective-permute-start(f32[272,128]{1,0:T(8,128)S(1)} %get-tuple-element.42), channel_id=1, source_target_pairs={{0,5},{1,4},{2,7},{3,6},{4,1},{5,0},{6,3},{7,2},{8,13},{9,12},{10,... | collective-permute-start | bytes 417800 | tf_op jit(solution)/shard_map/ppermute | solution.py:654
  9.2 6.5 %collective-permute-start.5 = (f32[272,128]{1,0:T(8,128)S(1)}, f32[272,128]{1,0:T(8,128)S(1)}, u32[]{:S(2)}, u32[]{:S(2)}) collective-permute-start(f32[272,128]{1,0:T(8,128)S(1)} %get-tuple-element.43), channel_id=1, source_target_pairs={{0,4},{1,6},{2,5},{3,7},{4,0},{5,2},{6,1},{7,3},{8,12},{9,14},{10,... | collective-permute-start | bytes 417800 | tf_op jit(solution)/shard_map/ppermute | solution.py:654
  9.9 6.9 %collective-permute-start.6 = (f32[272,128]{1,0:T(8,128)S(1)}, f32[272,128]{1,0:T(8,128)S(1)}, u32[]{:S(2)}, u32[]{:S(2)}) collective-permute-start(f32[272,128]{1,0:T(8,128)S(1)} %get-tuple-element.44), channel_id=1, source_target_pairs={{0,1},{1,0},{2,3},{3,2},{4,9},{5,8},{6,11},{7,10},{8,5},{9,4},{10,... | collective-permute-start | bytes 417800 | tf_op jit(solution)/shard_map/ppermute | solution.py:654
  12.7 10.4 %collective-permute-start = (f32[512,128]{1,0:T(8,128)S(1)}, f32[512,128]{1,0:T(8,128)S(1)}, u32[]{:S(2)}, u32[]{:S(2)}) collective-permute-start(f32[512,128]{1,0:T(8,128)S(1)} %get-tuple-element.38), channel_id=1, source_target_pairs={{0,4},{1,5},{2,6},{3,7},{4,0},{5,1},{6,2},{7,3},{8,12},{9,13},{10,... | collective-permute-start | bytes 786440 | tf_op jit(solution)/shard_map/ppermute | solution.py:654
  13.7 9.4 %collective-permute-start.1 = (f32[512,128]{1,0:T(8,128)S(1)}, f32[512,128]{1,0:T(8,128)S(1)}, u32[]{:S(2)}, u32[]{:S(2)}) collective-permute-start(f32[512,128]{1,0:T(8,128)S(1)} %get-tuple-element.39), channel_id=1, source_target_pairs={{0,1},{1,0},{2,3},{3,2},{4,8},{5,9},{6,10},{7,11},{8,4},{9,5},{10,... | collective-permute-start | bytes 786440 | tf_op jit(solution)/shard_map/ppermute | solution.py:654
  13.7 12.0 %collective-permute-start.2 = (f32[512,128]{1,0:T(8,128)S(1)}, f32[512,128]{1,0:T(8,128)S(1)}, u32[]{:S(2)}, u32[]{:S(2)}) collective-permute-start(f32[512,128]{1,0:T(8,128)S(1)} %get-tuple-element.40), channel_id=1, source_target_pairs={{0,1},{1,0},{2,3},{3,2},{4,5},{5,4},{6,7},{7,6},{8,9},{9,8},{10,11... | collective-permute-start | bytes 786440 | tf_op jit(solution)/shard_map/ppermute | solution.py:654
  15.8 9.9 %collective-permute-start.3 = (f32[512,128]{1,0:T(8,128)S(1)}, f32[512,128]{1,0:T(8,128)S(1)}, u32[]{:S(2)}, u32[]{:S(2)}) collective-permute-start(f32[512,128]{1,0:T(8,128)S(1)} %get-tuple-element.41), channel_id=1, source_target_pairs={{0,4},{1,2},{2,1},{3,7},{4,0},{5,6},{6,5},{7,3},{8,12},{9,10},{10,... | collective-permute-start | bytes 786440 | tf_op jit(solution)/shard_map/ppermute | solution.py:654
  16.8 6.3 %collective-permute-start.7 = (f32[272,128]{1,0:T(8,128)S(1)}, f32[272,128]{1,0:T(8,128)S(1)}, u32[]{:S(2)}, u32[]{:S(2)}) collective-permute-start(f32[272,128]{1,0:T(8,128)S(1)} %get-tuple-element.45), channel_id=1, source_target_pairs={{0,28},{1,2},{2,1},{3,31},{4,8},{5,10},{6,9},{7,11},{8,4},{9,6},{1... | collective-permute-start | bytes 417800 | tf_op jit(solution)/shard_map/ppermute | solution.py:654
  25.7 0.9 copy-start.1
  26.6 0.7 copy-start.7
  39.3 8.5 %collective-permute-start.12 = (f32[392,128]{1,0:T(8,128)S(1)}, f32[392,128]{1,0:T(8,128)S(1)}, u32[]{:S(2)}, u32[]{:S(2)}) collective-permute-start(f32[392,128]{1,0:T(8,128)S(1)} %get-tuple-element.57), channel_id=1, source_target_pairs={{0,5},{1,4},{2,7},{3,6},{4,1},{5,0},{6,3},{7,2},{8,13},{9,12},{10,... | collective-permute-start | bytes 602120 | tf_op jit(solution)/shard_map/ppermute | solution.py:654
  42.3 6.0 %collective-permute-start.13 = (f32[392,128]{1,0:T(8,128)S(1)}, f32[392,128]{1,0:T(8,128)S(1)}, u32[]{:S(2)}, u32[]{:S(2)}) collective-permute-start(f32[392,128]{1,0:T(8,128)S(1)} %get-tuple-element.58), channel_id=1, source_target_pairs={{0,4},{1,6},{2,5},{3,7},{4,0},{5,2},{6,1},{7,3},{8,12},{9,14},{10,... | collective-permute-start | bytes 602120 | tf_op jit(solution)/shard_map/ppermute | solution.py:654
  42.3 9.7 %collective-permute-start.14 = (f32[392,128]{1,0:T(8,128)S(1)}, f32[392,128]{1,0:T(8,128)S(1)}, u32[]{:S(2)}, u32[]{:S(2)}) collective-permute-start(f32[392,128]{1,0:T(8,128)S(1)} %get-tuple-element.59), channel_id=1, source_target_pairs={{0,1},{1,0},{2,3},{3,2},{4,9},{5,8},{6,11},{7,10},{8,5},{9,4},{10,... | collective-permute-start | bytes 602120 | tf_op jit(solution)/shard_map/ppermute | solution.py:654
  44.0 15.8 %collective-permute-start.8 = (f32[448,128]{1,0:T(8,128)S(1)}, f32[448,128]{1,0:T(8,128)S(1)}, u32[]{:S(2)}, u32[]{:S(2)}) collective-permute-start(f32[448,128]{1,0:T(8,128)S(1)} %get-tuple-element.53), channel_id=1, source_target_pairs={{0,4},{1,5},{2,6},{3,7},{4,0},{5,1},{6,2},{7,3},{8,12},{9,13},{10,... | collective-permute-start | bytes 688136 | tf_op jit(solution)/shard_map/ppermute | solution.py:654
  45.0 14.8 %collective-permute-start.9 = (f32[448,128]{1,0:T(8,128)S(1)}, f32[448,128]{1,0:T(8,128)S(1)}, u32[]{:S(2)}, u32[]{:S(2)}) collective-permute-start(f32[448,128]{1,0:T(8,128)S(1)} %get-tuple-element.54), channel_id=1, source_target_pairs={{0,1},{1,0},{2,3},{3,2},{4,8},{5,9},{6,10},{7,11},{8,4},{9,5},{10,... | collective-permute-start | bytes 688136 | tf_op jit(solution)/shard_map/ppermute | solution.py:654
  47.8 12.0 %collective-permute-start.10 = (f32[448,128]{1,0:T(8,128)S(1)}, f32[448,128]{1,0:T(8,128)S(1)}, u32[]{:S(2)}, u32[]{:S(2)}) collective-permute-start(f32[448,128]{1,0:T(8,128)S(1)} %get-tuple-element.55), channel_id=1, source_target_pairs={{0,1},{1,0},{2,3},{3,2},{4,5},{5,4},{6,7},{7,6},{8,9},{9,8},{10,11... | collective-permute-start | bytes 688136 | tf_op jit(solution)/shard_map/ppermute | solution.py:654
  48.3 11.5 %collective-permute-start.11 = (f32[448,128]{1,0:T(8,128)S(1)}, f32[448,128]{1,0:T(8,128)S(1)}, u32[]{:S(2)}, u32[]{:S(2)}) collective-permute-start(f32[448,128]{1,0:T(8,128)S(1)} %get-tuple-element.56), channel_id=1, source_target_pairs={{0,4},{1,2},{2,1},{3,7},{4,0},{5,6},{6,5},{7,3},{8,12},{9,10},{10,... | collective-permute-start | bytes 688136 | tf_op jit(solution)/shard_map/ppermute | solution.py:654
  52.0 7.8 %collective-permute-start.15 = (f32[392,128]{1,0:T(8,128)S(1)}, f32[392,128]{1,0:T(8,128)S(1)}, u32[]{:S(2)}, u32[]{:S(2)}) collective-permute-start(f32[392,128]{1,0:T(8,128)S(1)} %get-tuple-element.60), channel_id=1, source_target_pairs={{0,28},{1,2},{2,1},{3,31},{4,8},{5,10},{6,9},{7,11},{8,4},{9,6},{1... | collective-permute-start | bytes 602120 | tf_op jit(solution)/shard_map/ppermute | solution.py:654
  59.8 29.8 %copy-start = (f32[13,104,128]{2,1,0:T(8,128)S(1)}, f32[13,104,128]{2,1,0:T(8,128)}, u32[]{:S(2)}) copy-start(f32[13,104,128]{2,1,0:T(8,128)} %get-tuple-element.52.u_ref) | copy-start | bytes 2076676

commit v2 on v1

v2 whole, which is shorter than its diff:
```python
import functools
import math

import jax
import jax.numpy as jnp
import numpy as np
from jax import lax
from jax.experimental import pallas as pl
from jax.experimental.pallas import tpu as pltpu
from jax.sharding import PartitionSpec as P

SWEEPS = 4
EMIN = 0.001
RADIUS = 1.5

OWN = 8
ELEMS = OWN // 2
HALO_U = 5
HALO_F = 3
HALO_Z = 7
PARTS = [
    (None, 0),
    (None, 1),
    (1, 0),
    (1, 1),
    (1, None),
    (0, None),
]
MATE = (0, None)
UP_X, UP_Y, LOW_X, HIGH_X, LOW_Y, HIGH_Y = range(6)
SHIFTS = (0.59, 0.73, 0.645, 0.69)
F32 = jnp.float32
BF16 = jnp.bfloat16


def element_matrix():
    poisson = 0.3
    lame_first = poisson / ((1.0 + poisson) * (1.0 - 2.0 * poisson))
    shear = 1.0 / (2.0 * (1.0 + poisson))
    elastic = np.zeros((6, 6))
    elastic[:3, :3] = lame_first
    for entry in range(3):
        elastic[entry, entry] += 2.0 * shear
        elastic[entry + 3, entry + 3] = shear
    points = [-math.sqrt(0.6), 0.0, math.sqrt(0.6)]
    weights = [5.0 / 9.0, 8.0 / 9.0, 5.0 / 9.0]

    def values(point):
        return np.array(
            [point * (point - 1.0) / 2.0, 1.0 - point * point, point * (point + 1.0) / 2.0]
        )

    def slopes(point):
        return np.array([point - 0.5, -2.0 * point, point + 0.5])

    stiff = np.zeros((81, 81))
    for first in range(3):
        for second in range(3):
            for third in range(3):
                val_x, val_y, val_z = (
                    values(points[first]),
                    values(points[second]),
                    values(points[third]),
                )
                der_x, der_y, der_z = (
                    slopes(points[first]),
                    slopes(points[second]),
                    slopes(points[third]),
                )
                strain = np.zeros((6, 81))
                for node_a in range(3):
                    for node_b in range(3):
                        for node_c in range(3):
                            node = node_a * 9 + node_b * 3 + node_c
                            grad_x = 2.0 * der_x[node_a] * val_y[node_b] * val_z[node_c]
                            grad_y = 2.0 * val_x[node_a] * der_y[node_b] * val_z[node_c]
                            grad_z = 2.0 * val_x[node_a] * val_y[node_b] * der_z[node_c]
                            strain[0, node] = grad_x
                            strain[1, 27 + node] = grad_y
                            strain[2, 54 + node] = grad_z
                            strain[3, node] = grad_y
                            strain[3, 27 + node] = grad_x
                            strain[4, 27 + node] = grad_z
                            strain[4, 54 + node] = grad_y
                            strain[5, node] = grad_z
                            strain[5, 54 + node] = grad_x
                factor = weights[first] * weights[second] * weights[third] * 0.125
                stiff = stiff + factor * strain.T @ elastic @ strain
    return stiff.astype(np.float32)


def operator_matrix(stiff):
    hi = stiff.astype(BF16).astype(np.float32)
    lo = stiff - hi
    out = np.zeros((240, 256), np.float32)

    def out_row(comp, a, b, c):
        if c < 2:
            return 80 * a + b * 8 + c * 3 + comp
        return 80 * a + 24 + (b // 2) * 8 + (b % 2) * 3 + comp

    def in_row(comp, a, b, c, low):
        if c < 2:
            return (a * 3 + b) * 16 + low * 8 + c * 3 + comp
        return 144 + (a * 2 + b // 2) * 16 + (b % 2) * 8 + low * 3 + comp

    index = [(p, a, b, c) for p in range(3) for a in range(3) for b in range(3) for c in range(3)]
    for i, first in enumerate(index):
        for j, second in enumerate(index):
            row = out_row(*first)
            out[row, in_row(*second, 0)] = hi[i, j]
            out[row, in_row(*second, 1)] = hi[i, j]
            out[row + 40, in_row(*second, 0)] = lo[i, j]
    return out.astype(BF16)


def diagonal_columns(stiff):
    out = np.zeros((4, 8, 128), np.float32)
    for pa in range(2):
        for pb in range(2):
            for c in range(2):
                for comp in range(3):
                    dof = comp * 27 + pa * 9 + pb * 3 + c
                    out[pa * 2 + pb, c * 3 + comp] = 1.0 / stiff[dof, dof]
    return out


def iota(shape, dim):
    return lax.broadcasted_iota(jnp.int32, shape, dim)


def parity_matrix(transposed):
    node = iota((256, 256), 1 if transposed else 0)
    place = iota((256, 256), 0 if transposed else 1)
    return (node == 2 * (place % 128) + place // 128).astype(F32).astype(BF16)


def exact_product(rows, matrix):
    first = rows.astype(BF16)
    left = rows - first.astype(F32)
    second = left.astype(BF16)
    third = (left - second.astype(F32)).astype(BF16)
    stacked = jnp.concatenate([first, second, third], axis=0)
    out = jnp.dot(stacked, matrix, preferred_element_type=F32)
    count = rows.shape[0]
    return out[:count] + out[count : 2 * count] + out[2 * count :]


def span(k, up, width):
    if k is None:
        return 0, OWN
    upward = up if k == 0 else 1 - up
    return upward * (OWN - width), width


def landing(k, up, width, margin):
    if k is None:
        return margin, OWN
    upward = up if k == 0 else 1 - up
    return upward * (OWN + margin) + (1 - upward) * (margin - width), width


def rows8(start):
    return pl.multiple_of(start * 8, 8) if not isinstance(start, int) else start * 8


def part_shape(part, width):
    return [OWN if k is None else width for k in part]


def take(ref, part, flags, width):
    sx, nx = span(part[0], flags[UP_X], width)
    sy, ny = span(part[1], flags[UP_Y], width)
    return ref[pl.ds(sx, nx), pl.ds(rows8(sy), ny * 8), :].reshape(nx * ny * 8, 128)


def place(ref, value, part, flags, width, passed=False):
    dx, nx = landing(part[0], flags[UP_X], OWN if passed else width, OWN)
    dy, ny = landing(part[1], flags[UP_Y], width, width)
    valid = present(part[0], flags, 0) * present(part[1], flags, 1)
    value = value * valid.astype(F32)
    ref[pl.ds(dx, nx), pl.ds(rows8(dy), ny * 8), :] = value.reshape(nx, ny * 8, 128)


def position():
    index = [lax.axis_index(axis) for axis in ("sx", "sy")]
    last = [lax.axis_size(axis) - 1 for axis in ("sx", "sy")]
    out = [1 - lax.rem(i, 2) for i in index]
    for i, end in zip(index, last):
        out += [jnp.minimum(i, 1), jnp.minimum(end - i, 1)]
    return out


def dense(cols):
    count = cols.shape[0] // 4
    c = cols.reshape(count, 4, 8, 128)
    row = iota((count, 8, 128), 1)
    tiles = [
        jnp.where(row < 6, c[:, 0], pltpu.roll(c[:, 1], 6, 1)),
        jnp.where(row < 4, pltpu.roll(c[:, 1], 6, 1), pltpu.roll(c[:, 2], 4, 1)),
        jnp.where(row < 2, pltpu.roll(c[:, 2], 4, 1), pltpu.roll(c[:, 3], 2, 1)),
    ]
    return jnp.stack(tiles, axis=1).reshape(count * 24, 128)


def sparse(rows):
    count = rows.shape[0] // 24
    t = rows.reshape(count, 3, 8, 128)
    row = iota((count, 8, 128), 1)
    cols = [
        t[:, 0],
        jnp.where(row < 2, pltpu.roll(t[:, 0], 2, 1), pltpu.roll(t[:, 1], 2, 1)),
        jnp.where(row < 4, pltpu.roll(t[:, 1], 4, 1), pltpu.roll(t[:, 2], 4, 1)),
        pltpu.roll(t[:, 2], 6, 1),
    ]
    return jnp.stack(cols, axis=1).reshape(count * 4, 8, 128)


def column_count(part, width):
    return math.prod(part_shape(part, width))


def present(k, flags, dim):
    if k is None:
        return 1
    up, low, high = flags[(UP_X, UP_Y)[dim]], flags[(LOW_X, LOW_Y)[dim]], flags[(HIGH_X, HIGH_Y)[dim]]
    upward = up if k == 0 else 1 - up
    return upward * high + (1 - upward) * low


def young_place(e):
    return e if e <= 2 else 7 if e == 3 else e + 4


def moduli_row(f_reg, e, f, row):
    start = 8 * (young_place(f) + HALO_F) + row
    return f_reg[young_place(e) + OWN, start : start + 1, :]


def split_store(z, x, s_ref, t_ref):
    count = z.shape[0]
    far = z * 65537.0
    hi = far - (far - z)
    lo = z - hi
    s_ref[x, : count * 16, :] = jnp.concatenate([hi, lo], axis=1).astype(BF16).reshape(count * 16, 128)
    row = iota(z.shape, 1)
    nxt = next_even(jnp.where(row < 3, hi, pltpu.roll(lo, 3, 1)))
    if count % 2:
        nxt = jnp.concatenate([nxt, nxt[count - 1 :]], axis=0)
        count += 1
    t_ref[x, : count * 8, :] = nxt.reshape(count // 2, 16, 128).astype(BF16).reshape(count * 8, 128)


def next_even(z):
    count = z.shape[0]
    moved = pltpu.roll(z.reshape(count * 8, 128), 127, 1)
    return jnp.where(iota(moved.shape, 1) < 127, moved, 0.0).reshape(count, 8, 128)


def element_operand(s_ref, t_ref, x, y, pair):
    pieces = [s_ref[x + a, pl.ds(y * 16, 48), :] for a in range(3)]
    pieces += [t_ref[x + a, pl.ds(pair * 16, 32), :] for a in range(3)]
    pieces.append(jnp.zeros((16, 128), BF16))
    return jnp.concatenate(pieces, axis=0)


def products(matrix, s_ref, t_ref, x, j):
    operand = jnp.concatenate(
        [element_operand(s_ref, t_ref, x, 2 * e, e) for e in (j, j + 1)], axis=1
    )
    out = jnp.dot(matrix, operand, preferred_element_type=F32)
    layers = [out[r : r + 40] + out[r + 40 : r + 80] for r in range(0, matrix.shape[0], 80)]
    return [[layer[:, :128] for layer in layers], [layer[:, 128:] for layer in layers]]


def apply(matrix_ref, s_ref, t_ref, young_ref, w_ref, o_ref, count_x, pairs_y, young_at, last=(0,)):
    for i in range(count_x):
        layers = (2,) if i == 0 else last if i == count_x - 1 else (0, 1, 2)
        matrix = matrix_ref[80 * layers[0] : 80 * (layers[-1] + 1), :]
        tails = [None] * 3
        for j in range(0, 2 * pairs_y, 2):
            both = products(matrix, s_ref, t_ref, 2 * i, j)
            for e in range(2):
                k = j + e
                scale = young_ref[i + young_at, k + young_at : k + young_at + 1, :]
                for a, out in zip(layers, both[e]):
                    out = out * scale
                    x = 2 * i + a
                    nodes, over = out[:16], out[24:32]
                    if tails[a] is not None:
                        nodes = jnp.concatenate([nodes[:8] + tails[a][0], nodes[8:]], axis=0)
                        over = over + tails[a][1]
                    if a == 0:
                        nodes = nodes + w_ref[x, 16 * k : 16 * k + 16, :]
                        over = over + o_ref[x, 8 * k : 8 * k + 8, :]
                    w_ref[x, 16 * k : 16 * k + 16, :] = nodes
                    o_ref[x, 8 * k : 8 * k + 8, :] = over
                    tails[a] = (out[16:24], out[32:40])
        k = 2 * pairs_y
        for a in layers:
            x = 2 * i + a
            nodes, over = tails[a]
            if a == 0:
                nodes = nodes + w_ref[x, 16 * k : 16 * k + 8, :]
                over = over + o_ref[x, 8 * k : 8 * k + 8, :]
            w_ref[x, 16 * k : 16 * k + 8, :] = nodes
            o_ref[x, 8 * k : 8 * k + 8, :] = over


def collect(w_ref, o_ref, x, low, count):
    half = (count + 1) // 2
    moved = pltpu.roll(o_ref[x, 4 * low : 4 * low + 8 * half, :], 1, 1)
    moved = jnp.where(iota(moved.shape, 1) > 0, moved, 0.0).reshape(half, 8, 128)
    row = iota(moved.shape, 1)
    even = jnp.where(row < 3, moved, 0.0)
    odd = jnp.where(row < 3, pltpu.roll(moved, 5, 1), 0.0)
    both = jnp.stack([even, odd], axis=1).reshape(2 * half, 8, 128)[:count]
    return w_ref[x, 8 * low : 8 * (low + count), :].reshape(count, 8, 128) + both


def load_columns(ref, x, low, count):
    return ref[x, 8 * low : 8 * (low + count), :].reshape(count, 8, 128)


def store_columns(ref, x, value):
    ref[x, : 8 * value.shape[0], :] = value.reshape(8 * value.shape[0], 128)


def prepare_kernel(fields, moduli, u_ref, f_ref, matrix_ref, diag_ref, *sends):
    flags = position()
    matrix = parity_matrix(False)
    matrix_ref[...] = fields[448:688, :].astype(BF16)
    for index in range(4):
        diag_ref[index] = fields[688 + 8 * index : 696 + 8 * index, :128]
    young, factor = moduli[0], moduli[1]
    for x in range(OWN):
        rows = [fields[64 * c + 8 * x : 64 * c + 8 * x + 8, :] for c in range(7)]
        split = exact_product(jnp.concatenate(rows, axis=0), matrix)
        for index in range(7):
            ref, row = ((u_ref, index), (f_ref, index - 3), (u_ref, 6))[index // 3]
            step = 1 if index == 6 else 3
            for parity in range(2):
                ref[x, pl.ds(row + parity * step, 8, stride=8), :] = split[
                    8 * index : 8 * index + 8, 128 * parity : 128 * parity + 128
                ]
        element = {0: 0, 1: 1, 2: 2, 5: 1, 6: 2, 7: 3}.get(x)
        for row, values in ((6, young), (7, factor)):
            if element is None:
                column = jnp.zeros((8, 128), F32)
            else:
                column = jnp.concatenate(
                    [values[element, :3], jnp.zeros((2, 128), F32), values[element, 1:]], axis=0
                )
            f_ref[x, pl.ds(row, 8, stride=8), :] = column
    for part, send in zip(PARTS, sends):
        first = take(u_ref, part, flags, HALO_U)
        send[: first.shape[0], :] = first
        send[first.shape[0] :, :] = take(f_ref, part, flags, HALO_F)


def first_kernel(matrix, diag, u_own, f_own, *rest):
    flags = position()
    received, rest = rest[:8], rest[8:]
    (z0_ref, u_ref, dinv, young, factor, w0_ref, w1_ref, z1_ref), rest = rest[:8], rest[8:]
    sends, (u_reg, f_reg, s_ref, t_ref, w_ref, o_ref) = rest[:6], rest[6:]
    u_reg[OWN : 2 * OWN, 8 * HALO_U : 8 * (HALO_U + OWN), :] = u_own[...]
    f_reg[OWN : 2 * OWN, 8 * HALO_F : 8 * (HALO_F + OWN), :] = f_own[...]
    for index, value in enumerate(received):
        passed = index >= 6
        part = (0, index - 6) if passed else PARTS[index]
        end = column_count(PARTS[index - 6] if passed else part, HALO_U) * 8
        place(u_reg, value[:end, :], part, flags, HALO_U, passed)
        place(f_reg, value[end:, :], part, flags, HALO_F, passed)
    zero = jnp.zeros((1, 128), F32)
    for e in range(-3, 7):
        rows = [moduli_row(f_reg, e, f, 6) for f in range(-3, 7)]
        young[e + 3] = jnp.concatenate(rows + [zero] * 6, axis=0)
    for e in range(-1, 5):
        rows = [moduli_row(f_reg, e, f, 7) for f in range(-1, 5)]
        factor[e + 1] = jnp.concatenate(rows + [zero] * 2, axis=0)

    def inverse(x):
        e = x // 2
        near = young[e] + young[e + 1] if x % 2 == 0 else young[e + 1]
        both = near + pltpu.roll(near, 1, 0)
        lines = {}
        for pb, total in ((0, both), (1, near)):
            before = jnp.where(iota(total.shape, 1) > 0, pltpu.roll(total, 1, 1), 0.0)
            for pc, value in ((0, total + before), (1, total)):
                lines[pb, pc] = jnp.where(value > 0.0, 1.0 / value, 0.0)
        row = iota((8, 128), 0)
        cols = []
        for y in range(17):
            pb, f = y % 2, y // 2 + 1
            even, odd = [
                lines[pb, pc][f : f + 1] * u_reg[x + 4, 8 * (y + 1) + 6 + pc : 8 * (y + 1) + 7 + pc, :]
                for pc in range(2)
            ]
            line = jnp.where(row < 3, jnp.broadcast_to(even, (8, 128)), jnp.broadcast_to(odd, (8, 128)))
            cols.append(line * diag[(x % 2) * 2 + pb])
        dinv[x] = jnp.concatenate(cols, axis=0)

    for x in range(17):
        inverse(x)

    def operand(x):
        split_store(load_columns(u_reg, x + 4, 1, 17), x, s_ref, t_ref)

    for x in range(17):
        operand(x)
    apply(matrix, s_ref, t_ref, young, w_ref, o_ref, 8, 4, 1)

    def residual(x):
        image = collect(w_ref, o_ref, x + 2, 2, 13)
        inv = load_columns(dinv, x + 2, 2, 13)
        res = load_columns(f_reg, x + 6, 1, 13) - image
        z0 = inv * res
        store_columns(z0_ref, x, z0)
        store_columns(u_ref, x, load_columns(u_reg, x + 6, 3, 13))

        if 2 <= x < 10:
            store_columns(w0_ref, x - 2, jnp.where(inv > 0.0, res, 0.0)[2:10])

    for x in range(13):
        residual(x)

    def operand_0(x):
        split_store(load_columns(z0_ref, x, 0, 13), x, s_ref, t_ref)

    for x in range(13):
        operand_0(x)
    apply(matrix, s_ref, t_ref, young, w_ref, o_ref, 5, 3, 2, last=(0, 1))

    def image_1(x):
        image = collect(w_ref, o_ref, x + 2, 2, 8)
        inv = load_columns(dinv, x + 4, 4, 8)
        image = SHIFTS[0] * jnp.where(inv > 0.0, image, 0.0)
        store_columns(w1_ref, x, load_columns(w0_ref, x, 0, 8) - image)
        store_columns(z1_ref, x, load_columns(z0_ref, x + 2, 2, 8) - inv * image)

    for x in range(OWN):
        image_1(x)
    for part, send in zip(PARTS, sends):
        cols = take(z1_ref, part, flags, HALO_Z)
        extra = send.shape[0] * 8 // 6 - cols.shape[0]
        if extra:
            cols = jnp.concatenate([cols, jnp.zeros((extra, 128), F32)], axis=0)
        send[...] = dense(cols.reshape(-1, 8, 128))


def second_kernel(matrix, z1_own, dinv, young, w0_ref, w1_ref, z0_ref, u_ref, f_own, *rest):
    received, rest = rest[:8], rest[8:]
    (z1_ref, z2_ref, z3_ref, sums_ref), rest = rest[:4], rest[4:]
    z_reg, s_ref, t_ref, w_ref, o_ref, w2_ref, w3_ref = rest
    flags = position()
    z_reg[OWN : 2 * OWN, 8 * HALO_Z : 8 * (HALO_Z + OWN), :] = z1_own[...]
    for index, value in enumerate(received):
        passed = index >= 6
        part = (0, index - 6) if passed else PARTS[index]
        count = column_count(PARTS[index - 6] if passed else part, HALO_Z)
        place(z_reg, sparse(value[...])[:count], part, flags, HALO_Z, passed)

    def operand_1(x):
        split_store(load_columns(z_reg, x + 2, 1, 21), x, s_ref, t_ref)

    for x in range(21):
        operand_1(x)

    def keep(x):
        store_columns(z1_ref, x, load_columns(z_reg, x + 6, 5, 13))

    for x in range(13):
        keep(x)
    apply(matrix, s_ref, t_ref, young, w_ref, o_ref, 10, 5, 0)

    def image_2(x):
        image = collect(w_ref, o_ref, x + 2, 2, 17)
        inv = load_columns(dinv, x, 0, 17)
        image = SHIFTS[1] * jnp.where(inv > 0.0, image, 0.0)
        z2 = load_columns(z_reg, x + 4, 3, 17) - inv * image
        split_store(z2, x, s_ref, t_ref)

        if 2 <= x < 15:
            store_columns(z2_ref, x - 2, z2[2:15])

        if 4 <= x < 12:
            store_columns(w2_ref, x - 4, load_columns(w1_ref, x - 4, 0, 8) - image[4:12])

    for x in range(17):
        image_2(x)
    apply(matrix, s_ref, t_ref, young, w_ref, o_ref, 8, 4, 1)

    def image_3(x):
        image = collect(w_ref, o_ref, x + 2, 2, 13)
        inv = load_columns(dinv, x + 2, 2, 13)
        image = SHIFTS[2] * jnp.where(inv > 0.0, image, 0.0)
        z3 = load_columns(z2_ref, x, 0, 13) - inv * image
        split_store(z3, x, s_ref, t_ref)
        store_columns(z3_ref, x, z3)

        if 2 <= x < 10:
            store_columns(w3_ref, x - 2, load_columns(w2_ref, x - 2, 0, 8) - image[2:10])

    for x in range(13):
        image_3(x)
    apply(matrix, s_ref, t_ref, young, w_ref, o_ref, 5, 3, 2, last=(0, 1))
    sums = [jnp.zeros((8, 128), F32) for _ in dot_list()]

    def dots(x):
        inv = load_columns(dinv, x + 4, 4, 8)
        w = [load_columns(ref, x, 0, 8) for ref in (w0_ref, w1_ref, w2_ref, w3_ref)]
        w.append(w[3] - SHIFTS[3] * jnp.where(inv > 0.0, collect(w_ref, o_ref, x + 2, 2, 8), 0.0))
        z = [inv * value for value in w[:4]]
        load = jnp.where(inv > 0.0, load_columns(f_own, x, 0, 8), 0.0)
        u = load_columns(u_ref, x + 2, 2, 8)
        for index, (first, second) in enumerate(dot_list()):
            first = u if first is None else (w if first[0] == "w" else z)[first[1]]
            second = load if second is None else w[second[1]]
            sums[index] += jnp.sum(first * second, axis=0)

    for x in range(OWN):
        dots(x)
    shape = (48, 128)
    lines = [jnp.sum(value, axis=0, keepdims=True) for value in sums]
    lines = jnp.concatenate(lines + [jnp.zeros((shape[0] - len(lines), 128), F32)], axis=0)
    totals = jnp.sum(lines, axis=1, keepdims=True)
    line = jnp.sum(
        jnp.where(iota(shape, 0) == iota(shape, 1), jnp.broadcast_to(totals, shape), 0.0),
        axis=0,
        keepdims=True,
    )
    sums_ref[...] = jnp.broadcast_to(line, sums_ref.shape)


def dot_list():
    out = [(("w", i), ("w", j)) for i in range(5) for j in range(i, 5)]
    out += [(None, None)] + [(("z", i), None) for i in range(4)]
    out += [(None, ("w", j)) for j in range(5)]
    out += [(("z", i), ("w", j)) for i in range(4) for j in range(i, 5)]
    return out


def step_sizes(total):
    place_of = {pair: index for index, pair in enumerate(dot_list())}

    def gram(i, j):
        return total(place_of[("w", min(i, j)), ("w", max(i, j))])

    poly = [jnp.ones((1, 128), F32)]
    coef = [jnp.zeros((1, 128), F32)] * SWEEPS
    for sweep in range(SWEEPS):
        scaled = [poly[i] / SHIFTS[i] for i in range(sweep + 1)]
        image = [scaled[0]] + [scaled[i] - scaled[i - 1] for i in range(1, sweep + 1)] + [-scaled[sweep]]
        times = [sum(gram(i, j) * image[j] for j in range(sweep + 2)) for i in range(sweep + 2)]
        top = sum(poly[i] * times[i] for i in range(sweep + 1))
        bottom = sum(image[i] * times[i] for i in range(sweep + 2))
        omega = top / bottom
        for i in range(sweep + 1):
            coef[i] = coef[i] + omega * poly[i]
        poly = [
            (poly[i] if i <= sweep else 0.0) - omega * image[i] for i in range(sweep + 2)
        ]
    work = total(place_of[None, None])
    for i in range(SWEEPS):
        work = work + coef[i] * total(place_of[("z", i), None])
    for j in range(SWEEPS + 1):
        part = total(place_of[None, ("w", j)])
        for i in range(SWEEPS):
            part = part + coef[i] * total(place_of[("z", min(i, j)), ("w", max(i, j))])
        work = work - poly[j] * part
    return coef, work


def last_kernel(matrix, sums, u_ref, z0_ref, z1_ref, z2_ref, z3_ref, factor, *rest):
    (out_u, out_f, out_c), (own, s_ref, t_ref, uf_ref, tf_ref, sens_ref) = rest[:3], rest[3:]
    flags = position()
    line = jnp.sum(sums[...], axis=0, keepdims=True)
    shape = (48, 128)
    spread = jnp.where(iota(shape, 0) == iota(shape, 1), jnp.broadcast_to(line, shape), 0.0)
    spread = jnp.broadcast_to(jnp.sum(spread, axis=1, keepdims=True), shape)
    coef, work = step_sizes(lambda index: spread[index : index + 1])
    out_c[...] = work

    def combine(x):
        value = load_columns(u_ref, x, 0, 13)
        for index, ref in enumerate((z0_ref, z1_ref, z2_ref, z3_ref)):
            value = value + coef[index] * load_columns(ref, x, 0, 13)
        store_columns(uf_ref, x, value)
        split_store(value, x, s_ref, t_ref)
        row = iota((7, 8, 128), 1)
        even = jnp.concatenate([value[y : y + 1] for y in range(0, 13, 2)], axis=0)
        odd = jnp.concatenate([value[min(y, 12) : min(y, 12) + 1] for y in range(1, 14, 2)], axis=0)
        nxt = next_even(jnp.where(row < 3, even, pltpu.roll(odd, 3, 1)))
        store_columns(tf_ref, x, nxt)

        if 2 <= x < 10:
            store_columns(own, x - 2, value[2:10])

    for x in range(13):
        combine(x)

    for i in range(6):
        for j in range(0, 6, 2):
            both = products(matrix[...], s_ref, t_ref, 2 * i, j)
            for e in range(2):
                k = j + e
                acc = jnp.zeros((8, 128), F32)
                for a in range(3):
                    left = uf_ref[2 * i + a, 16 * k : 16 * k + 24, :] * both[e][a][:24]
                    right = tf_ref[2 * i + a, 8 * k : 8 * k + 16, :] * both[e][a][24:]
                    acc = acc + left[:8] + left[8:16] + left[16:] + right[:8] + right[8:]
                sens_ref[i, k : k + 1, :] = jnp.sum(acc, axis=0, keepdims=True)
        sens_ref[i, 6:8, :] = jnp.zeros((2, 128), F32)
    edge = RADIUS - 1.0
    corner = RADIUS - math.sqrt(2.0)
    row = iota((8, 128), 0)
    lane = iota((8, 128), 1)
    sens = [sens_ref[x] * factor[x] for x in range(6)]
    low, high = flags[LOW_Y].astype(F32), flags[HIGH_Y].astype(F32)
    inside = jnp.where(row == 0, low, jnp.where(row < 5, 1.0, jnp.where(row == 5, high, 0.0)))
    inside_x = [flags[LOW_X].astype(F32)] + [1.0] * 4 + [flags[HIGH_X].astype(F32)]
    covered = [inside * value for value in inside_x]

    def along_y(v):
        return pltpu.roll(v, 1, 0) + pltpu.roll(v, 7, 0)

    def along_z(v):
        return jnp.where(lane > 0, pltpu.roll(v, 1, 1), 0.0) + jnp.where(lane < 127, pltpu.roll(v, 127, 1), 0.0)

    def gathered(layers, x):
        here, sides = layers[x], layers[x - 1] + layers[x + 1]
        ys = along_y(here)
        return (
            RADIUS * here
            + edge * (ys + along_z(here) + sides)
            + corner * (along_z(ys) + along_y(sides) + along_z(sides))
        )

    for x in range(ELEMS):
        out_f[x] = (gathered(sens, x + 1) / gathered(covered, x + 1))[1:5]
    merge = parity_matrix(True)
    for x in range(OWN):
        rows = [
            jnp.concatenate(
                [own[x, pl.ds(comp + 3 * parity, 8, stride=8), :] for parity in range(2)], axis=1
            )
            for comp in range(3)
        ]
        joined = exact_product(jnp.concatenate(rows, axis=0), merge)
        for comp in range(3):
            out_u[comp, x] = joined[8 * comp : 8 * comp + 8]


def partners(part, count_x, count_y):
    def other(i, k, count):
        if k is None:
            return i
        if k == 0:
            return i ^ 1
        return ((i + 1) ^ 1) - 1 if 0 < i < count - 1 else None

    out = []
    for x in range(count_x):
        for y in range(count_y):
            px, py = other(x, part[0], count_x), other(y, part[1], count_y)
            if px is None and py is None:
                px, py = count_x - 1 - x, y
            elif px is None:
                px, py = x, (y ^ 1 if part[1] is None else py)
            elif py is None:
                px, py = (x ^ 1 if part[0] is None else px), y
            out.append((x * count_y + y, px * count_y + py))
    return out


def shapes(*items):
    return [jax.ShapeDtypeStruct(item, F32) for item in items]


def call(kernel, out_shape, scratch, operands):
    spec = pl.BlockSpec(memory_space=pltpu.VMEM)
    return pl.pallas_call(
        kernel,
        out_shape=out_shape,
        in_specs=[spec] * len(operands),
        out_specs=[spec] * len(out_shape),
        scratch_shapes=scratch,
        compiler_params=pltpu.CompilerParams(vmem_limit_bytes=24 * 1024 * 1024),
    )(*operands)


def body(force, load_mask, support_mask, start_field, density, passive_mask):
    count_x, count_y = lax.axis_size("sx"), lax.axis_size("sy")
    devices = count_x * count_y
    stiff = element_matrix()
    constants = np.zeros((272, 256), np.float32)
    constants[:240] = operator_matrix(stiff).astype(np.float32)
    constants[240:, :128] = diagonal_columns(stiff).reshape(32, 128)
    free = (1 - support_mask).astype(F32)[None]
    load = free * load_mask.astype(F32)[None] * force
    fields = jnp.concatenate(
        [value.reshape(-1, 256) for value in (free * start_field, load, free)] + [jnp.asarray(constants)]
    )
    rho = jnp.where(passive_mask == 1, F32(1.0), density)
    young = EMIN + (1.0 - EMIN) * rho**3
    moduli = jnp.stack([young, jnp.where(passive_mask == 1, F32(0.0), -3.0 * (1.0 - EMIN) * rho**2)])

    def send(value, part):
        return lax.ppermute(value, ("sx", "sy"), partners(part, count_x, count_y))

    def swap(values):
        received = [send(value, part) for part, value in zip(PARTS, values)]
        return received + [send(value, MATE) for value in received[:2]]

    def sizes(width):
        return [column_count(part, width) for part in PARTS]

    own = (OWN, OWN * 8, 128)
    middle = (13, 13 * 8, 128)
    first = call(
        prepare_kernel,
        [
            *shapes(own, own),
            jax.ShapeDtypeStruct((240, 256), BF16),
            *shapes((4, 8, 128)),
            *shapes(*((8 * (a + b), 128) for a, b in zip(sizes(HALO_U), sizes(HALO_F)))),
        ],
        [],
        [fields, moduli],
    )
    u_own, f_own, matrix, diag = first[:4]
    second = call(
        first_kernel,
        shapes(
            middle,
            middle,
            (17, 17 * 8, 128),
            (10, 16, 128),
            (6, 8, 128),
            own,
            own,
            own,
            *(((a + 3) // 4 * 24, 128) for a in sizes(HALO_Z)),
        ),
        [
            pltpu.VMEM((24, 18 * 8, 128), F32),
            pltpu.VMEM((24, 14 * 8, 128), F32),
            pltpu.VMEM((17, 17 * 16, 128), BF16),
            pltpu.VMEM((17, 9 * 16, 128), BF16),
            pltpu.VMEM((17, 17 * 8, 128), F32),
            pltpu.VMEM((17, 9 * 8, 128), F32),
        ],
        [matrix, diag, u_own, f_own, *swap(first[4:])],
    )
    z0, u0, dinv, young, factor, w0, w1, z1 = second[:8]
    z1, z2, z3, sums = call(
        second_kernel,
        shapes(middle, middle, middle, (devices, 128)),
        [
            pltpu.VMEM((24, 22 * 8, 128), F32),
            pltpu.VMEM((21, 21 * 16, 128), BF16),
            pltpu.VMEM((21, 11 * 16, 128), BF16),
            pltpu.VMEM((21, 21 * 8, 128), F32),
            pltpu.VMEM((21, 11 * 8, 128), F32),
            pltpu.VMEM(own, F32),
            pltpu.VMEM(own, F32),
        ],
        [matrix, z1, dinv, young, w0, w1, z0, u0, f_own, *swap(second[8:])],
    )
    sums = lax.all_to_all(sums, ("sx", "sy"), 0, 0, tiled=True)
    displacement, filtered, compliance = call(
        last_kernel,
        shapes(start_field.shape, density.shape, (1, 128)),
        [
            pltpu.VMEM(own, F32),
            pltpu.VMEM((13, 13 * 16, 128), BF16),
            pltpu.VMEM((13, 7 * 16, 128), BF16),
            pltpu.VMEM(middle, F32),
            pltpu.VMEM((13, 7 * 8, 128), F32),
            pltpu.VMEM((6, 8, 128), F32),
        ],
        [matrix, sums, u0, z0, z1, z2, z3, factor],
    )
    return displacement, filtered, compliance[0, 0]


def solution(mesh):
    in_specs = (
        P(None, "sx", "sy", None),
        P("sx", "sy", None),
        P("sx", "sy", None),
        P(None, "sx", "sy", None),
        P("sx", "sy", None),
        P("sx", "sy", None),
    )
    out_specs = (P(None, "sx", "sy", None), P("sx", "sy", None), P())
    return jax.shard_map(body, mesh=mesh, in_specs=in_specs, out_specs=out_specs, check_vma=False)
```

time: 94.8 us -> 64.2 us (0.68)
  Pallas kernels: 35.5 us -> 10.1 us
  local copies, waits for them, and re-layouts: 6.64 us -> 0.01 us
  other arithmetic: 0 us -> 5.16 us
  waiting for transfers between devices: 19.5 us -> 16 us
  starting transfers between devices: 20 us -> 18.2 us
  blocking collectives: 12.1 us -> 13.7 us
    pallas_call x4, Pallas kernels: 35.5 us -> 10.1 us  [call(): pl.pallas_call(kernel, out_shape=out_shape, in_specs=[spec] * len(operand...]
    unnamed x20 -> x2, local copies, waits for them, and re-layouts: 6.55 us -> 0.01 us
    ppermute x16, waiting for transfers between devices: 19.5 us -> 16 us  [send(): return lax.ppermute(value, ('sx', 'sy'), partners(part, count_x, count_y))]
    mul x0 -> x3, other arithmetic: none -> 2.78 us  [the longest x2 1.83 us: body(): load = free * load_mask.astype(F32)[None] * force]
    ppermute x16, starting transfers between devices: 20 us -> 18.2 us  [send(): return lax.ppermute(value, ('sx', 'sy'), partners(part, count_x, count_y))]
    all_to_all x1, blocking collectives: 12.1 us -> 13.7 us  [body(): sums = lax.all_to_all(sums, ('sx', 'sy'), 0, 0, tiled=True)]
    another operation x0 -> x3, other arithmetic: none -> 1.48 us  [body(): jnp.stack([young, jnp.where(passive_mask == 1, F32(0.0), -3.0 * (1.0 - EM...]
where the time goes in v2:
time: 64.2 us; the launch traced here: 63.9 us
  starting transfers between devices  18.2 us (28%)
  waiting for transfers between devices  16 us (25%)
  blocking collectives  13.7 us (21%)
  Pallas kernels  10.1 us (16%)
  other arithmetic  5.16 us (8%)
  between operations  0.73 us (1%)
    ppermute x16, starting transfers between devices, send(): return lax.ppermute(value, ('sx', 'sy'), partners(part, count_x, count_y))  18.2 us
    ppermute x16, waiting for transfers between devices, send(): return lax.ppermute(value, ('sx', 'sy'), partners(part, count_x, count_y))  16 us
    all_to_all x1, blocking collectives, body(): sums = lax.all_to_all(sums, ('sx', 'sy'), 0, 0, tiled=True)  13.7 us
    pallas_call x4, Pallas kernels, call(): pl.pallas_call(kernel, out_shape=out_shape, in_specs=[spec] * len(operand...  10.1 us
    mul x2, other arithmetic, body(): load = free * load_mask.astype(F32)[None] * force  1.83 us
    another operation x3, other arithmetic, body(): jnp.stack([young, jnp.where(passive_mask == 1, F32(0.0), -3.0 * (1.0 - EM...  1.48 us
  transfers between devices with their start and end apart: 16, of which 6 were waited for; matrix products, arithmetic and copies ran while one was open for 0% of the time, Pallas kernels for 0%

profile of v2, /device:TPU:0, one launch (start us, length us, event | category | flops | bytes accessed | tf_op | source)
XLA Modules:
  0.0 63.9 jit_solution(7030323523245889703)
XLA Ops:
  0.6 0.0 copy-start
  0.6 0.8 %fusion.2 = (f32[1,4,4,128]{3,2,1,0:T(4,128)S(1)}, pred[4,4,128]{2,1,0:T(4,128)(4,1)S(1)}) fusion(f32[4,4,128]{2,1,0:T(4,128)} %param.11, s32[4,4,128]{2,1,0:T(4,128)} %param.12), kind=kLoop, calls=%fused_computation.10 | loop fusion | flops 12288 | bytes 26624 | tf_op jit(solution)/shard_map/stack | solution.py:706
  1.4 0.7 %fusion.4 = f32[1,4,4,128]{3,2,1,0:T(4,128)S(1)} fusion(pred[4,4,128]{2,1,0:T(4,128)(4,1)S(1)} %get-tuple-element.66, f32[4,4,128]{2,1,0:T(4,128)} %param.11), kind=kLoop, calls=%fused_computation.12 | loop fusion | flops 8192 | bytes 18432 | tf_op jit(solution)/shard_map/stack | solution.py:706
  2.1 0.8 %subtract_convert_fusion = (f32[8,8,256]{2,1,0:T(8,128)S(1)}, f32[64,256]{1,0:T(8,128)S(1)}) fusion(s32[8,8,256]{2,1,0:T(8,128)} %param.9), kind=kLoop, calls=%fused_computation.4 | loop fusion | flops 32768 | bytes 196608 | tf_op jit(solution)/shard_map/convert_element_type | solution.py:699
  3.0 0.9 %convert_multiply_fusion = f32[8,8,256]{2,1,0:T(8,128)S(1)} fusion(s32[8,8,256]{2,1,0:T(8,128)} %param.8, s32[8,8,256]{2,1,0:T(8,128)} %param.9), kind=kLoop, calls=%fused_computation.3 | loop fusion | flops 65536 | bytes 196608 | tf_op jit(solution)/shard_map/mul | solution.py:700
  3.9 0.9 %broadcast_multiply_fusion = f32[3,8,8,256]{3,2,1,0:T(8,128)S(1)} fusion(f32[3,8,8,256]{3,2,1,0:T(8,128)} %param.7, f32[8,8,256]{2,1,0:T(8,128)S(1)} %convert_multiply_fusion), kind=kLoop, calls=%fused_computation.1 | loop fusion | flops 49152 | bytes 458752 | tf_op jit(solution)/shard_map/mul | solution.py:700
  4.8 0.9 %broadcast_multiply_fusion.1 = f32[3,8,8,256]{3,2,1,0:T(8,128)S(1)} fusion(f32[3,8,8,256]{3,2,1,0:T(8,128)} %param.10, f32[8,8,256]{2,1,0:T(8,128)S(1)} %get-tuple-element.67), kind=kLoop, calls=%fused_computation.2 | loop fusion | flops 49152 | bytes 458752 | tf_op jit(solution)/shard_map/mul | solution.py:702
  5.8 0.1 pad_maximum_fusion.fields
  5.8 0.4 shard_map.94
  6.3 3.1 %collective-permute-start = (f32[512,128]{1,0:T(8,128)S(1)}, f32[512,128]{1,0:T(8,128)S(1)}, u32[]{:S(2)}, u32[]{:S(2)}) collective-permute-start(f32[512,128]{1,0:T(8,128)S(1)} %get-tuple-element.38), channel_id=1, source_target_pairs={{0,1},{1,0},{2,3},{3,2},{4,5},{5,4},{6,7},{7,6},{8,9},{9,8},{10,11... | collective-permute-start | bytes 786440 | tf_op jit(solution)/shard_map/ppermute | solution.py:709
  9.4 3.2 %collective-permute-start.2 = (f32[272,128]{1,0:T(8,128)S(1)}, f32[272,128]{1,0:T(8,128)S(1)}, u32[]{:S(2)}, u32[]{:S(2)}) collective-permute-start(f32[272,128]{1,0:T(8,128)S(1)} %get-tuple-element.40), channel_id=1, source_target_pairs={{0,1},{1,0},{2,3},{3,2},{4,9},{5,8},{6,11},{7,10},{8,5},{9,4},{10,... | collective-permute-start | bytes 417800 | tf_op jit(solution)/shard_map/ppermute | solution.py:709
  12.5 0.0 collective-permute-start.4
  12.6 1.0 %collective-permute-start.5 = (f32[512,128]{1,0:T(8,128)S(1)}, f32[512,128]{1,0:T(8,128)S(1)}, u32[]{:S(2)}, u32[]{:S(2)}) collective-permute-start(f32[512,128]{1,0:T(8,128)S(1)} %get-tuple-element.43), channel_id=1, source_target_pairs={{0,4},{1,5},{2,6},{3,7},{4,0},{5,1},{6,2},{7,3},{8,12},{9,13},{10,... | collective-permute-start | bytes 786440 | tf_op jit(solution)/shard_map/ppermute | solution.py:709
  13.6 2.9 %collective-permute-done.rest_0_ = f32[512,128]{1,0:T(8,128)S(1)} collective-permute-done((f32[512,128]{1,0:T(8,128)S(1)}, f32[512,128]{1,0:T(8,128)S(1)}, u32[]{:S(2)}, u32[]{:S(2)}) %collective-permute-start) | collective-permute-done | bytes 262176 | tf_op jit(solution)/shard_map/ppermute | solution.py:709
  16.5 0.5 collective-permute-start.7
  17.0 1.6 %collective-permute-done.2.rest_2_ = f32[272,128]{1,0:T(8,128)S(1)} collective-permute-done((f32[272,128]{1,0:T(8,128)S(1)}, f32[272,128]{1,0:T(8,128)S(1)}, u32[]{:S(2)}, u32[]{:S(2)}) %collective-permute-start.2) | collective-permute-done | bytes 139296 | tf_op jit(solution)/shard_map/ppermute | solution.py:709
  18.7 1.2 %collective-permute-start.3 = (f32[272,128]{1,0:T(8,128)S(1)}, f32[272,128]{1,0:T(8,128)S(1)}, u32[]{:S(2)}, u32[]{:S(2)}) collective-permute-start(f32[272,128]{1,0:T(8,128)S(1)} %get-tuple-element.41), channel_id=1, source_target_pairs={{0,28},{1,2},{2,1},{3,31},{4,8},{5,10},{6,9},{7,11},{8,4},{9,6},{1... | collective-permute-start | bytes 417800 | tf_op jit(solution)/shard_map/ppermute | solution.py:709
  19.8 4.2 %collective-permute-done.3.rest_3_ = f32[272,128]{1,0:T(8,128)S(1)} collective-permute-done((f32[272,128]{1,0:T(8,128)S(1)}, f32[272,128]{1,0:T(8,128)S(1)}, u32[]{:S(2)}, u32[]{:S(2)}) %collective-permute-start.3) | collective-permute-done | bytes 139296 | tf_op jit(solution)/shard_map/ppermute | solution.py:709
  24.1 2.5 %shard_map.95 = (f32[13,104,128]{2,1,0:T(8,128)S(1)}, f32[13,104,128]{2,1,0:T(8,128)S(1)}, f32[17,136,128]{2,1,0:T(8,128)S(1)}, f32[10,16,128]{2,1,0:T(8,128)S(1...) custom-call(bf16[240,256]{1,0:T(8,128)(2,1)S(1)} %get-tuple-element., ...), custom_call_target="tpu_custom_call" | custom-call | tf_op jit(solution)/shard_map/pallas_call | solution.py:682
  26.6 2.7 %collective-permute-start.8 = (f32[336,128]{1,0:T(8,128)S(1)}, f32[336,128]{1,0:T(8,128)S(1)}, u32[]{:S(2)}, u32[]{:S(2)}) collective-permute-start(f32[336,128]{1,0:T(8,128)S(1)} %get-tuple-element.51), channel_id=1, source_target_pairs={{0,1},{1,0},{2,3},{3,2},{4,5},{5,4},{6,7},{7,6},{8,9},{9,8},{10,11... | collective-permute-start | bytes 516104 | tf_op jit(solution)/shard_map/ppermute | solution.py:709
  29.3 1.2 %collective-permute-start.9 = (f32[336,128]{1,0:T(8,128)S(1)}, f32[336,128]{1,0:T(8,128)S(1)}, u32[]{:S(2)}, u32[]{:S(2)}) collective-permute-start(f32[336,128]{1,0:T(8,128)S(1)} %get-tuple-element.52), channel_id=1, source_target_pairs={{0,4},{1,2},{2,1},{3,7},{4,0},{5,6},{6,5},{7,3},{8,12},{9,10},{10,... | collective-permute-start | bytes 516104 | tf_op jit(solution)/shard_map/ppermute | solution.py:709
  30.4 1.1 %collective-permute-start.10 = (f32[312,128]{1,0:T(8,128)S(1)}, f32[312,128]{1,0:T(8,128)S(1)}, u32[]{:S(2)}, u32[]{:S(2)}) collective-permute-start(f32[312,128]{1,0:T(8,128)S(1)} %get-tuple-element.53), channel_id=1, source_target_pairs={{0,1},{1,0},{2,3},{3,2},{4,9},{5,8},{6,11},{7,10},{8,5},{9,4},{10,... | collective-permute-start | bytes 479240 | tf_op jit(solution)/shard_map/ppermute | solution.py:709
  31.5 0.9 %collective-permute-start.12 = (f32[336,128]{1,0:T(8,128)S(1)}, f32[336,128]{1,0:T(8,128)S(1)}, u32[]{:S(2)}, u32[]{:S(2)}) collective-permute-start(f32[336,128]{1,0:T(8,128)S(1)} %get-tuple-element.55), channel_id=1, source_target_pairs={{0,1},{1,0},{2,3},{3,2},{4,8},{5,9},{6,10},{7,11},{8,4},{9,5},{10,... | collective-permute-start | bytes 516104 | tf_op jit(solution)/shard_map/ppermute | solution.py:709
  32.5 0.9 %collective-permute-start.13 = (f32[336,128]{1,0:T(8,128)S(1)}, f32[336,128]{1,0:T(8,128)S(1)}, u32[]{:S(2)}, u32[]{:S(2)}) collective-permute-start(f32[336,128]{1,0:T(8,128)S(1)} %get-tuple-element.56), channel_id=1, source_target_pairs={{0,4},{1,5},{2,6},{3,7},{4,0},{5,1},{6,2},{7,3},{8,12},{9,13},{10,... | collective-permute-start | bytes 516104 | tf_op jit(solution)/shard_map/ppermute | solution.py:709
  33.3 0.3 collective-permute-done.8.rest_0_
  33.6 1.4 %collective-permute-start.14 = (f32[336,128]{1,0:T(8,128)S(1)}, f32[336,128]{1,0:T(8,128)S(1)}, u32[]{:S(2)}, u32[]{:S(2)}) collective-permute-start(f32[336,128]{1,0:T(8,128)S(1)} %collective-permute-done.8.rest_0_), channel_id=1, source_target_pairs={{0,4},{1,5},{2,6},{3,7},{4,0},{5,1},{6,2},{7,3},{8,12},{9,13},{10,... | collective-permute-start | bytes 516104 | tf_op jit(solution)/shard_map/ppermute | solution.py:709
  35.0 2.4 %collective-permute-done.10.rest_2_ = f32[312,128]{1,0:T(8,128)S(1)} collective-permute-done((f32[312,128]{1,0:T(8,128)S(1)}, f32[312,128]{1,0:T(8,128)S(1)}, u32[]{:S(2)}, u32[]{:S(2)}) %collective-permute-start.10) | collective-permute-done | bytes 159776 | tf_op jit(solution)/shard_map/ppermute | solution.py:709
  37.4 1.1 %collective-permute-start.11 = (f32[312,128]{1,0:T(8,128)S(1)}, f32[312,128]{1,0:T(8,128)S(1)}, u32[]{:S(2)}, u32[]{:S(2)}) collective-permute-start(f32[312,128]{1,0:T(8,128)S(1)} %get-tuple-element.54), channel_id=1, source_target_pairs={{0,28},{1,2},{2,1},{3,31},{4,8},{5,10},{6,9},{7,11},{8,4},{9,6},{1... | collective-permute-start | bytes 479240 | tf_op jit(solution)/shard_map/ppermute | solution.py:709
  38.5 4.5 %collective-permute-done.11.rest_3_ = f32[312,128]{1,0:T(8,128)S(1)} collective-permute-done((f32[312,128]{1,0:T(8,128)S(1)}, f32[312,128]{1,0:T(8,128)S(1)}, u32[]{:S(2)}, u32[]{:S(2)}) %collective-permute-start.11) | collective-permute-done | bytes 159776 | tf_op jit(solution)/shard_map/ppermute | solution.py:709
  43.0 5.0 %shard_map.96 = (f32[13,104,128]{2,1,0:T(8,128)S(1)}, f32[13,104,128]{2,1,0:T(8,128)S(1)}, f32[13,104,128]{2,1,0:T(8,128)S(1)}, f32[32,128]{1,0:T(8,128)S(1)}) custom-call(bf16[240,256]{1,0:T(8,128)(2,1)S(1)} %get-tuple-element.34.matrix, f32[8,64,128]{2,1,0:T(8,128)S(1)} %get-tuple-element.44.z1_own, f32[17,136,128]{2,1,0:T(8,128)S(1)} %get-tuple-element.45.dinv, ...), custom_call_target="tpu_custom_call" | custom-call | tf_op jit(solution)/shard_map/pallas_call | solution.py:682
  48.0 13.7 %all_to_all.11 = f32[32,1,128]{2,1,0:T(1,128)S(1)} all-to-all(f32[32,1,128]{2,1,0:T(1,128)S(1)} %bitcast.15), channel_id=1, replica_groups=mesh['sx'=8,'sy'=4] {'sx','sy'}, dimensions={0} | all-to-all | bytes 32768 | tf_op jit(solution)/shard_map/all_to_all | solution.py:770
  61.7 2.2 %shard_map.97 = (f32[3,8,8,256]{3,2,1,0:T(8,128)}, f32[4,4,128]{2,1,0:T(4,128)}, f32[1,128]{1,0:T(1,128)}) custom-call(bf16[240,256]{1,0:T(8,128)(2,1)S(1)} %get-tuple-element.34.matrix, f32[32,128]{1,0:T(8,128)S(1)} %bitcast.14, f32[13,104,128]{2,1,0:T(8,128)S(1)} %get-tuple-element.50.u_ref, f32[13,104,128]{2,1,0:T(8,128)S(1)} %get-tuple-element.49.z0_ref, ...), custom_call_target="tpu_custom_call" | custom-call | tf_op jit(solution)/shard_map/pallas_call | solution.py:682
  (15 shorter events, 0.0 us)
Async XLA Ops:
  0.6 5.2 %copy-start = (f32[272,256]{1,0:T(8,128)S(1)}, f32[272,256]{1,0:T(8,128)}, u32[]{:S(2)}) copy-start(f32[272,256]{1,0:T(8,128)} %constant.6.clone) | copy-start | bytes 835588
  6.3 10.2 %collective-permute-start = (f32[512,128]{1,0:T(8,128)S(1)}, f32[512,128]{1,0:T(8,128)S(1)}, u32[]{:S(2)}, u32[]{:S(2)}) collective-permute-start(f32[512,128]{1,0:T(8,128)S(1)} %get-tuple-element.38), channel_id=1, source_target_pairs={{0,1},{1,0},{2,3},{3,2},{4,5},{5,4},{6,7},{7,6},{8,9},{9,8},{10,11... | collective-permute-start | bytes 786440 | tf_op jit(solution)/shard_map/ppermute | solution.py:709
  9.4 7.1 %collective-permute-start.1 = (f32[512,128]{1,0:T(8,128)S(1)}, f32[512,128]{1,0:T(8,128)S(1)}, u32[]{:S(2)}, u32[]{:S(2)}) collective-permute-start(f32[512,128]{1,0:T(8,128)S(1)} %get-tuple-element.39), channel_id=1, source_target_pairs={{0,4},{1,2},{2,1},{3,7},{4,0},{5,6},{6,5},{7,3},{8,12},{9,10},{10,... | collective-permute-start | bytes 786440 | tf_op jit(solution)/shard_map/ppermute | solution.py:709
  9.4 9.3 %collective-permute-start.2 = (f32[272,128]{1,0:T(8,128)S(1)}, f32[272,128]{1,0:T(8,128)S(1)}, u32[]{:S(2)}, u32[]{:S(2)}) collective-permute-start(f32[272,128]{1,0:T(8,128)S(1)} %get-tuple-element.40), channel_id=1, source_target_pairs={{0,1},{1,0},{2,3},{3,2},{4,9},{5,8},{6,11},{7,10},{8,5},{9,4},{10,... | collective-permute-start | bytes 417800 | tf_op jit(solution)/shard_map/ppermute | solution.py:709
  12.5 11.5 %collective-permute-start.4 = (f32[512,128]{1,0:T(8,128)S(1)}, f32[512,128]{1,0:T(8,128)S(1)}, u32[]{:S(2)}, u32[]{:S(2)}) collective-permute-start(f32[512,128]{1,0:T(8,128)S(1)} %get-tuple-element.42), channel_id=1, source_target_pairs={{0,1},{1,0},{2,3},{3,2},{4,8},{5,9},{6,10},{7,11},{8,4},{9,5},{10,... | collective-permute-start | bytes 786440 | tf_op jit(solution)/shard_map/ppermute | solution.py:709
  12.6 11.5 %collective-permute-start.5 = (f32[512,128]{1,0:T(8,128)S(1)}, f32[512,128]{1,0:T(8,128)S(1)}, u32[]{:S(2)}, u32[]{:S(2)}) collective-permute-start(f32[512,128]{1,0:T(8,128)S(1)} %get-tuple-element.43), channel_id=1, source_target_pairs={{0,4},{1,5},{2,6},{3,7},{4,0},{5,1},{6,2},{7,3},{8,12},{9,13},{10,... | collective-permute-start | bytes 786440 | tf_op jit(solution)/shard_map/ppermute | solution.py:709
  16.5 7.5 %collective-permute-start.6 = (f32[512,128]{1,0:T(8,128)S(1)}, f32[512,128]{1,0:T(8,128)S(1)}, u32[]{:S(2)}, u32[]{:S(2)}) collective-permute-start(f32[512,128]{1,0:T(8,128)S(1)} %collective-permute-done.rest_0_), channel_id=1, source_target_pairs={{0,4},{1,5},{2,6},{3,7},{4,0},{5,1},{6,2},{7,3},{8,12},{9,13},{10,... | collective-permute-start | bytes 786440 | tf_op jit(solution)/shard_map/ppermute | solution.py:709
  16.5 7.5 %collective-permute-start.7 = (f32[512,128]{1,0:T(8,128)S(1)}, f32[512,128]{1,0:T(8,128)S(1)}, u32[]{:S(2)}, u32[]{:S(2)}) collective-permute-start(f32[512,128]{1,0:T(8,128)S(1)} %collective-permute-done.1.rest_1_), channel_id=1, source_target_pairs={{0,4},{1,5},{2,6},{3,7},{4,0},{5,1},{6,2},{7,3},{8,12},{9,13},{10,... | collective-permute-start | bytes 786440 | tf_op jit(solution)/shard_map/ppermute | solution.py:709
  18.7 5.4 %collective-permute-start.3 = (f32[272,128]{1,0:T(8,128)S(1)}, f32[272,128]{1,0:T(8,128)S(1)}, u32[]{:S(2)}, u32[]{:S(2)}) collective-permute-start(f32[272,128]{1,0:T(8,128)S(1)} %get-tuple-element.41), channel_id=1, source_target_pairs={{0,28},{1,2},{2,1},{3,31},{4,8},{5,10},{6,9},{7,11},{8,4},{9,6},{1... | collective-permute-start | bytes 417800 | tf_op jit(solution)/shard_map/ppermute | solution.py:709
  26.6 7.0 %collective-permute-start.8 = (f32[336,128]{1,0:T(8,128)S(1)}, f32[336,128]{1,0:T(8,128)S(1)}, u32[]{:S(2)}, u32[]{:S(2)}) collective-permute-start(f32[336,128]{1,0:T(8,128)S(1)} %get-tuple-element.51), channel_id=1, source_target_pairs={{0,1},{1,0},{2,3},{3,2},{4,5},{5,4},{6,7},{7,6},{8,9},{9,8},{10,11... | collective-permute-start | bytes 516104 | tf_op jit(solution)/shard_map/ppermute | solution.py:709
  29.3 5.8 %collective-permute-start.9 = (f32[336,128]{1,0:T(8,128)S(1)}, f32[336,128]{1,0:T(8,128)S(1)}, u32[]{:S(2)}, u32[]{:S(2)}) collective-permute-start(f32[336,128]{1,0:T(8,128)S(1)} %get-tuple-element.52), channel_id=1, source_target_pairs={{0,4},{1,2},{2,1},{3,7},{4,0},{5,6},{6,5},{7,3},{8,12},{9,10},{10,... | collective-permute-start | bytes 516104 | tf_op jit(solution)/shard_map/ppermute | solution.py:709
  30.4 7.0 %collective-permute-start.10 = (f32[312,128]{1,0:T(8,128)S(1)}, f32[312,128]{1,0:T(8,128)S(1)}, u32[]{:S(2)}, u32[]{:S(2)}) collective-permute-start(f32[312,128]{1,0:T(8,128)S(1)} %get-tuple-element.53), channel_id=1, source_target_pairs={{0,1},{1,0},{2,3},{3,2},{4,9},{5,8},{6,11},{7,10},{8,5},{9,4},{10,... | collective-permute-start | bytes 479240 | tf_op jit(solution)/shard_map/ppermute | solution.py:709
  31.5 11.5 %collective-permute-start.12 = (f32[336,128]{1,0:T(8,128)S(1)}, f32[336,128]{1,0:T(8,128)S(1)}, u32[]{:S(2)}, u32[]{:S(2)}) collective-permute-start(f32[336,128]{1,0:T(8,128)S(1)} %get-tuple-element.55), channel_id=1, source_target_pairs={{0,1},{1,0},{2,3},{3,2},{4,8},{5,9},{6,10},{7,11},{8,4},{9,5},{10,... | collective-permute-start | bytes 516104 | tf_op jit(solution)/shard_map/ppermute | solution.py:709
  32.5 10.6 %collective-permute-start.13 = (f32[336,128]{1,0:T(8,128)S(1)}, f32[336,128]{1,0:T(8,128)S(1)}, u32[]{:S(2)}, u32[]{:S(2)}) collective-permute-start(f32[336,128]{1,0:T(8,128)S(1)} %get-tuple-element.56), channel_id=1, source_target_pairs={{0,4},{1,5},{2,6},{3,7},{4,0},{5,1},{6,2},{7,3},{8,12},{9,13},{10,... | collective-permute-start | bytes 516104 | tf_op jit(solution)/shard_map/ppermute | solution.py:709
  33.6 9.4 %collective-permute-start.14 = (f32[336,128]{1,0:T(8,128)S(1)}, f32[336,128]{1,0:T(8,128)S(1)}, u32[]{:S(2)}, u32[]{:S(2)}) collective-permute-start(f32[336,128]{1,0:T(8,128)S(1)} %collective-permute-done.8.rest_0_), channel_id=1, source_target_pairs={{0,4},{1,5},{2,6},{3,7},{4,0},{5,1},{6,2},{7,3},{8,12},{9,13},{10,... | collective-permute-start | bytes 516104 | tf_op jit(solution)/shard_map/ppermute | solution.py:709
  35.0 8.0 %collective-permute-start.15 = (f32[336,128]{1,0:T(8,128)S(1)}, f32[336,128]{1,0:T(8,128)S(1)}, u32[]{:S(2)}, u32[]{:S(2)}) collective-permute-start(f32[336,128]{1,0:T(8,128)S(1)} %collective-permute-done.9.rest_1_), channel_id=1, source_target_pairs={{0,4},{1,5},{2,6},{3,7},{4,0},{5,1},{6,2},{7,3},{8,12},{9,13},{10,... | collective-permute-start | bytes 516104 | tf_op jit(solution)/shard_map/ppermute | solution.py:709
  37.4 5.6 %collective-permute-start.11 = (f32[312,128]{1,0:T(8,128)S(1)}, f32[312,128]{1,0:T(8,128)S(1)}, u32[]{:S(2)}, u32[]{:S(2)}) collective-permute-start(f32[312,128]{1,0:T(8,128)S(1)} %get-tuple-element.54), channel_id=1, source_target_pairs={{0,28},{1,2},{2,1},{3,31},{4,8},{5,10},{6,9},{7,11},{8,4},{9,6},{1... | collective-permute-start | bytes 479240 | tf_op jit(solution)/shard_map/ppermute | solution.py:709

commit v3 on v2

--- a/solution.py
+++ b/solution.py
@@ -326,15 +326,17 @@
     ref[x, : 8 * value.shape[0], :] = value.reshape(8 * value.shape[0], 128)
 
 
-def prepare_kernel(fields, moduli, u_ref, f_ref, matrix_ref, diag_ref, *sends):
+def prepare_kernel(fields, design, u_ref, f_ref, *sends):
     flags = position()
     matrix = parity_matrix(False)
-    matrix_ref[...] = fields[448:688, :].astype(BF16)
-    for index in range(4):
-        diag_ref[index] = fields[688 + 8 * index : 696 + 8 * index, :128]
-    young, factor = moduli[0], moduli[1]
+    solid = design[1] == 1.0
+    rho = jnp.where(solid, 1.0, design[0])
+    young = EMIN + (1.0 - EMIN) * (rho * rho * rho)
+    factor = jnp.where(solid, 0.0, -3.0 * (1.0 - EMIN) * (rho * rho))
     for x in range(OWN):
-        rows = [fields[64 * c + 8 * x : 64 * c + 8 * x + 8, :] for c in range(7)]
+        free = 1.0 - fields[7, x]
+        loaded = free * fields[6, x]
+        rows = [free * fields[c, x] for c in range(3)] + [loaded * fields[c, x] for c in range(3, 6)] + [free]
         split = exact_product(jnp.concatenate(rows, axis=0), matrix)
         for index in range(7):
             ref, row = ((u_ref, index), (f_ref, index - 3), (u_ref, 6))[index // 3]
@@ -693,24 +695,31 @@
     count_x, count_y = lax.axis_size("sx"), lax.axis_size("sy")
     devices = count_x * count_y
     stiff = element_matrix()
-    constants = np.zeros((272, 256), np.float32)
-    constants[:240] = operator_matrix(stiff).astype(np.float32)
-    constants[240:, :128] = diagonal_columns(stiff).reshape(32, 128)
-    free = (1 - support_mask).astype(F32)[None]
-    load = free * load_mask.astype(F32)[None] * force
-    fields = jnp.concatenate(
-        [value.reshape(-1, 256) for value in (free * start_field, load, free)] + [jnp.asarray(constants)]
+    matrix = jnp.asarray(operator_matrix(stiff))
+    diag = jnp.asarray(diagonal_columns(stiff))
+    zero = F32(0.0)
+    none = (0, 0, 0)
+    fields = (
+        lax.pad(start_field, zero, ((0, 5, 0), none, none, none))
+        + lax.pad(force, zero, ((3, 2, 0), none, none, none))
+        + (
+            lax.pad(load_mask[None], 0, ((6, 1, 0), none, none, none))
+            + lax.pad(support_mask[None], 0, ((7, 0, 0), none, none, none))
+        ).astype(F32)
     )
-    rho = jnp.where(passive_mask == 1, F32(1.0), density)
-    young = EMIN + (1.0 - EMIN) * rho**3
-    moduli = jnp.stack([young, jnp.where(passive_mask == 1, F32(0.0), -3.0 * (1.0 - EMIN) * rho**2)])
+    design = lax.pad(density[None], zero, ((0, 1, 0), none, none, none)) + lax.pad(
+        passive_mask[None], 0, ((1, 0, 0), none, none, none)
+    ).astype(F32)
 
     def send(value, part):
         return lax.ppermute(value, ("sx", "sy"), partners(part, count_x, count_y))
 
     def swap(values):
-        received = [send(value, part) for part, value in zip(PARTS, values)]
-        return received + [send(value, MATE) for value in received[:2]]
+        first, second, *corners, x_side = [send(value, part) for part, value in zip(PARTS[:5], values)]
+        x_side, mate = lax.optimization_barrier((x_side, values[5]))
+        *corners, second = lax.optimization_barrier((*corners, second))
+        passed = [send(value, MATE) for value in (mate, first, second)]
+        return [first, second, *corners, x_side, *passed]
 
     def sizes(width):
         return [column_count(part, width) for part in PARTS]
@@ -721,14 +730,12 @@
         prepare_kernel,
         [
             *shapes(own, own),
-            jax.ShapeDtypeStruct((240, 256), BF16),
-            *shapes((4, 8, 128)),
             *shapes(*((8 * (a + b), 128) for a, b in zip(sizes(HALO_U), sizes(HALO_F)))),
         ],
         [],
-        [fields, moduli],
+        [fields, design],
     )
-    u_own, f_own, matrix, diag = first[:4]
+    u_own, f_own = first[:2]
     second = call(
         first_kernel,
         shapes(
@@ -750,7 +757,7 @@
             pltpu.VMEM((17, 17 * 8, 128), F32),
             pltpu.VMEM((17, 9 * 8, 128), F32),
         ],
-        [matrix, diag, u_own, f_own, *swap(first[4:])],
+        [matrix, diag, u_own, f_own, *swap(first[2:])],
     )
     z0, u0, dinv, young, factor, w0, w1, z1 = second[:8]
     z1, z2, z3, sums = call(

time: 64.2 us -> 60.3 us (0.939)
  waiting for transfers between devices: 16 us -> 21.6 us
  starting transfers between devices: 18.2 us -> 13.2 us
  other arithmetic: 5.16 us -> 1.88 us
  blocking collectives: 13.7 us -> 12.6 us
    ppermute x16, waiting for transfers between devices: 16 us -> 21.6 us  [send(): return lax.ppermute(value, ('sx', 'sy'), partners(part, count_x, count_y))]
    ppermute x16, starting transfers between devices: 18.2 us -> 13.2 us  [send(): return lax.ppermute(value, ('sx', 'sy'), partners(part, count_x, count_y))]
    mul x3 -> x0, other arithmetic: 2.78 us -> none  [the longest x2 1.83 us: body(): load = free * load_mask.astype(F32)[None] * force]
    add x0 -> x2, other arithmetic: none -> 1.88 us  [the longest x1 1.13 us: body(): lax.pad(start_field, zero, ((0, 5, 0), none, none, none))]
    another operation x3 -> x0, other arithmetic: 1.48 us -> none  [body(): jnp.stack([young, jnp.where(passive_mask == 1, F32(0.0), -3.0 * (1.0 - EM...]
    all_to_all x1, blocking collectives: 13.7 us -> 12.6 us  [body(): sums = lax.all_to_all(sums, ('sx', 'sy'), 0, 0, tiled=True)]
    convert_element_type x1 -> x0, other arithmetic: 0.85 us -> none  [body(): free = (1 - support_mask).astype(F32)[None]]
where the time goes in v3:
time: 60.3 us; the launch traced here: 60.1 us
  waiting for transfers between devices  21.6 us (36%)
  starting transfers between devices  13.2 us (22%)
  blocking collectives  12.6 us (21%)
  Pallas kernels  10.1 us (17%)
  other arithmetic  1.88 us (3%)
  between operations  0.73 us (1%)
    ppermute x16, waiting for transfers between devices, send(): return lax.ppermute(value, ('sx', 'sy'), partners(part, count_x, count_y))  21.6 us
    ppermute x16, starting transfers between devices, send(): return lax.ppermute(value, ('sx', 'sy'), partners(part, count_x, count_y))  13.2 us
    all_to_all x1, blocking collectives, body(): sums = lax.all_to_all(sums, ('sx', 'sy'), 0, 0, tiled=True)  12.6 us
    pallas_call x4, Pallas kernels, call(): pl.pallas_call(kernel, out_shape=out_shape, in_specs=[spec] * len(operand...  10.1 us
  transfers between devices with their start and end apart: 16, of which 6 were waited for; matrix products, arithmetic and copies ran while one was open for 0% of the time, Pallas kernels for 0%

profile of v3, /device:TPU:0, one launch (start us, length us, event | category | flops | bytes accessed | tf_op | source)
XLA Modules:
  0.0 60.1 jit_solution(2586631744202858437)
XLA Ops:
  0.6 0.0 copy-start
  0.6 0.0 copy-start.1
  0.7 0.8 %convert_add_fusion.1.design = f32[2,4,4,128]{3,2,1,0:T(4,128)S(1)} fusion(s32[1,4,4,128]{3,2,1,0:T(4,128)} %bitcast.14, f32[1,4,4,128]{3,2,1,0:T(4,128)} %bitcast.15), kind=kLoop, calls=%fused_computation.1 | loop fusion | flops 8192 | bytes 32768 | tf_op jit(solution)/shard_map/add | solution.py:710
  1.4 1.1 %convert_add_fusion.fields = f32[8,8,8,256]{3,2,1,0:T(8,128)S(1)} fusion(s32[1,8,8,256]{3,2,1,0:T(8,128)} %bitcast.12, s32[1,8,8,256]{3,2,1,0:T(8,128)} %bitcast.13, f32[3,8,8,256]{3,2,1,0:T(8,128)} %param.8, f32[3,8,8,256]{3,2,1,0:T(8,128)} %param.11), kind=kLoop, calls=%fused_computation | loop fusion | flops 524288 | bytes 1048576 | tf_op jit(solution)/shard_map/add | solution.py:703
  2.5 0.4 shard_map.103
  3.0 0.5 collective-permute-start.3
  3.5 4.1 %collective-permute-start.4 = (f32[512,128]{1,0:T(8,128)S(1)}, f32[512,128]{1,0:T(8,128)S(1)}, u32[]{:S(2)}, u32[]{:S(2)}) collective-permute-start(f32[512,128]{1,0:T(8,128)S(1)} %get-tuple-element.51), channel_id=1, source_target_pairs={{0,1},{1,0},{2,3},{3,2},{4,8},{5,9},{6,10},{7,11},{8,4},{9,5},{10,... | collective-permute-start | bytes 786440 | tf_op jit(solution)/shard_map/ppermute | solution.py:715
  7.7 0.0 collective-permute-start
  7.7 2.0 %collective-permute-start.1 = (f32[272,128]{1,0:T(8,128)S(1)}, f32[272,128]{1,0:T(8,128)S(1)}, u32[]{:S(2)}, u32[]{:S(2)}) collective-permute-start(f32[272,128]{1,0:T(8,128)S(1)} %get-tuple-element.45), channel_id=1, source_target_pairs={{0,1},{1,0},{2,3},{3,2},{4,9},{5,8},{6,11},{7,10},{8,5},{9,4},{10,... | collective-permute-start | bytes 417800 | tf_op jit(solution)/shard_map/ppermute | solution.py:715
  9.7 0.8 %collective-permute-start.2 = (f32[272,128]{1,0:T(8,128)S(1)}, f32[272,128]{1,0:T(8,128)S(1)}, u32[]{:S(2)}, u32[]{:S(2)}) collective-permute-start(f32[272,128]{1,0:T(8,128)S(1)} %get-tuple-element.46), channel_id=1, source_target_pairs={{0,28},{1,2},{2,1},{3,31},{4,8},{5,10},{6,9},{7,11},{8,4},{9,6},{1... | collective-permute-start | bytes 417800 | tf_op jit(solution)/shard_map/ppermute | solution.py:715
  10.5 10.1 %collective-permute-done.1.rest_2_ = f32[272,128]{1,0:T(8,128)S(1)} collective-permute-done((f32[272,128]{1,0:T(8,128)S(1)}, f32[272,128]{1,0:T(8,128)S(1)}, u32[]{:S(2)}, u32[]{:S(2)}) %collective-permute-start.1) | collective-permute-done | bytes 139296 | tf_op jit(solution)/shard_map/ppermute | solution.py:715
  20.6 0.0 collective-permute-done.4.rest_4_
  20.6 0.5 collective-permute-start.6
  21.1 0.1 collective-permute-start.5
  21.2 1.3 %collective-permute-done.6.rest_6_ = f32[512,128]{1,0:T(8,128)S(1)} collective-permute-done((f32[512,128]{1,0:T(8,128)S(1)}, f32[512,128]{1,0:T(8,128)S(1)}, u32[]{:S(2)}, u32[]{:S(2)}) %collective-permute-start.6) | collective-permute-done | bytes 262176 | tf_op jit(solution)/shard_map/ppermute | solution.py:715
  22.5 0.0 collective-permute-done.7.rest_7_
  22.5 0.4 collective-permute-done.5.rest_5_
  22.9 2.5 %shard_map.104 = (f32[13,104,128]{2,1,0:T(8,128)S(1)}, f32[13,104,128]{2,1,0:T(8,128)S(1)}, f32[17,136,128]{2,1,0:T(8,128)S(1)}, f32[10,16,128]{2,1,0:T(8,128)S(...) custom-call(bf16[240,256]{1,0:T(8,128)(2,1)S(1)} %copy-done, ...), custom_call_target="tpu_custom_call" | custom-call | tf_op jit(solution)/shard_map/pallas_call | solution.py:684
  25.4 0.2 collective-permute-start.11
  25.6 2.3 %collective-permute-start.12 = (f32[336,128]{1,0:T(8,128)S(1)}, f32[336,128]{1,0:T(8,128)S(1)}, u32[]{:S(2)}, u32[]{:S(2)}) collective-permute-start(f32[336,128]{1,0:T(8,128)S(1)} %get-tuple-element.69), channel_id=1, source_target_pairs={{0,1},{1,0},{2,3},{3,2},{4,8},{5,9},{6,10},{7,11},{8,4},{9,5},{10,... | collective-permute-start | bytes 516104 | tf_op jit(solution)/shard_map/ppermute | solution.py:715
  27.9 0.0 collective-permute-start.8
  27.9 2.0 %collective-permute-start.9 = (f32[312,128]{1,0:T(8,128)S(1)}, f32[312,128]{1,0:T(8,128)S(1)}, u32[]{:S(2)}, u32[]{:S(2)}) collective-permute-start(f32[312,128]{1,0:T(8,128)S(1)} %get-tuple-element.63), channel_id=1, source_target_pairs={{0,1},{1,0},{2,3},{3,2},{4,9},{5,8},{6,11},{7,10},{8,5},{9,4},{10,... | collective-permute-start | bytes 479240 | tf_op jit(solution)/shard_map/ppermute | solution.py:715
  29.9 0.0 collective-permute-start.10
  29.9 8.5 %collective-permute-done.9.rest_2_ = f32[312,128]{1,0:T(8,128)S(1)} collective-permute-done((f32[312,128]{1,0:T(8,128)S(1)}, f32[312,128]{1,0:T(8,128)S(1)}, u32[]{:S(2)}, u32[]{:S(2)}) %collective-permute-start.9) | collective-permute-done | bytes 159776 | tf_op jit(solution)/shard_map/ppermute | solution.py:715
  38.4 0.0 collective-permute-done.10.rest_3_
  38.4 0.5 collective-permute-start.14
  38.9 0.1 collective-permute-start.13
  39.0 1.0 %collective-permute-done.14.rest_6_ = f32[336,128]{1,0:T(8,128)S(1)} collective-permute-done((f32[336,128]{1,0:T(8,128)S(1)}, f32[336,128]{1,0:T(8,128)S(1)}, u32[]{:S(2)}, u32[]{:S(2)}) %collective-permute-start.14) | collective-permute-done | bytes 172064 | tf_op jit(solution)/shard_map/ppermute | solution.py:715
  40.1 0.3 collective-permute-done.13.rest_5_
  40.3 5.0 %shard_map.105 = (f32[13,104,128]{2,1,0:T(8,128)S(1)}, f32[13,104,128]{2,1,0:T(8,128)S(1)}, f32[13,104,128]{2,1,0:T(8,128)S(1)}, f32[32,128]{1,0:T(8,128)S(1)}) custom-call(bf16[240,256]{1,0:T(8,128)(2,1)S(1)} %copy-done, f32[8,64,128]{2,1,0:T(8,128)S(1)} %get-tuple-element.55.z1_own, f32[17,136,128]{2,1,0:T(8,128)S(1)} %get-tuple-element.56.dinv, ...), custom_call_target="tpu_custom_call" | custom-call | tf_op jit(solution)/shard_map/pallas_call | solution.py:684
  45.3 12.6 %all_to_all.11 = f32[32,1,128]{2,1,0:T(1,128)S(1)} all-to-all(f32[32,1,128]{2,1,0:T(1,128)S(1)} %bitcast.11), channel_id=1, replica_groups=mesh['sx'=8,'sy'=4] {'sx','sy'}, dimensions={0} | all-to-all | bytes 32768 | tf_op jit(solution)/shard_map/all_to_all | solution.py:777
  57.9 2.2 %shard_map.106 = (f32[3,8,8,256]{3,2,1,0:T(8,128)}, f32[4,4,128]{2,1,0:T(4,128)}, f32[1,128]{1,0:T(1,128)}) custom-call(bf16[240,256]{1,0:T(8,128)(2,1)S(1)} %copy-done, f32[32,128]{1,0:T(8,128)S(1)} %bitcast.10, f32[13,104,128]{2,1,0:T(8,128)S(1)} %get-tuple-element.61.u_ref, f32[13,104,128]{2,1,0:T(8,128)S(1)} %get-tuple-element.60.z0_ref, ...), custom_call_target="tpu_custom_call" | custom-call | tf_op jit(solution)/shard_map/pallas_call | solution.py:684
  (11 shorter events, 0.0 us)
Async XLA Ops:
  0.6 22.3 %copy-start = (bf16[240,256]{1,0:T(8,128)(2,1)S(1)}, bf16[240,256]{1,0:T(8,128)(2,1)}, u32[]{:S(2)}) copy-start(bf16[240,256]{1,0:T(8,128)(2,1)} %constant.8.clone.matrix) | copy-start | bytes 368644
  0.6 22.3 %copy-start.1 = (f32[4,8,128]{2,1,0:T(8,128)S(1)}, f32[4,8,128]{2,1,0:T(8,128)}, u32[]{:S(2)}) copy-start(f32[4,8,128]{2,1,0:T(8,128)} %constant.9.clone.diag) | copy-start | bytes 49156
  3.0 17.6 %collective-permute-start.3 = (f32[512,128]{1,0:T(8,128)S(1)}, f32[512,128]{1,0:T(8,128)S(1)}, u32[]{:S(2)}, u32[]{:S(2)}) collective-permute-start(f32[512,128]{1,0:T(8,128)S(1)} %get-tuple-element.47), channel_id=1, source_target_pairs={{0,4},{1,2},{2,1},{3,7},{4,0},{5,6},{6,5},{7,3},{8,12},{9,10},{10,... | collective-permute-start | bytes 786440 | tf_op jit(solution)/shard_map/ppermute | solution.py:715
  3.5 17.1 %collective-permute-start.4 = (f32[512,128]{1,0:T(8,128)S(1)}, f32[512,128]{1,0:T(8,128)S(1)}, u32[]{:S(2)}, u32[]{:S(2)}) collective-permute-start(f32[512,128]{1,0:T(8,128)S(1)} %get-tuple-element.51), channel_id=1, source_target_pairs={{0,1},{1,0},{2,3},{3,2},{4,8},{5,9},{6,10},{7,11},{8,4},{9,5},{10,... | collective-permute-start | bytes 786440 | tf_op jit(solution)/shard_map/ppermute | solution.py:715
  7.7 13.0 %collective-permute-start = (f32[512,128]{1,0:T(8,128)S(1)}, f32[512,128]{1,0:T(8,128)S(1)}, u32[]{:S(2)}, u32[]{:S(2)}) collective-permute-start(f32[512,128]{1,0:T(8,128)S(1)} %get-tuple-element.44), channel_id=1, source_target_pairs={{0,1},{1,0},{2,3},{3,2},{4,5},{5,4},{6,7},{7,6},{8,9},{9,8},{10,11... | collective-permute-start | bytes 786440 | tf_op jit(solution)/shard_map/ppermute | solution.py:715
  7.7 12.9 %collective-permute-start.1 = (f32[272,128]{1,0:T(8,128)S(1)}, f32[272,128]{1,0:T(8,128)S(1)}, u32[]{:S(2)}, u32[]{:S(2)}) collective-permute-start(f32[272,128]{1,0:T(8,128)S(1)} %get-tuple-element.45), channel_id=1, source_target_pairs={{0,1},{1,0},{2,3},{3,2},{4,9},{5,8},{6,11},{7,10},{8,5},{9,4},{10,... | collective-permute-start | bytes 417800 | tf_op jit(solution)/shard_map/ppermute | solution.py:715
  9.7 10.9 %collective-permute-start.2 = (f32[272,128]{1,0:T(8,128)S(1)}, f32[272,128]{1,0:T(8,128)S(1)}, u32[]{:S(2)}, u32[]{:S(2)}) collective-permute-start(f32[272,128]{1,0:T(8,128)S(1)} %get-tuple-element.46), channel_id=1, source_target_pairs={{0,28},{1,2},{2,1},{3,31},{4,8},{5,10},{6,9},{7,11},{8,4},{9,6},{1... | collective-permute-start | bytes 417800 | tf_op jit(solution)/shard_map/ppermute | solution.py:715
  20.6 1.9 %collective-permute-start.7 = (f32[512,128]{1,0:T(8,128)S(1)}, f32[512,128]{1,0:T(8,128)S(1)}, u32[]{:S(2)}, u32[]{:S(2)}) collective-permute-start(f32[512,128]{1,0:T(8,128)S(1)} %collective-permute-done.3.rest_1_), channel_id=1, source_target_pairs={{0,4},{1,5},{2,6},{3,7},{4,0},{5,1},{6,2},{7,3},{8,12},{9,13},{10,... | collective-permute-start | bytes 786440 | tf_op jit(solution)/shard_map/ppermute | solution.py:715
  20.6 1.9 %collective-permute-start.6 = (f32[512,128]{1,0:T(8,128)S(1)}, f32[512,128]{1,0:T(8,128)S(1)}, u32[]{:S(2)}, u32[]{:S(2)}) collective-permute-start(f32[512,128]{1,0:T(8,128)S(1)} %collective-permute-done.rest_0_), channel_id=1, source_target_pairs={{0,4},{1,5},{2,6},{3,7},{4,0},{5,1},{6,2},{7,3},{8,12},{9,13},{10,... | collective-permute-start | bytes 786440 | tf_op jit(solution)/shard_map/ppermute | solution.py:715
  21.1 1.8 %collective-permute-start.5 = (f32[512,128]{1,0:T(8,128)S(1)}, f32[512,128]{1,0:T(8,128)S(1)}, u32[]{:S(2)}, u32[]{:S(2)}) collective-permute-start(f32[512,128]{1,0:T(8,128)S(1)} %get-tuple-element.54), channel_id=1, source_target_pairs={{0,4},{1,5},{2,6},{3,7},{4,0},{5,1},{6,2},{7,3},{8,12},{9,13},{10,... | collective-permute-start | bytes 786440 | tf_op jit(solution)/shard_map/ppermute | solution.py:715
  25.4 13.0 %collective-permute-start.11 = (f32[336,128]{1,0:T(8,128)S(1)}, f32[336,128]{1,0:T(8,128)S(1)}, u32[]{:S(2)}, u32[]{:S(2)}) collective-permute-start(f32[336,128]{1,0:T(8,128)S(1)} %get-tuple-element.65), channel_id=1, source_target_pairs={{0,4},{1,2},{2,1},{3,7},{4,0},{5,6},{6,5},{7,3},{8,12},{9,10},{10,... | collective-permute-start | bytes 516104 | tf_op jit(solution)/shard_map/ppermute | solution.py:715
  25.6 12.8 %collective-permute-start.12 = (f32[336,128]{1,0:T(8,128)S(1)}, f32[336,128]{1,0:T(8,128)S(1)}, u32[]{:S(2)}, u32[]{:S(2)}) collective-permute-start(f32[336,128]{1,0:T(8,128)S(1)} %get-tuple-element.69), channel_id=1, source_target_pairs={{0,1},{1,0},{2,3},{3,2},{4,8},{5,9},{6,10},{7,11},{8,4},{9,5},{10,... | collective-permute-start | bytes 516104 | tf_op jit(solution)/shard_map/ppermute | solution.py:715
  27.9 10.5 %collective-permute-start.8 = (f32[336,128]{1,0:T(8,128)S(1)}, f32[336,128]{1,0:T(8,128)S(1)}, u32[]{:S(2)}, u32[]{:S(2)}) collective-permute-start(f32[336,128]{1,0:T(8,128)S(1)} %get-tuple-element.62), channel_id=1, source_target_pairs={{0,1},{1,0},{2,3},{3,2},{4,5},{5,4},{6,7},{7,6},{8,9},{9,8},{10,11... | collective-permute-start | bytes 516104 | tf_op jit(solution)/shard_map/ppermute | solution.py:715
  27.9 10.5 %collective-permute-start.9 = (f32[312,128]{1,0:T(8,128)S(1)}, f32[312,128]{1,0:T(8,128)S(1)}, u32[]{:S(2)}, u32[]{:S(2)}) collective-permute-start(f32[312,128]{1,0:T(8,128)S(1)} %get-tuple-element.63), channel_id=1, source_target_pairs={{0,1},{1,0},{2,3},{3,2},{4,9},{5,8},{6,11},{7,10},{8,5},{9,4},{10,... | collective-permute-start | bytes 479240 | tf_op jit(solution)/shard_map/ppermute | solution.py:715
  29.9 8.5 %collective-permute-start.10 = (f32[312,128]{1,0:T(8,128)S(1)}, f32[312,128]{1,0:T(8,128)S(1)}, u32[]{:S(2)}, u32[]{:S(2)}) collective-permute-start(f32[312,128]{1,0:T(8,128)S(1)} %get-tuple-element.64), channel_id=1, source_target_pairs={{0,28},{1,2},{2,1},{3,31},{4,8},{5,10},{6,9},{7,11},{8,4},{9,6},{1... | collective-permute-start | bytes 479240 | tf_op jit(solution)/shard_map/ppermute | solution.py:715
  38.4 1.7 %collective-permute-start.15 = (f32[336,128]{1,0:T(8,128)S(1)}, f32[336,128]{1,0:T(8,128)S(1)}, u32[]{:S(2)}, u32[]{:S(2)}) collective-permute-start(f32[336,128]{1,0:T(8,128)S(1)} %collective-permute-done.11.rest_1_), channel_id=1, source_target_pairs={{0,4},{1,5},{2,6},{3,7},{4,0},{5,1},{6,2},{7,3},{8,12},{9,13},{10,... | collective-permute-start | bytes 516104 | tf_op jit(solution)/shard_map/ppermute | solution.py:715
  38.4 1.6 %collective-permute-start.14 = (f32[336,128]{1,0:T(8,128)S(1)}, f32[336,128]{1,0:T(8,128)S(1)}, u32[]{:S(2)}, u32[]{:S(2)}) collective-permute-start(f32[336,128]{1,0:T(8,128)S(1)} %collective-permute-done.8.rest_0_), channel_id=1, source_target_pairs={{0,4},{1,5},{2,6},{3,7},{4,0},{5,1},{6,2},{7,3},{8,12},{9,13},{10,... | collective-permute-start | bytes 516104 | tf_op jit(solution)/shard_map/ppermute | solution.py:715
  38.9 1.4 %collective-permute-start.13 = (f32[336,128]{1,0:T(8,128)S(1)}, f32[336,128]{1,0:T(8,128)S(1)}, u32[]{:S(2)}, u32[]{:S(2)}) collective-permute-start(f32[336,128]{1,0:T(8,128)S(1)} %get-tuple-element.72), channel_id=1, source_target_pairs={{0,4},{1,5},{2,6},{3,7},{4,0},{5,1},{6,2},{7,3},{8,12},{9,13},{10,... | collective-permute-start | bytes 516104 | tf_op jit(solution)/shard_map/ppermute | solution.py:715

commit v4 on v3

--- a/solution.py
+++ b/solution.py
@@ -97,12 +97,12 @@
     def out_row(comp, a, b, c):
         if c < 2:
             return 80 * a + b * 8 + c * 3 + comp
-        return 80 * a + 24 + (b // 2) * 8 + (b % 2) * 3 + comp
+        return 80 * a + 24 + (b // 2) * 8 + (b % 2) * 4 + comp
 
     def in_row(comp, a, b, c, low):
         if c < 2:
             return (a * 3 + b) * 16 + low * 8 + c * 3 + comp
-        return 144 + (a * 2 + b // 2) * 16 + (b % 2) * 8 + low * 3 + comp
+        return 144 + (a * 2 + b // 2) * 16 + low * 8 + (b % 2) * 4 + comp
 
     index = [(p, a, b, c) for p in range(3) for a in range(3) for b in range(3) for c in range(3)]
     for i, first in enumerate(index):
@@ -237,24 +237,24 @@
     return f_reg[young_place(e) + OWN, start : start + 1, :]
 
 
+def parts_of(z):
+    far = z * 65537.0
+    hi = far - (far - z)
+    return jnp.concatenate([hi, z - hi], axis=1).astype(BF16).reshape(z.shape[0] * 16, 128)
+
+
 def split_store(z, x, s_ref, t_ref):
     count = z.shape[0]
-    far = z * 65537.0
-    hi = far - (far - z)
-    lo = z - hi
-    s_ref[x, : count * 16, :] = jnp.concatenate([hi, lo], axis=1).astype(BF16).reshape(count * 16, 128)
-    row = iota(z.shape, 1)
-    nxt = next_even(jnp.where(row < 3, hi, pltpu.roll(lo, 3, 1)))
+    s_ref[x, : count * 16, :] = parts_of(z)
     if count % 2:
-        nxt = jnp.concatenate([nxt, nxt[count - 1 :]], axis=0)
+        z = jnp.concatenate([z, z[count - 1 :]], axis=0)
         count += 1
-    t_ref[x, : count * 8, :] = nxt.reshape(count // 2, 16, 128).astype(BF16).reshape(count * 8, 128)
-
-
-def next_even(z):
-    count = z.shape[0]
-    moved = pltpu.roll(z.reshape(count * 8, 128), 127, 1)
-    return jnp.where(iota(moved.shape, 1) < 127, moved, 0.0).reshape(count, 8, 128)
+    z = z.reshape(count // 2, 2, 8, 128)
+    nxt = jnp.where(iota((count // 2, 8, 128), 1) < 4, z[:, 0], pltpu.roll(z[:, 1], 4, 1))
+    nxt = pltpu.roll(nxt.reshape(count * 4, 128), 127, 1)
+    nxt = jnp.where(iota(nxt.shape, 1) < 127, nxt, 0.0).reshape(count // 2, 8, 128)
+    t_ref[x, : count * 8, :] = parts_of(nxt)
+    return nxt
 
 
 def element_operand(s_ref, t_ref, x, y, pair):
@@ -313,7 +313,7 @@
     moved = jnp.where(iota(moved.shape, 1) > 0, moved, 0.0).reshape(half, 8, 128)
     row = iota(moved.shape, 1)
     even = jnp.where(row < 3, moved, 0.0)
-    odd = jnp.where(row < 3, pltpu.roll(moved, 5, 1), 0.0)
+    odd = jnp.where(row < 3, pltpu.roll(moved, 4, 1), 0.0)
     both = jnp.stack([even, odd], axis=1).reshape(2 * half, 8, 128)[:count]
     return w_ref[x, 8 * low : 8 * (low + count), :].reshape(count, 8, 128) + both
 
@@ -326,11 +326,11 @@
     ref[x, : 8 * value.shape[0], :] = value.reshape(8 * value.shape[0], 128)
 
 
-def prepare_kernel(fields, design, u_ref, f_ref, *sends):
+def prepare_kernel(fields, u_ref, f_ref, *sends):
     flags = position()
     matrix = parity_matrix(False)
-    solid = design[1] == 1.0
-    rho = jnp.where(solid, 1.0, design[0])
+    solid = fields[9, :ELEMS, :ELEMS, :128] == 1.0
+    rho = jnp.where(solid, 1.0, fields[8, :ELEMS, :ELEMS, :128])
     young = EMIN + (1.0 - EMIN) * (rho * rho * rho)
     factor = jnp.where(solid, 0.0, -3.0 * (1.0 - EMIN) * (rho * rho))
     for x in range(OWN):
@@ -588,13 +588,7 @@
         for index, ref in enumerate((z0_ref, z1_ref, z2_ref, z3_ref)):
             value = value + coef[index] * load_columns(ref, x, 0, 13)
         store_columns(uf_ref, x, value)
-        split_store(value, x, s_ref, t_ref)
-        row = iota((7, 8, 128), 1)
-        even = jnp.concatenate([value[y : y + 1] for y in range(0, 13, 2)], axis=0)
-        odd = jnp.concatenate([value[min(y, 12) : min(y, 12) + 1] for y in range(1, 14, 2)], axis=0)
-        nxt = next_even(jnp.where(row < 3, even, pltpu.roll(odd, 3, 1)))
-        store_columns(tf_ref, x, nxt)
-
+        store_columns(tf_ref, x, split_store(value, x, s_ref, t_ref))
         if 2 <= x < 10:
             store_columns(own, x - 2, value[2:10])
 
@@ -699,17 +693,17 @@
     diag = jnp.asarray(diagonal_columns(stiff))
     zero = F32(0.0)
     none = (0, 0, 0)
+    small = ((0, OWN - ELEMS, 0), (0, OWN - ELEMS, 0), (0, 128, 0))
     fields = (
-        lax.pad(start_field, zero, ((0, 5, 0), none, none, none))
-        + lax.pad(force, zero, ((3, 2, 0), none, none, none))
+        lax.pad(start_field, zero, ((0, 7, 0), none, none, none))
+        + lax.pad(force, zero, ((3, 4, 0), none, none, none))
+        + lax.pad(density[None], zero, ((8, 1, 0), *small))
         + (
-            lax.pad(load_mask[None], 0, ((6, 1, 0), none, none, none))
-            + lax.pad(support_mask[None], 0, ((7, 0, 0), none, none, none))
+            lax.pad(load_mask[None], 0, ((6, 3, 0), none, none, none))
+            + lax.pad(support_mask[None], 0, ((7, 2, 0), none, none, none))
+            + lax.pad(passive_mask[None], 0, ((9, 0, 0), *small))
         ).astype(F32)
     )
-    design = lax.pad(density[None], zero, ((0, 1, 0), none, none, none)) + lax.pad(
-        passive_mask[None], 0, ((1, 0, 0), none, none, none)
-    ).astype(F32)
 
     def send(value, part):
         return lax.ppermute(value, ("sx", "sy"), partners(part, count_x, count_y))
@@ -733,7 +727,7 @@
             *shapes(*((8 * (a + b), 128) for a, b in zip(sizes(HALO_U), sizes(HALO_F)))),
         ],
         [],
-        [fields, design],
+        [fields],
     )
     u_own, f_own = first[:2]
     second = call(

time: 60.3 us -> 59.4 us (0.985)
  other arithmetic: 1.88 us -> 1.2 us
    add x2 -> x1, other arithmetic: 1.88 us -> 1.2 us  [body(): lax.pad(start_field, zero, ((0, 7, 0), none, none, none))]
where the time goes in v4:
time: 59.4 us; the launch traced here: 59.3 us
  waiting for transfers between devices  21.6 us (36%)
  starting transfers between devices  13.2 us (22%)
  blocking collectives  12.6 us (21%)
  Pallas kernels  9.89 us (17%)
  other arithmetic  1.2 us (2%)
  between operations  0.73 us (1%)
    ppermute x16, waiting for transfers between devices, send(): return lax.ppermute(value, ('sx', 'sy'), partners(part, count_x, count_y))  21.6 us
    ppermute x16, starting transfers between devices, send(): return lax.ppermute(value, ('sx', 'sy'), partners(part, count_x, count_y))  13.2 us
    all_to_all x1, blocking collectives, body(): sums = lax.all_to_all(sums, ('sx', 'sy'), 0, 0, tiled=True)  12.6 us
    pallas_call x4, Pallas kernels, call(): pl.pallas_call(kernel, out_shape=out_shape, in_specs=[spec] * len(operand...  9.89 us
    add x1, other arithmetic, body(): lax.pad(start_field, zero, ((0, 7, 0), none, none, none))  1.2 us
  transfers between devices with their start and end apart: 16, of which 6 were waited for; matrix products, arithmetic and copies ran while one was open for 0% of the time, Pallas kernels for 0%

profile of v4, /device:TPU:0, one launch (start us, length us, event | category | flops | bytes accessed | tf_op | source)
XLA Modules:
  0.0 59.3 jit_solution(3228187842067391623)
XLA Ops:
  0.6 0.0 copy-start
  0.6 0.0 copy-start.1
  0.7 1.2 %convert_add_fusion.fields = f32[10,8,8,256]{3,2,1,0:T(8,128)S(1)} fusion(s32[1,4,4,128]{3,2,1,0:T(4,128)} %bitcast.14, s32[1,8,8,256]{3,2,1,0:T(8,128)} %bitcast.12, s32[1,8,8,256]{3,2,1,0:T(8,128)} %bitcast.13, f32[1,4,4,128]{3,2,1,0:T(4,128)} %bitcast.15, f32[3,8,8,256]{3,2,1,0:T(8,128)} %param.8, f32[3,8,8,256]{3,2,1,0:T(8,128)} %param.11), kind=kLoop, calls=%fused_computation | loop fusion | flops 983040 | bytes 1196032 | tf_op jit(solution)/shard_map/add | solution.py:698
  1.9 0.4 shard_map.103
  2.3 0.5 collective-permute-start.3
  2.8 4.1 %collective-permute-start.4 = (f32[512,128]{1,0:T(8,128)S(1)}, f32[512,128]{1,0:T(8,128)S(1)}, u32[]{:S(2)}, u32[]{:S(2)}) collective-permute-start(f32[512,128]{1,0:T(8,128)S(1)} %get-tuple-element.51), channel_id=1, source_target_pairs={{0,1},{1,0},{2,3},{3,2},{4,8},{5,9},{6,10},{7,11},{8,4},{9,5},{10,... | collective-permute-start | bytes 786440 | tf_op jit(solution)/shard_map/ppermute | solution.py:709
  7.0 0.0 collective-permute-start
  7.0 2.0 %collective-permute-start.1 = (f32[272,128]{1,0:T(8,128)S(1)}, f32[272,128]{1,0:T(8,128)S(1)}, u32[]{:S(2)}, u32[]{:S(2)}) collective-permute-start(f32[272,128]{1,0:T(8,128)S(1)} %get-tuple-element.45), channel_id=1, source_target_pairs={{0,1},{1,0},{2,3},{3,2},{4,9},{5,8},{6,11},{7,10},{8,5},{9,4},{10,... | collective-permute-start | bytes 417800 | tf_op jit(solution)/shard_map/ppermute | solution.py:709
  9.0 0.8 %collective-permute-start.2 = (f32[272,128]{1,0:T(8,128)S(1)}, f32[272,128]{1,0:T(8,128)S(1)}, u32[]{:S(2)}, u32[]{:S(2)}) collective-permute-start(f32[272,128]{1,0:T(8,128)S(1)} %get-tuple-element.46), channel_id=1, source_target_pairs={{0,28},{1,2},{2,1},{3,31},{4,8},{5,10},{6,9},{7,11},{8,4},{9,6},{1... | collective-permute-start | bytes 417800 | tf_op jit(solution)/shard_map/ppermute | solution.py:709
  9.8 10.2 %collective-permute-done.1.rest_2_ = f32[272,128]{1,0:T(8,128)S(1)} collective-permute-done((f32[272,128]{1,0:T(8,128)S(1)}, f32[272,128]{1,0:T(8,128)S(1)}, u32[]{:S(2)}, u32[]{:S(2)}) %collective-permute-start.1) | collective-permute-done | bytes 139296 | tf_op jit(solution)/shard_map/ppermute | solution.py:709
  19.9 0.0 collective-permute-done.2.rest_3_
  19.9 0.0 collective-permute-done.4.rest_4_
  20.0 0.5 collective-permute-start.6
  20.5 0.1 collective-permute-start.5
  20.5 1.3 %collective-permute-done.6.rest_6_ = f32[512,128]{1,0:T(8,128)S(1)} collective-permute-done((f32[512,128]{1,0:T(8,128)S(1)}, f32[512,128]{1,0:T(8,128)S(1)}, u32[]{:S(2)}, u32[]{:S(2)}) %collective-permute-start.6) | collective-permute-done | bytes 262176 | tf_op jit(solution)/shard_map/ppermute | solution.py:709
  21.8 0.4 collective-permute-done.5.rest_5_
  22.2 2.4 %shard_map.104 = (f32[13,104,128]{2,1,0:T(8,128)S(1)}, f32[13,104,128]{2,1,0:T(8,128)S(1)}, f32[17,136,128]{2,1,0:T(8,128)S(1)}, f32[10,16,128]{2,1,0:T(8,128)S(...) custom-call(bf16[240,256]{1,0:T(8,128)(2,1)S(1)} %copy-done, ...), custom_call_target="tpu_custom_call" | custom-call | tf_op jit(solution)/shard_map/pallas_call | solution.py:678
  24.7 0.2 collective-permute-start.11
  24.9 2.3 %collective-permute-start.12 = (f32[336,128]{1,0:T(8,128)S(1)}, f32[336,128]{1,0:T(8,128)S(1)}, u32[]{:S(2)}, u32[]{:S(2)}) collective-permute-start(f32[336,128]{1,0:T(8,128)S(1)} %get-tuple-element.69), channel_id=1, source_target_pairs={{0,1},{1,0},{2,3},{3,2},{4,8},{5,9},{6,10},{7,11},{8,4},{9,5},{10,... | collective-permute-start | bytes 516104 | tf_op jit(solution)/shard_map/ppermute | solution.py:709
  27.2 0.0 collective-permute-start.8
  27.2 2.0 %collective-permute-start.9 = (f32[312,128]{1,0:T(8,128)S(1)}, f32[312,128]{1,0:T(8,128)S(1)}, u32[]{:S(2)}, u32[]{:S(2)}) collective-permute-start(f32[312,128]{1,0:T(8,128)S(1)} %get-tuple-element.63), channel_id=1, source_target_pairs={{0,1},{1,0},{2,3},{3,2},{4,9},{5,8},{6,11},{7,10},{8,5},{9,4},{10,... | collective-permute-start | bytes 479240 | tf_op jit(solution)/shard_map/ppermute | solution.py:709
  29.2 0.0 collective-permute-start.10
  29.2 8.5 %collective-permute-done.9.rest_2_ = f32[312,128]{1,0:T(8,128)S(1)} collective-permute-done((f32[312,128]{1,0:T(8,128)S(1)}, f32[312,128]{1,0:T(8,128)S(1)}, u32[]{:S(2)}, u32[]{:S(2)}) %collective-permute-start.9) | collective-permute-done | bytes 159776 | tf_op jit(solution)/shard_map/ppermute | solution.py:709
  37.7 0.0 collective-permute-done.10.rest_3_
  37.7 0.0 collective-permute-done.11.rest_1_
  37.7 0.5 collective-permute-start.14
  38.2 0.1 collective-permute-start.13
  38.3 1.0 %collective-permute-done.14.rest_6_ = f32[336,128]{1,0:T(8,128)S(1)} collective-permute-done((f32[336,128]{1,0:T(8,128)S(1)}, f32[336,128]{1,0:T(8,128)S(1)}, u32[]{:S(2)}, u32[]{:S(2)}) %collective-permute-start.14) | collective-permute-done | bytes 172064 | tf_op jit(solution)/shard_map/ppermute | solution.py:709
  39.4 0.3 collective-permute-done.13.rest_5_
  39.6 4.9 %shard_map.105 = (f32[13,104,128]{2,1,0:T(8,128)S(1)}, f32[13,104,128]{2,1,0:T(8,128)S(1)}, f32[13,104,128]{2,1,0:T(8,128)S(1)}, f32[32,128]{1,0:T(8,128)S(1)}) custom-call(bf16[240,256]{1,0:T(8,128)(2,1)S(1)} %copy-done, f32[8,64,128]{2,1,0:T(8,128)S(1)} %get-tuple-element.55.z1_own, f32[17,136,128]{2,1,0:T(8,128)S(1)} %get-tuple-element.56.dinv, ...), custom_call_target="tpu_custom_call" | custom-call | tf_op jit(solution)/shard_map/pallas_call | solution.py:678
  44.5 12.6 %all_to_all.11 = f32[32,1,128]{2,1,0:T(1,128)S(1)} all-to-all(f32[32,1,128]{2,1,0:T(1,128)S(1)} %bitcast.11), channel_id=1, replica_groups=mesh['sx'=8,'sy'=4] {'sx','sy'}, dimensions={0} | all-to-all | bytes 32768 | tf_op jit(solution)/shard_map/all_to_all | solution.py:771
  57.1 2.1 %shard_map.106 = (f32[3,8,8,256]{3,2,1,0:T(8,128)}, f32[4,4,128]{2,1,0:T(4,128)}, f32[1,128]{1,0:T(1,128)}) custom-call(bf16[240,256]{1,0:T(8,128)(2,1)S(1)} %copy-done, f32[32,128]{1,0:T(8,128)S(1)} %bitcast.10, f32[13,104,128]{2,1,0:T(8,128)S(1)} %get-tuple-element.61.u_ref, f32[13,104,128]{2,1,0:T(8,128)S(1)} %get-tuple-element.60.z0_ref, ...), custom_call_target="tpu_custom_call" | custom-call | tf_op jit(solution)/shard_map/pallas_call | solution.py:678
  (10 shorter events, 0.0 us)
Async XLA Ops:
  0.6 21.6 %copy-start = (bf16[240,256]{1,0:T(8,128)(2,1)S(1)}, bf16[240,256]{1,0:T(8,128)(2,1)}, u32[]{:S(2)}) copy-start(bf16[240,256]{1,0:T(8,128)(2,1)} %constant.8.clone.matrix) | copy-start | bytes 368644
  0.6 21.6 %copy-start.1 = (f32[4,8,128]{2,1,0:T(8,128)S(1)}, f32[4,8,128]{2,1,0:T(8,128)}, u32[]{:S(2)}) copy-start(f32[4,8,128]{2,1,0:T(8,128)} %constant.9.clone.diag) | copy-start | bytes 49156
  2.3 17.6 %collective-permute-start.3 = (f32[512,128]{1,0:T(8,128)S(1)}, f32[512,128]{1,0:T(8,128)S(1)}, u32[]{:S(2)}, u32[]{:S(2)}) collective-permute-start(f32[512,128]{1,0:T(8,128)S(1)} %get-tuple-element.47), channel_id=1, source_target_pairs={{0,4},{1,2},{2,1},{3,7},{4,0},{5,6},{6,5},{7,3},{8,12},{9,10},{10,... | collective-permute-start | bytes 786440 | tf_op jit(solution)/shard_map/ppermute | solution.py:709
  2.8 17.1 %collective-permute-start.4 = (f32[512,128]{1,0:T(8,128)S(1)}, f32[512,128]{1,0:T(8,128)S(1)}, u32[]{:S(2)}, u32[]{:S(2)}) collective-permute-start(f32[512,128]{1,0:T(8,128)S(1)} %get-tuple-element.51), channel_id=1, source_target_pairs={{0,1},{1,0},{2,3},{3,2},{4,8},{5,9},{6,10},{7,11},{8,4},{9,5},{10,... | collective-permute-start | bytes 786440 | tf_op jit(solution)/shard_map/ppermute | solution.py:709
  7.0 13.0 %collective-permute-start = (f32[512,128]{1,0:T(8,128)S(1)}, f32[512,128]{1,0:T(8,128)S(1)}, u32[]{:S(2)}, u32[]{:S(2)}) collective-permute-start(f32[512,128]{1,0:T(8,128)S(1)} %get-tuple-element.44), channel_id=1, source_target_pairs={{0,1},{1,0},{2,3},{3,2},{4,5},{5,4},{6,7},{7,6},{8,9},{9,8},{10,11... | collective-permute-start | bytes 786440 | tf_op jit(solution)/shard_map/ppermute | solution.py:709
  7.0 12.9 %collective-permute-start.1 = (f32[272,128]{1,0:T(8,128)S(1)}, f32[272,128]{1,0:T(8,128)S(1)}, u32[]{:S(2)}, u32[]{:S(2)}) collective-permute-start(f32[272,128]{1,0:T(8,128)S(1)} %get-tuple-element.45), channel_id=1, source_target_pairs={{0,1},{1,0},{2,3},{3,2},{4,9},{5,8},{6,11},{7,10},{8,5},{9,4},{10,... | collective-permute-start | bytes 417800 | tf_op jit(solution)/shard_map/ppermute | solution.py:709
  9.0 10.9 %collective-permute-start.2 = (f32[272,128]{1,0:T(8,128)S(1)}, f32[272,128]{1,0:T(8,128)S(1)}, u32[]{:S(2)}, u32[]{:S(2)}) collective-permute-start(f32[272,128]{1,0:T(8,128)S(1)} %get-tuple-element.46), channel_id=1, source_target_pairs={{0,28},{1,2},{2,1},{3,31},{4,8},{5,10},{6,9},{7,11},{8,4},{9,6},{1... | collective-permute-start | bytes 417800 | tf_op jit(solution)/shard_map/ppermute | solution.py:709
  19.9 1.9 %collective-permute-start.7 = (f32[512,128]{1,0:T(8,128)S(1)}, f32[512,128]{1,0:T(8,128)S(1)}, u32[]{:S(2)}, u32[]{:S(2)}) collective-permute-start(f32[512,128]{1,0:T(8,128)S(1)} %collective-permute-done.3.rest_1_), channel_id=1, source_target_pairs={{0,4},{1,5},{2,6},{3,7},{4,0},{5,1},{6,2},{7,3},{8,12},{9,13},{10,... | collective-permute-start | bytes 786440 | tf_op jit(solution)/shard_map/ppermute | solution.py:709
  20.0 1.9 %collective-permute-start.6 = (f32[512,128]{1,0:T(8,128)S(1)}, f32[512,128]{1,0:T(8,128)S(1)}, u32[]{:S(2)}, u32[]{:S(2)}) collective-permute-start(f32[512,128]{1,0:T(8,128)S(1)} %collective-permute-done.rest_0_), channel_id=1, source_target_pairs={{0,4},{1,5},{2,6},{3,7},{4,0},{5,1},{6,2},{7,3},{8,12},{9,13},{10,... | collective-permute-start | bytes 786440 | tf_op jit(solution)/shard_map/ppermute | solution.py:709
  20.5 1.8 %collective-permute-start.5 = (f32[512,128]{1,0:T(8,128)S(1)}, f32[512,128]{1,0:T(8,128)S(1)}, u32[]{:S(2)}, u32[]{:S(2)}) collective-permute-start(f32[512,128]{1,0:T(8,128)S(1)} %get-tuple-element.54), channel_id=1, source_target_pairs={{0,4},{1,5},{2,6},{3,7},{4,0},{5,1},{6,2},{7,3},{8,12},{9,13},{10,... | collective-permute-start | bytes 786440 | tf_op jit(solution)/shard_map/ppermute | solution.py:709
  24.7 13.0 %collective-permute-start.11 = (f32[336,128]{1,0:T(8,128)S(1)}, f32[336,128]{1,0:T(8,128)S(1)}, u32[]{:S(2)}, u32[]{:S(2)}) collective-permute-start(f32[336,128]{1,0:T(8,128)S(1)} %get-tuple-element.65), channel_id=1, source_target_pairs={{0,4},{1,2},{2,1},{3,7},{4,0},{5,6},{6,5},{7,3},{8,12},{9,10},{10,... | collective-permute-start | bytes 516104 | tf_op jit(solution)/shard_map/ppermute | solution.py:709
  24.9 12.8 %collective-permute-start.12 = (f32[336,128]{1,0:T(8,128)S(1)}, f32[336,128]{1,0:T(8,128)S(1)}, u32[]{:S(2)}, u32[]{:S(2)}) collective-permute-start(f32[336,128]{1,0:T(8,128)S(1)} %get-tuple-element.69), channel_id=1, source_target_pairs={{0,1},{1,0},{2,3},{3,2},{4,8},{5,9},{6,10},{7,11},{8,4},{9,5},{10,... | collective-permute-start | bytes 516104 | tf_op jit(solution)/shard_map/ppermute | solution.py:709
  27.2 10.5 %collective-permute-start.8 = (f32[336,128]{1,0:T(8,128)S(1)}, f32[336,128]{1,0:T(8,128)S(1)}, u32[]{:S(2)}, u32[]{:S(2)}) collective-permute-start(f32[336,128]{1,0:T(8,128)S(1)} %get-tuple-element.62), channel_id=1, source_target_pairs={{0,1},{1,0},{2,3},{3,2},{4,5},{5,4},{6,7},{7,6},{8,9},{9,8},{10,11... | collective-permute-start | bytes 516104 | tf_op jit(solution)/shard_map/ppermute | solution.py:709
  27.2 10.5 %collective-permute-start.9 = (f32[312,128]{1,0:T(8,128)S(1)}, f32[312,128]{1,0:T(8,128)S(1)}, u32[]{:S(2)}, u32[]{:S(2)}) collective-permute-start(f32[312,128]{1,0:T(8,128)S(1)} %get-tuple-element.63), channel_id=1, source_target_pairs={{0,1},{1,0},{2,3},{3,2},{4,9},{5,8},{6,11},{7,10},{8,5},{9,4},{10,... | collective-permute-start | bytes 479240 | tf_op jit(solution)/shard_map/ppermute | solution.py:709
  29.2 8.5 %collective-permute-start.10 = (f32[312,128]{1,0:T(8,128)S(1)}, f32[312,128]{1,0:T(8,128)S(1)}, u32[]{:S(2)}, u32[]{:S(2)}) collective-permute-start(f32[312,128]{1,0:T(8,128)S(1)} %get-tuple-element.64), channel_id=1, source_target_pairs={{0,28},{1,2},{2,1},{3,31},{4,8},{5,10},{6,9},{7,11},{8,4},{9,6},{1... | collective-permute-start | bytes 479240 | tf_op jit(solution)/shard_map/ppermute | solution.py:709
  37.7 1.7 %collective-permute-start.15 = (f32[336,128]{1,0:T(8,128)S(1)}, f32[336,128]{1,0:T(8,128)S(1)}, u32[]{:S(2)}, u32[]{:S(2)}) collective-permute-start(f32[336,128]{1,0:T(8,128)S(1)} %collective-permute-done.11.rest_1_), channel_id=1, source_target_pairs={{0,4},{1,5},{2,6},{3,7},{4,0},{5,1},{6,2},{7,3},{8,12},{9,13},{10,... | collective-permute-start | bytes 516104 | tf_op jit(solution)/shard_map/ppermute | solution.py:709
  37.7 1.6 %collective-permute-start.14 = (f32[336,128]{1,0:T(8,128)S(1)}, f32[336,128]{1,0:T(8,128)S(1)}, u32[]{:S(2)}, u32[]{:S(2)}) collective-permute-start(f32[336,128]{1,0:T(8,128)S(1)} %collective-permute-done.8.rest_0_), channel_id=1, source_target_pairs={{0,4},{1,5},{2,6},{3,7},{4,0},{5,1},{6,2},{7,3},{8,12},{9,13},{10,... | collective-permute-start | bytes 516104 | tf_op jit(solution)/shard_map/ppermute | solution.py:709
  38.2 1.4 %collective-permute-start.13 = (f32[336,128]{1,0:T(8,128)S(1)}, f32[336,128]{1,0:T(8,128)S(1)}, u32[]{:S(2)}, u32[]{:S(2)}) collective-permute-start(f32[336,128]{1,0:T(8,128)S(1)} %get-tuple-element.72), channel_id=1, source_target_pairs={{0,4},{1,5},{2,6},{3,7},{4,0},{5,1},{6,2},{7,3},{8,12},{9,13},{10,... | collective-permute-start | bytes 516104 | tf_op jit(solution)/shard_map/ppermute | solution.py:709

commit v5 on v4

--- a/solution.py
+++ b/solution.py
@@ -86,12 +86,30 @@
                             strain[5, 54 + node] = grad_x
                 factor = weights[first] * weights[second] * weights[third] * 0.125
                 stiff = stiff + factor * strain.T @ elastic @ strain
-    return stiff.astype(np.float32)
+    return stiff
+
+
+def balanced_parts(stiff):
+    hi = stiff.astype(BF16).astype(np.float64)
+    lo = (stiff - hi).astype(BF16).astype(np.float64)
+    unit = 2.0 ** (np.floor(np.log2(np.maximum(np.abs(lo), 1e-30))) - 7)
+    left = (hi + lo).reshape(81, 3, 27).sum(axis=2)
+    moved = np.zeros((81, 81))
+    for _ in range(6):
+        for i in range(81):
+            for j in range(i):
+                first, second = left[i, j // 27], left[j, i // 27]
+                step = np.clip(np.round(-(first + second) / 2 / unit[i, j]), -1 - moved[i, j], 1 - moved[i, j])
+                if step and lo[i, j]:
+                    moved[i, j] += step
+                    left[i, j // 27] += step * unit[i, j]
+                    left[j, i // 27] += step * unit[i, j]
+    moved = moved + moved.T
+    return hi.astype(np.float32), (lo + moved * unit).astype(np.float32)
 
 
 def operator_matrix(stiff):
-    hi = stiff.astype(BF16).astype(np.float32)
-    lo = stiff - hi
+    hi, lo = balanced_parts(stiff)
     out = np.zeros((240, 256), np.float32)
 
     def out_row(comp, a, b, c):
@@ -111,6 +129,7 @@
             out[row, in_row(*second, 0)] = hi[i, j]
             out[row, in_row(*second, 1)] = hi[i, j]
             out[row + 40, in_row(*second, 0)] = lo[i, j]
+            out[row + 40, in_row(*second, 1)] = lo[i, j]
     return out.astype(BF16)
 
 
@@ -363,7 +382,7 @@
 def first_kernel(matrix, diag, u_own, f_own, *rest):
     flags = position()
     received, rest = rest[:8], rest[8:]
-    (z0_ref, u_ref, dinv, young, factor, w0_ref, w1_ref, z1_ref), rest = rest[:8], rest[8:]
+    (z0_ref, u_ref, dinv, young, factor, v0_ref, g0_ref, z1_ref), rest = rest[:8], rest[8:]
     sends, (u_reg, f_reg, s_ref, t_ref, w_ref, o_ref) = rest[:6], rest[6:]
     u_reg[OWN : 2 * OWN, 8 * HALO_U : 8 * (HALO_U + OWN), :] = u_own[...]
     f_reg[OWN : 2 * OWN, 8 * HALO_F : 8 * (HALO_F + OWN), :] = f_own[...]
@@ -421,7 +440,7 @@
         store_columns(u_ref, x, load_columns(u_reg, x + 6, 3, 13))
 
         if 2 <= x < 10:
-            store_columns(w0_ref, x - 2, jnp.where(inv > 0.0, res, 0.0)[2:10])
+            store_columns(v0_ref, x - 2, jnp.where(inv > 0.0, res, 0.0)[2:10])
 
     for x in range(13):
         residual(x)
@@ -437,7 +456,7 @@
         image = collect(w_ref, o_ref, x + 2, 2, 8)
         inv = load_columns(dinv, x + 4, 4, 8)
         image = SHIFTS[0] * jnp.where(inv > 0.0, image, 0.0)
-        store_columns(w1_ref, x, load_columns(w0_ref, x, 0, 8) - image)
+        store_columns(g0_ref, x, image)
         store_columns(z1_ref, x, load_columns(z0_ref, x + 2, 2, 8) - inv * image)
 
     for x in range(OWN):
@@ -450,10 +469,10 @@
         send[...] = dense(cols.reshape(-1, 8, 128))
 
 
-def second_kernel(matrix, z1_own, dinv, young, w0_ref, w1_ref, z0_ref, u_ref, f_own, *rest):
+def second_kernel(matrix, z1_own, dinv, young, v0_ref, g0_ref, z0_ref, u_ref, f_own, *rest):
     received, rest = rest[:8], rest[8:]
     (z1_ref, z2_ref, z3_ref, sums_ref), rest = rest[:4], rest[4:]
-    z_reg, s_ref, t_ref, w_ref, o_ref, w2_ref, w3_ref = rest
+    z_reg, s_ref, t_ref, w_ref, o_ref, g1_ref, g2_ref = rest
     flags = position()
     z_reg[OWN : 2 * OWN, 8 * HALO_Z : 8 * (HALO_Z + OWN), :] = z1_own[...]
     for index, value in enumerate(received):
@@ -486,7 +505,7 @@
             store_columns(z2_ref, x - 2, z2[2:15])
 
         if 4 <= x < 12:
-            store_columns(w2_ref, x - 4, load_columns(w1_ref, x - 4, 0, 8) - image[4:12])
+            store_columns(g1_ref, x - 4, image[4:12])
 
     for x in range(17):
         image_2(x)
@@ -501,7 +520,7 @@
         store_columns(z3_ref, x, z3)
 
         if 2 <= x < 10:
-            store_columns(w3_ref, x - 2, load_columns(w2_ref, x - 2, 0, 8) - image[2:10])
+            store_columns(g2_ref, x - 2, image[2:10])
 
     for x in range(13):
         image_3(x)
@@ -510,14 +529,23 @@
 
     def dots(x):
         inv = load_columns(dinv, x + 4, 4, 8)
-        w = [load_columns(ref, x, 0, 8) for ref in (w0_ref, w1_ref, w2_ref, w3_ref)]
-        w.append(w[3] - SHIFTS[3] * jnp.where(inv > 0.0, collect(w_ref, o_ref, x + 2, 2, 8), 0.0))
-        z = [inv * value for value in w[:4]]
-        load = jnp.where(inv > 0.0, load_columns(f_own, x, 0, 8), 0.0)
-        u = load_columns(u_ref, x + 2, 2, 8)
-        for index, (first, second) in enumerate(dot_list()):
-            first = u if first is None else (w if first[0] == "w" else z)[first[1]]
-            second = load if second is None else w[second[1]]
+        v0 = load_columns(v0_ref, x, 0, 8)
+        last = SHIFTS[3] * jnp.where(inv > 0.0, collect(w_ref, o_ref, x + 2, 2, 8), 0.0)
+        vectors = {
+            "v": v0,
+            "u": load_columns(u_ref, x + 2, 2, 8),
+            "Au": jnp.where(inv > 0.0, load_columns(f_own, x, 0, 8), 0.0) - v0,
+            ("z", 0): load_columns(z0_ref, x + 2, 2, 8),
+            ("z", 1): load_columns(z1_own, x, 0, 8),
+            ("z", 2): load_columns(z2_ref, x + 2, 2, 8),
+            ("z", 3): load_columns(z3_ref, x + 2, 2, 8),
+            ("g", 0): load_columns(g0_ref, x, 0, 8),
+            ("g", 1): load_columns(g1_ref, x, 0, 8),
+            ("g", 2): load_columns(g2_ref, x, 0, 8),
+            ("g", 3): last,
+        }
+        for index, (one, other) in enumerate(dot_list()):
+            first, second = vectors[one], vectors[other]
             sums[index] += jnp.sum(first * second, axis=0)
 
     for x in range(OWN):
@@ -535,41 +563,46 @@
 
 
 def dot_list():
-    out = [(("w", i), ("w", j)) for i in range(5) for j in range(i, 5)]
-    out += [(None, None)] + [(("z", i), None) for i in range(4)]
-    out += [(None, ("w", j)) for j in range(5)]
-    out += [(("z", i), ("w", j)) for i in range(4) for j in range(i, 5)]
+    steps = range(SWEEPS)
+    out = [("v", ("g", j)) for j in steps]
+    out += [(("g", i), ("g", j)) for i in steps for j in steps if i <= j]
+    out += [("u", "Au")] + [(("z", i), "Au") for i in steps] + [("u", ("g", j)) for j in steps]
+    out += [(("z", i), ("g", j)) for i in steps for j in steps if i <= j]
     return out
 
 
 def step_sizes(total):
     place_of = {pair: index for index, pair in enumerate(dot_list())}
 
+    def dot(one, other):
+        return total(place_of[one, other])
+
     def gram(i, j):
-        return total(place_of[("w", min(i, j)), ("w", max(i, j))])
-
-    poly = [jnp.ones((1, 128), F32)]
-    coef = [jnp.zeros((1, 128), F32)] * SWEEPS
+        return dot(("g", min(i, j)), ("g", max(i, j)))
+
+    def work_of(i, j):
+        if i <= j:
+            return dot(("z", i), ("g", j))
+        return dot(("z", j), ("g", i)) * (SHIFTS[j] / SHIFTS[i])
+
+    taken = [jnp.zeros((1, 128), F32)] * SWEEPS
+    coef = list(taken)
     for sweep in range(SWEEPS):
-        scaled = [poly[i] / SHIFTS[i] for i in range(sweep + 1)]
-        image = [scaled[0]] + [scaled[i] - scaled[i - 1] for i in range(1, sweep + 1)] + [-scaled[sweep]]
-        times = [sum(gram(i, j) * image[j] for j in range(sweep + 2)) for i in range(sweep + 2)]
-        top = sum(poly[i] * times[i] for i in range(sweep + 1))
-        bottom = sum(image[i] * times[i] for i in range(sweep + 2))
+        known = range(sweep + 1)
+        part = [(taken[i - 1] if i else 1.0) - taken[i] for i in known]
+        image = [part[i] / SHIFTS[i] for i in known]
+        top = sum(
+            image[j] * (dot("v", ("g", j)) - sum(taken[i] * gram(i, j) for i in known)) for j in known
+        )
+        bottom = sum(image[j] * sum(image[i] * gram(i, j) for i in known) for j in known)
         omega = top / bottom
-        for i in range(sweep + 1):
-            coef[i] = coef[i] + omega * poly[i]
-        poly = [
-            (poly[i] if i <= sweep else 0.0) - omega * image[i] for i in range(sweep + 2)
-        ]
-    work = total(place_of[None, None])
+        for i in known:
+            coef[i] = coef[i] + omega * part[i]
+            taken[i] = taken[i] + omega * image[i]
+    work = dot("u", "Au")
     for i in range(SWEEPS):
-        work = work + coef[i] * total(place_of[("z", i), None])
-    for j in range(SWEEPS + 1):
-        part = total(place_of[None, ("w", j)])
-        for i in range(SWEEPS):
-            part = part + coef[i] * total(place_of[("z", min(i, j)), ("w", max(i, j))])
-        work = work - poly[j] * part
+        work = work + coef[i] * dot(("z", i), "Au") + taken[i] * dot("u", ("g", i))
+        work = work + coef[i] * sum(taken[j] * work_of(i, j) for j in range(SWEEPS))
     return coef, work
 
 
@@ -690,7 +723,7 @@
     devices = count_x * count_y
     stiff = element_matrix()
     matrix = jnp.asarray(operator_matrix(stiff))
-    diag = jnp.asarray(diagonal_columns(stiff))
+    diag = jnp.asarray(diagonal_columns(stiff.astype(np.float32)))
     zero = F32(0.0)
     none = (0, 0, 0)
     small = ((0, OWN - ELEMS, 0), (0, OWN - ELEMS, 0), (0, 128, 0))

time: 59.4 us -> 59.5 us (level)
  no operation moved by 1% of the time
where the time goes in v5:
time: 59.5 us; the launch traced here: 59.3 us
  waiting for transfers between devices  21.6 us (36%)
  starting transfers between devices  13.2 us (22%)
  blocking collectives  12.6 us (21%)
  Pallas kernels  9.99 us (17%)
  other arithmetic  1.2 us (2%)
  between operations  0.73 us (1%)
    ppermute x16, waiting for transfers between devices, send(): return lax.ppermute(value, ('sx', 'sy'), partners(part, count_x, count_y))  21.6 us
    ppermute x16, starting transfers between devices, send(): return lax.ppermute(value, ('sx', 'sy'), partners(part, count_x, count_y))  13.2 us
    all_to_all x1, blocking collectives, body(): sums = lax.all_to_all(sums, ('sx', 'sy'), 0, 0, tiled=True)  12.6 us
    pallas_call x4, Pallas kernels, call(): pl.pallas_call(kernel, out_shape=out_shape, in_specs=[spec] * len(operand...  9.99 us
    add x1, other arithmetic, body(): lax.pad(start_field, zero, ((0, 7, 0), none, none, none))  1.2 us
  transfers between devices with their start and end apart: 16, of which 6 were waited for; matrix products, arithmetic and copies ran while one was open for 0% of the time, Pallas kernels for 0%

profile of v5, /device:TPU:0, one launch (start us, length us, event | category | flops | bytes accessed | tf_op | source)
XLA Modules:
  0.0 59.3 jit_solution(8508484509578859544)
XLA Ops:
  0.6 0.0 copy-start
  0.6 0.0 copy-start.1
  0.7 1.2 %convert_add_fusion.fields = f32[10,8,8,256]{3,2,1,0:T(8,128)S(1)} fusion(s32[1,4,4,128]{3,2,1,0:T(4,128)} %bitcast.14, s32[1,8,8,256]{3,2,1,0:T(8,128)} %bitcast.12, s32[1,8,8,256]{3,2,1,0:T(8,128)} %bitcast.13, f32[1,4,4,128]{3,2,1,0:T(4,128)} %bitcast.15, f32[3,8,8,256]{3,2,1,0:T(8,128)} %param.8, f32[3,8,8,256]{3,2,1,0:T(8,128)} %param.11), kind=kLoop, calls=%fused_computation | loop fusion | flops 983040 | bytes 1196032 | tf_op jit(solution)/shard_map/add | solution.py:731
  1.9 0.4 shard_map.103
  2.3 0.5 collective-permute-start.3
  2.8 4.1 %collective-permute-start.4 = (f32[512,128]{1,0:T(8,128)S(1)}, f32[512,128]{1,0:T(8,128)S(1)}, u32[]{:S(2)}, u32[]{:S(2)}) collective-permute-start(f32[512,128]{1,0:T(8,128)S(1)} %get-tuple-element.51), channel_id=1, source_target_pairs={{0,1},{1,0},{2,3},{3,2},{4,8},{5,9},{6,10},{7,11},{8,4},{9,5},{10,... | collective-permute-start | bytes 786440 | tf_op jit(solution)/shard_map/ppermute | solution.py:742
  7.0 0.0 collective-permute-start
  7.0 2.0 %collective-permute-start.1 = (f32[272,128]{1,0:T(8,128)S(1)}, f32[272,128]{1,0:T(8,128)S(1)}, u32[]{:S(2)}, u32[]{:S(2)}) collective-permute-start(f32[272,128]{1,0:T(8,128)S(1)} %get-tuple-element.45), channel_id=1, source_target_pairs={{0,1},{1,0},{2,3},{3,2},{4,9},{5,8},{6,11},{7,10},{8,5},{9,4},{10,... | collective-permute-start | bytes 417800 | tf_op jit(solution)/shard_map/ppermute | solution.py:742
  9.0 0.8 %collective-permute-start.2 = (f32[272,128]{1,0:T(8,128)S(1)}, f32[272,128]{1,0:T(8,128)S(1)}, u32[]{:S(2)}, u32[]{:S(2)}) collective-permute-start(f32[272,128]{1,0:T(8,128)S(1)} %get-tuple-element.46), channel_id=1, source_target_pairs={{0,28},{1,2},{2,1},{3,31},{4,8},{5,10},{6,9},{7,11},{8,4},{9,6},{1... | collective-permute-start | bytes 417800 | tf_op jit(solution)/shard_map/ppermute | solution.py:742
  9.8 10.2 %collective-permute-done.1.rest_2_ = f32[272,128]{1,0:T(8,128)S(1)} collective-permute-done((f32[272,128]{1,0:T(8,128)S(1)}, f32[272,128]{1,0:T(8,128)S(1)}, u32[]{:S(2)}, u32[]{:S(2)}) %collective-permute-start.1) | collective-permute-done | bytes 139296 | tf_op jit(solution)/shard_map/ppermute | solution.py:742
  19.9 0.0 collective-permute-done.2.rest_3_
  19.9 0.0 collective-permute-done.4.rest_4_
  20.0 0.5 collective-permute-start.6
  20.5 0.1 collective-permute-start.5
  20.5 1.3 %collective-permute-done.6.rest_6_ = f32[512,128]{1,0:T(8,128)S(1)} collective-permute-done((f32[512,128]{1,0:T(8,128)S(1)}, f32[512,128]{1,0:T(8,128)S(1)}, u32[]{:S(2)}, u32[]{:S(2)}) %collective-permute-start.6) | collective-permute-done | bytes 262176 | tf_op jit(solution)/shard_map/ppermute | solution.py:742
  21.8 0.4 collective-permute-done.5.rest_5_
  22.2 2.4 %shard_map.104 = (f32[13,104,128]{2,1,0:T(8,128)S(1)}, f32[13,104,128]{2,1,0:T(8,128)S(1)}, f32[17,136,128]{2,1,0:T(8,128)S(1)}, f32[10,16,128]{2,1,0:T(8,128)S(...) custom-call(bf16[240,256]{1,0:T(8,128)(2,1)S(1)} %copy-done, ...), custom_call_target="tpu_custom_call" | custom-call | tf_op jit(solution)/shard_map/pallas_call | solution.py:711
  24.7 0.2 collective-permute-start.11
  24.9 2.3 %collective-permute-start.12 = (f32[336,128]{1,0:T(8,128)S(1)}, f32[336,128]{1,0:T(8,128)S(1)}, u32[]{:S(2)}, u32[]{:S(2)}) collective-permute-start(f32[336,128]{1,0:T(8,128)S(1)} %get-tuple-element.69), channel_id=1, source_target_pairs={{0,1},{1,0},{2,3},{3,2},{4,8},{5,9},{6,10},{7,11},{8,4},{9,5},{10,... | collective-permute-start | bytes 516104 | tf_op jit(solution)/shard_map/ppermute | solution.py:742
  27.2 0.0 collective-permute-start.8
  27.2 2.0 %collective-permute-start.9 = (f32[312,128]{1,0:T(8,128)S(1)}, f32[312,128]{1,0:T(8,128)S(1)}, u32[]{:S(2)}, u32[]{:S(2)}) collective-permute-start(f32[312,128]{1,0:T(8,128)S(1)} %get-tuple-element.63), channel_id=1, source_target_pairs={{0,1},{1,0},{2,3},{3,2},{4,9},{5,8},{6,11},{7,10},{8,5},{9,4},{10,... | collective-permute-start | bytes 479240 | tf_op jit(solution)/shard_map/ppermute | solution.py:742
  29.2 0.0 collective-permute-start.10
  29.2 8.5 %collective-permute-done.9.rest_2_ = f32[312,128]{1,0:T(8,128)S(1)} collective-permute-done((f32[312,128]{1,0:T(8,128)S(1)}, f32[312,128]{1,0:T(8,128)S(1)}, u32[]{:S(2)}, u32[]{:S(2)}) %collective-permute-start.9) | collective-permute-done | bytes 159776 | tf_op jit(solution)/shard_map/ppermute | solution.py:742
  37.7 0.0 collective-permute-done.10.rest_3_
  37.7 0.0 collective-permute-done.11.rest_1_
  37.7 0.5 collective-permute-start.14
  38.2 0.1 collective-permute-start.13
  38.3 1.0 %collective-permute-done.14.rest_6_ = f32[336,128]{1,0:T(8,128)S(1)} collective-permute-done((f32[336,128]{1,0:T(8,128)S(1)}, f32[336,128]{1,0:T(8,128)S(1)}, u32[]{:S(2)}, u32[]{:S(2)}) %collective-permute-start.14) | collective-permute-done | bytes 172064 | tf_op jit(solution)/shard_map/ppermute | solution.py:742
  39.4 0.3 collective-permute-done.13.rest_5_
  39.6 5.0 %shard_map.105 = (f32[13,104,128]{2,1,0:T(8,128)S(1)}, f32[13,104,128]{2,1,0:T(8,128)S(1)}, f32[13,104,128]{2,1,0:T(8,128)S(1)}, f32[32,128]{1,0:T(8,128)S(1)}) custom-call(bf16[240,256]{1,0:T(8,128)(2,1)S(1)} %copy-done, f32[8,64,128]{2,1,0:T(8,128)S(1)} %get-tuple-element.55.z1_own, f32[17,136,128]{2,1,0:T(8,128)S(1)} %get-tuple-element.56.dinv, ...), custom_call_target="tpu_custom_call" | custom-call | tf_op jit(solution)/shard_map/pallas_call | solution.py:711
  44.6 12.6 %all_to_all.11 = f32[32,1,128]{2,1,0:T(1,128)S(1)} all-to-all(f32[32,1,128]{2,1,0:T(1,128)S(1)} %bitcast.11), channel_id=1, replica_groups=mesh['sx'=8,'sy'=4] {'sx','sy'}, dimensions={0} | all-to-all | bytes 32768 | tf_op jit(solution)/shard_map/all_to_all | solution.py:804
  57.2 2.1 %shard_map.106 = (f32[3,8,8,256]{3,2,1,0:T(8,128)}, f32[4,4,128]{2,1,0:T(4,128)}, f32[1,128]{1,0:T(1,128)}) custom-call(bf16[240,256]{1,0:T(8,128)(2,1)S(1)} %copy-done, f32[32,128]{1,0:T(8,128)S(1)} %bitcast.10, f32[13,104,128]{2,1,0:T(8,128)S(1)} %get-tuple-element.61.u_ref, f32[13,104,128]{2,1,0:T(8,128)S(1)} %get-tuple-element.60.z0_ref, ...), custom_call_target="tpu_custom_call" | custom-call | tf_op jit(solution)/shard_map/pallas_call | solution.py:711
  (10 shorter events, 0.0 us)
Async XLA Ops:
  0.6 21.6 %copy-start = (bf16[240,256]{1,0:T(8,128)(2,1)S(1)}, bf16[240,256]{1,0:T(8,128)(2,1)}, u32[]{:S(2)}) copy-start(bf16[240,256]{1,0:T(8,128)(2,1)} %constant.8.clone.matrix) | copy-start | bytes 368644
  0.6 21.6 %copy-start.1 = (f32[4,8,128]{2,1,0:T(8,128)S(1)}, f32[4,8,128]{2,1,0:T(8,128)}, u32[]{:S(2)}) copy-start(f32[4,8,128]{2,1,0:T(8,128)} %constant.9.clone.diag) | copy-start | bytes 49156
  2.3 17.6 %collective-permute-start.3 = (f32[512,128]{1,0:T(8,128)S(1)}, f32[512,128]{1,0:T(8,128)S(1)}, u32[]{:S(2)}, u32[]{:S(2)}) collective-permute-start(f32[512,128]{1,0:T(8,128)S(1)} %get-tuple-element.47), channel_id=1, source_target_pairs={{0,4},{1,2},{2,1},{3,7},{4,0},{5,6},{6,5},{7,3},{8,12},{9,10},{10,... | collective-permute-start | bytes 786440 | tf_op jit(solution)/shard_map/ppermute | solution.py:742
  2.8 17.1 %collective-permute-start.4 = (f32[512,128]{1,0:T(8,128)S(1)}, f32[512,128]{1,0:T(8,128)S(1)}, u32[]{:S(2)}, u32[]{:S(2)}) collective-permute-start(f32[512,128]{1,0:T(8,128)S(1)} %get-tuple-element.51), channel_id=1, source_target_pairs={{0,1},{1,0},{2,3},{3,2},{4,8},{5,9},{6,10},{7,11},{8,4},{9,5},{10,... | collective-permute-start | bytes 786440 | tf_op jit(solution)/shard_map/ppermute | solution.py:742
  7.0 13.0 %collective-permute-start = (f32[512,128]{1,0:T(8,128)S(1)}, f32[512,128]{1,0:T(8,128)S(1)}, u32[]{:S(2)}, u32[]{:S(2)}) collective-permute-start(f32[512,128]{1,0:T(8,128)S(1)} %get-tuple-element.44), channel_id=1, source_target_pairs={{0,1},{1,0},{2,3},{3,2},{4,5},{5,4},{6,7},{7,6},{8,9},{9,8},{10,11... | collective-permute-start | bytes 786440 | tf_op jit(solution)/shard_map/ppermute | solution.py:742
  7.0 12.9 %collective-permute-start.1 = (f32[272,128]{1,0:T(8,128)S(1)}, f32[272,128]{1,0:T(8,128)S(1)}, u32[]{:S(2)}, u32[]{:S(2)}) collective-permute-start(f32[272,128]{1,0:T(8,128)S(1)} %get-tuple-element.45), channel_id=1, source_target_pairs={{0,1},{1,0},{2,3},{3,2},{4,9},{5,8},{6,11},{7,10},{8,5},{9,4},{10,... | collective-permute-start | bytes 417800 | tf_op jit(solution)/shard_map/ppermute | solution.py:742
  9.0 10.9 %collective-permute-start.2 = (f32[272,128]{1,0:T(8,128)S(1)}, f32[272,128]{1,0:T(8,128)S(1)}, u32[]{:S(2)}, u32[]{:S(2)}) collective-permute-start(f32[272,128]{1,0:T(8,128)S(1)} %get-tuple-element.46), channel_id=1, source_target_pairs={{0,28},{1,2},{2,1},{3,31},{4,8},{5,10},{6,9},{7,11},{8,4},{9,6},{1... | collective-permute-start | bytes 417800 | tf_op jit(solution)/shard_map/ppermute | solution.py:742
  19.9 1.9 %collective-permute-start.7 = (f32[512,128]{1,0:T(8,128)S(1)}, f32[512,128]{1,0:T(8,128)S(1)}, u32[]{:S(2)}, u32[]{:S(2)}) collective-permute-start(f32[512,128]{1,0:T(8,128)S(1)} %collective-permute-done.3.rest_1_), channel_id=1, source_target_pairs={{0,4},{1,5},{2,6},{3,7},{4,0},{5,1},{6,2},{7,3},{8,12},{9,13},{10,... | collective-permute-start | bytes 786440 | tf_op jit(solution)/shard_map/ppermute | solution.py:742
  20.0 1.9 %collective-permute-start.6 = (f32[512,128]{1,0:T(8,128)S(1)}, f32[512,128]{1,0:T(8,128)S(1)}, u32[]{:S(2)}, u32[]{:S(2)}) collective-permute-start(f32[512,128]{1,0:T(8,128)S(1)} %collective-permute-done.rest_0_), channel_id=1, source_target_pairs={{0,4},{1,5},{2,6},{3,7},{4,0},{5,1},{6,2},{7,3},{8,12},{9,13},{10,... | collective-permute-start | bytes 786440 | tf_op jit(solution)/shard_map/ppermute | solution.py:742
  20.5 1.8 %collective-permute-start.5 = (f32[512,128]{1,0:T(8,128)S(1)}, f32[512,128]{1,0:T(8,128)S(1)}, u32[]{:S(2)}, u32[]{:S(2)}) collective-permute-start(f32[512,128]{1,0:T(8,128)S(1)} %get-tuple-element.54), channel_id=1, source_target_pairs={{0,4},{1,5},{2,6},{3,7},{4,0},{5,1},{6,2},{7,3},{8,12},{9,13},{10,... | collective-permute-start | bytes 786440 | tf_op jit(solution)/shard_map/ppermute | solution.py:742
  24.7 13.0 %collective-permute-start.11 = (f32[336,128]{1,0:T(8,128)S(1)}, f32[336,128]{1,0:T(8,128)S(1)}, u32[]{:S(2)}, u32[]{:S(2)}) collective-permute-start(f32[336,128]{1,0:T(8,128)S(1)} %get-tuple-element.65), channel_id=1, source_target_pairs={{0,4},{1,2},{2,1},{3,7},{4,0},{5,6},{6,5},{7,3},{8,12},{9,10},{10,... | collective-permute-start | bytes 516104 | tf_op jit(solution)/shard_map/ppermute | solution.py:742
  24.9 12.8 %collective-permute-start.12 = (f32[336,128]{1,0:T(8,128)S(1)}, f32[336,128]{1,0:T(8,128)S(1)}, u32[]{:S(2)}, u32[]{:S(2)}) collective-permute-start(f32[336,128]{1,0:T(8,128)S(1)} %get-tuple-element.69), channel_id=1, source_target_pairs={{0,1},{1,0},{2,3},{3,2},{4,8},{5,9},{6,10},{7,11},{8,4},{9,5},{10,... | collective-permute-start | bytes 516104 | tf_op jit(solution)/shard_map/ppermute | solution.py:742
  27.2 10.5 %collective-permute-start.8 = (f32[336,128]{1,0:T(8,128)S(1)}, f32[336,128]{1,0:T(8,128)S(1)}, u32[]{:S(2)}, u32[]{:S(2)}) collective-permute-start(f32[336,128]{1,0:T(8,128)S(1)} %get-tuple-element.62), channel_id=1, source_target_pairs={{0,1},{1,0},{2,3},{3,2},{4,5},{5,4},{6,7},{7,6},{8,9},{9,8},{10,11... | collective-permute-start | bytes 516104 | tf_op jit(solution)/shard_map/ppermute | solution.py:742
  27.2 10.5 %collective-permute-start.9 = (f32[312,128]{1,0:T(8,128)S(1)}, f32[312,128]{1,0:T(8,128)S(1)}, u32[]{:S(2)}, u32[]{:S(2)}) collective-permute-start(f32[312,128]{1,0:T(8,128)S(1)} %get-tuple-element.63), channel_id=1, source_target_pairs={{0,1},{1,0},{2,3},{3,2},{4,9},{5,8},{6,11},{7,10},{8,5},{9,4},{10,... | collective-permute-start | bytes 479240 | tf_op jit(solution)/shard_map/ppermute | solution.py:742
  29.2 8.5 %collective-permute-start.10 = (f32[312,128]{1,0:T(8,128)S(1)}, f32[312,128]{1,0:T(8,128)S(1)}, u32[]{:S(2)}, u32[]{:S(2)}) collective-permute-start(f32[312,128]{1,0:T(8,128)S(1)} %get-tuple-element.64), channel_id=1, source_target_pairs={{0,28},{1,2},{2,1},{3,31},{4,8},{5,10},{6,9},{7,11},{8,4},{9,6},{1... | collective-permute-start | bytes 479240 | tf_op jit(solution)/shard_map/ppermute | solution.py:742
  37.7 1.7 %collective-permute-start.15 = (f32[336,128]{1,0:T(8,128)S(1)}, f32[336,128]{1,0:T(8,128)S(1)}, u32[]{:S(2)}, u32[]{:S(2)}) collective-permute-start(f32[336,128]{1,0:T(8,128)S(1)} %collective-permute-done.11.rest_1_), channel_id=1, source_target_pairs={{0,4},{1,5},{2,6},{3,7},{4,0},{5,1},{6,2},{7,3},{8,12},{9,13},{10,... | collective-permute-start | bytes 516104 | tf_op jit(solution)/shard_map/ppermute | solution.py:742
  37.7 1.6 %collective-permute-start.14 = (f32[336,128]{1,0:T(8,128)S(1)}, f32[336,128]{1,0:T(8,128)S(1)}, u32[]{:S(2)}, u32[]{:S(2)}) collective-permute-start(f32[336,128]{1,0:T(8,128)S(1)} %collective-permute-done.8.rest_0_), channel_id=1, source_target_pairs={{0,4},{1,5},{2,6},{3,7},{4,0},{5,1},{6,2},{7,3},{8,12},{9,13},{10,... | collective-permute-start | bytes 516104 | tf_op jit(solution)/shard_map/ppermute | solution.py:742
  38.2 1.4 %collective-permute-start.13 = (f32[336,128]{1,0:T(8,128)S(1)}, f32[336,128]{1,0:T(8,128)S(1)}, u32[]{:S(2)}, u32[]{:S(2)}) collective-permute-start(f32[336,128]{1,0:T(8,128)S(1)} %get-tuple-element.72), channel_id=1, source_target_pairs={{0,4},{1,5},{2,6},{3,7},{4,0},{5,1},{6,2},{7,3},{8,12},{9,13},{10,... | collective-permute-start | bytes 516104 | tf_op jit(solution)/shard_map/ppermute | solution.py:742

commit v6 on v5

--- a/solution.py
+++ b/solution.py
@@ -108,14 +108,17 @@
     return hi.astype(np.float32), (lo + moved * unit).astype(np.float32)
 
 
-def operator_matrix(stiff):
+def operator_matrix(stiff, size):
     hi, lo = balanced_parts(stiff)
-    out = np.zeros((240, 256), np.float32)
+    out = np.zeros((6 * size, 256), np.float32)
 
     def out_row(comp, a, b, c):
+        first = 2 * size * a
         if c < 2:
-            return 80 * a + b * 8 + c * 3 + comp
-        return 80 * a + 24 + (b // 2) * 8 + (b % 2) * 4 + comp
+            return first + b * 8 + c * 3 + comp
+        if b == 2 and size == 32:
+            return first + 6 + comp if comp < 2 else first + 27
+        return first + 24 + (b // 2) * 8 + (b % 2) * 4 + comp
 
     def in_row(comp, a, b, c, low):
         if c < 2:
@@ -128,8 +131,8 @@
             row = out_row(*first)
             out[row, in_row(*second, 0)] = hi[i, j]
             out[row, in_row(*second, 1)] = hi[i, j]
-            out[row + 40, in_row(*second, 0)] = lo[i, j]
-            out[row + 40, in_row(*second, 1)] = lo[i, j]
+            out[row + size, in_row(*second, 0)] = lo[i, j]
+            out[row + size, in_row(*second, 1)] = lo[i, j]
     return out.astype(BF16)
 
 
@@ -283,22 +286,22 @@
     return jnp.concatenate(pieces, axis=0)
 
 
-def products(matrix, s_ref, t_ref, x, j):
+def products(matrix, s_ref, t_ref, x, j, size):
     operand = jnp.concatenate(
         [element_operand(s_ref, t_ref, x, 2 * e, e) for e in (j, j + 1)], axis=1
     )
     out = jnp.dot(matrix, operand, preferred_element_type=F32)
-    layers = [out[r : r + 40] + out[r + 40 : r + 80] for r in range(0, matrix.shape[0], 80)]
+    layers = [out[r : r + size] + out[r + size : r + 2 * size] for r in range(0, matrix.shape[0], 2 * size)]
     return [[layer[:, :128] for layer in layers], [layer[:, 128:] for layer in layers]]
 
 
 def apply(matrix_ref, s_ref, t_ref, young_ref, w_ref, o_ref, count_x, pairs_y, young_at, last=(0,)):
     for i in range(count_x):
         layers = (2,) if i == 0 else last if i == count_x - 1 else (0, 1, 2)
-        matrix = matrix_ref[80 * layers[0] : 80 * (layers[-1] + 1), :]
+        matrix = matrix_ref[64 * layers[0] : 64 * (layers[-1] + 1), :]
         tails = [None] * 3
         for j in range(0, 2 * pairs_y, 2):
-            both = products(matrix, s_ref, t_ref, 2 * i, j)
+            both = products(matrix, s_ref, t_ref, 2 * i, j, 32)
             for e in range(2):
                 k = j + e
                 scale = young_ref[i + young_at, k + young_at : k + young_at + 1, :]
@@ -307,30 +310,31 @@
                     x = 2 * i + a
                     nodes, over = out[:16], out[24:32]
                     if tails[a] is not None:
-                        nodes = jnp.concatenate([nodes[:8] + tails[a][0], nodes[8:]], axis=0)
-                        over = over + tails[a][1]
+                        nodes = jnp.concatenate([nodes[:8] + tails[a], nodes[8:]], axis=0)
                     if a == 0:
                         nodes = nodes + w_ref[x, 16 * k : 16 * k + 16, :]
                         over = over + o_ref[x, 8 * k : 8 * k + 8, :]
                     w_ref[x, 16 * k : 16 * k + 16, :] = nodes
                     o_ref[x, 8 * k : 8 * k + 8, :] = over
-                    tails[a] = (out[16:24], out[32:40])
+                    tails[a] = out[16:24]
         k = 2 * pairs_y
         for a in layers:
             x = 2 * i + a
-            nodes, over = tails[a]
+            nodes = tails[a]
             if a == 0:
                 nodes = nodes + w_ref[x, 16 * k : 16 * k + 8, :]
-                over = over + o_ref[x, 8 * k : 8 * k + 8, :]
             w_ref[x, 16 * k : 16 * k + 8, :] = nodes
-            o_ref[x, 8 * k : 8 * k + 8, :] = over
 
 
 def collect(w_ref, o_ref, x, low, count):
     half = (count + 1) // 2
-    moved = pltpu.roll(o_ref[x, 4 * low : 4 * low + 8 * half, :], 1, 1)
+    over = o_ref[x, 4 * low - 8 : 4 * low + 8 * half, :].reshape(half + 1, 8, 128)
+    before = w_ref[x, 8 * low - 16 : 8 * low - 16 + 16 * half, :].reshape(half, 2, 8, 128)[:, 0]
+    row = iota(before.shape, 1)
+    third = jnp.where(row < 2, pltpu.roll(before, 2, 1), pltpu.roll(over[:-1], 7, 1))
+    moved = jnp.where(row < 3, over[1:] + third, over[1:])
+    moved = pltpu.roll(moved.reshape(half * 8, 128), 1, 1)
     moved = jnp.where(iota(moved.shape, 1) > 0, moved, 0.0).reshape(half, 8, 128)
-    row = iota(moved.shape, 1)
     even = jnp.where(row < 3, moved, 0.0)
     odd = jnp.where(row < 3, pltpu.roll(moved, 4, 1), 0.0)
     both = jnp.stack([even, odd], axis=1).reshape(2 * half, 8, 128)[:count]
@@ -630,7 +634,7 @@
 
     for i in range(6):
         for j in range(0, 6, 2):
-            both = products(matrix[...], s_ref, t_ref, 2 * i, j)
+            both = products(matrix[...], s_ref, t_ref, 2 * i, j, 40)
             for e in range(2):
                 k = j + e
                 acc = jnp.zeros((8, 128), F32)
@@ -722,7 +726,8 @@
     count_x, count_y = lax.axis_size("sx"), lax.axis_size("sy")
     devices = count_x * count_y
     stiff = element_matrix()
-    matrix = jnp.asarray(operator_matrix(stiff))
+    matrix = jnp.asarray(operator_matrix(stiff, 32))
+    wide = jnp.asarray(operator_matrix(stiff, 40))
     diag = jnp.asarray(diagonal_columns(stiff.astype(np.float32)))
     zero = F32(0.0)
     none = (0, 0, 0)
@@ -813,7 +818,7 @@
             pltpu.VMEM((13, 7 * 8, 128), F32),
             pltpu.VMEM((6, 8, 128), F32),
         ],
-        [matrix, sums, u0, z0, z1, z2, z3, factor],
+        [wide, sums, u0, z0, z1, z2, z3, factor],
     )
     return displacement, filtered, compliance[0, 0]
 

time: 59.5 us -> 58.7 us (0.987)
  Pallas kernels: 9.99 us -> 9.18 us
    pallas_call x4, Pallas kernels: 9.99 us -> 9.18 us  [call(): pl.pallas_call(kernel, out_shape=out_shape, in_specs=[spec] * len(operand...]
where the time goes in v6:
time: 58.7 us; the launch traced here: 58.5 us
  waiting for transfers between devices  21.6 us (37%)
  starting transfers between devices  13.2 us (22%)
  blocking collectives  12.6 us (21%)
  Pallas kernels  9.18 us (16%)
  other arithmetic  1.2 us (2%)
  between operations  0.73 us (1%)
    ppermute x16, waiting for transfers between devices, send(): return lax.ppermute(value, ('sx', 'sy'), partners(part, count_x, count_y))  21.6 us
    ppermute x16, starting transfers between devices, send(): return lax.ppermute(value, ('sx', 'sy'), partners(part, count_x, count_y))  13.2 us
    all_to_all x1, blocking collectives, body(): sums = lax.all_to_all(sums, ('sx', 'sy'), 0, 0, tiled=True)  12.6 us
    pallas_call x4, Pallas kernels, call(): pl.pallas_call(kernel, out_shape=out_shape, in_specs=[spec] * len(operand...  9.18 us
    add x1, other arithmetic, body(): lax.pad(start_field, zero, ((0, 7, 0), none, none, none))  1.2 us
  transfers between devices with their start and end apart: 16, of which 6 were waited for; matrix products, arithmetic and copies ran while one was open for 0% of the time, Pallas kernels for 0%

profile of v6, /device:TPU:0, one launch (start us, length us, event | category | flops | bytes accessed | tf_op | source)
XLA Modules:
  0.0 58.5 jit_solution(11536879052747409781)
XLA Ops:
  0.6 0.0 copy-start
  0.6 0.0 copy-start.2
  0.7 1.2 %convert_add_fusion.fields = f32[10,8,8,256]{3,2,1,0:T(8,128)S(1)} fusion(s32[1,4,4,128]{3,2,1,0:T(4,128)} %bitcast.14, s32[1,8,8,256]{3,2,1,0:T(8,128)} %bitcast.12, s32[1,8,8,256]{3,2,1,0:T(8,128)} %bitcast.13, f32[1,4,4,128]{3,2,1,0:T(4,128)} %bitcast.15, f32[3,8,8,256]{3,2,1,0:T(8,128)} %param.9, f32[3,8,8,256]{3,2,1,0:T(8,128)} %param.12), kind=kLoop, calls=%fused_computation | loop fusion | flops 983040 | bytes 1196032 | tf_op jit(solution)/shard_map/add | solution.py:736
  1.9 0.4 shard_map.112
  2.3 0.5 collective-permute-start.3
  2.8 4.1 %collective-permute-start.4 = (f32[512,128]{1,0:T(8,128)S(1)}, f32[512,128]{1,0:T(8,128)S(1)}, u32[]{:S(2)}, u32[]{:S(2)}) collective-permute-start(f32[512,128]{1,0:T(8,128)S(1)} %get-tuple-element.51), channel_id=1, source_target_pairs={{0,1},{1,0},{2,3},{3,2},{4,8},{5,9},{6,10},{7,11},{8,4},{9,5},{10,... | collective-permute-start | bytes 786440 | tf_op jit(solution)/shard_map/ppermute | solution.py:747
  7.0 0.0 collective-permute-start
  7.0 2.0 %collective-permute-start.1 = (f32[272,128]{1,0:T(8,128)S(1)}, f32[272,128]{1,0:T(8,128)S(1)}, u32[]{:S(2)}, u32[]{:S(2)}) collective-permute-start(f32[272,128]{1,0:T(8,128)S(1)} %get-tuple-element.45), channel_id=1, source_target_pairs={{0,1},{1,0},{2,3},{3,2},{4,9},{5,8},{6,11},{7,10},{8,5},{9,4},{10,... | collective-permute-start | bytes 417800 | tf_op jit(solution)/shard_map/ppermute | solution.py:747
  9.0 0.8 %collective-permute-start.2 = (f32[272,128]{1,0:T(8,128)S(1)}, f32[272,128]{1,0:T(8,128)S(1)}, u32[]{:S(2)}, u32[]{:S(2)}) collective-permute-start(f32[272,128]{1,0:T(8,128)S(1)} %get-tuple-element.46), channel_id=1, source_target_pairs={{0,28},{1,2},{2,1},{3,31},{4,8},{5,10},{6,9},{7,11},{8,4},{9,6},{1... | collective-permute-start | bytes 417800 | tf_op jit(solution)/shard_map/ppermute | solution.py:747
  9.8 10.2 %collective-permute-done.1.rest_2_ = f32[272,128]{1,0:T(8,128)S(1)} collective-permute-done((f32[272,128]{1,0:T(8,128)S(1)}, f32[272,128]{1,0:T(8,128)S(1)}, u32[]{:S(2)}, u32[]{:S(2)}) %collective-permute-start.1) | collective-permute-done | bytes 139296 | tf_op jit(solution)/shard_map/ppermute | solution.py:747
  19.9 0.0 collective-permute-done.2.rest_3_
  19.9 0.0 collective-permute-done.3.rest_1_
  19.9 0.0 collective-permute-start.7
  20.0 0.0 collective-permute-done.rest_0_
  20.0 0.5 collective-permute-start.6
  20.5 0.1 collective-permute-start.5
  20.5 1.3 %collective-permute-done.6.rest_6_ = f32[512,128]{1,0:T(8,128)S(1)} collective-permute-done((f32[512,128]{1,0:T(8,128)S(1)}, f32[512,128]{1,0:T(8,128)S(1)}, u32[]{:S(2)}, u32[]{:S(2)}) %collective-permute-start.6) | collective-permute-done | bytes 262176 | tf_op jit(solution)/shard_map/ppermute | solution.py:747
  21.9 0.4 collective-permute-done.5.rest_5_
  22.2 2.2 %shard_map.113 = (f32[13,104,128]{2,1,0:T(8,128)S(1)}, f32[13,104,128]{2,1,0:T(8,128)S(1)}, f32[17,136,128]{2,1,0:T(8,128)S(1)}, f32[10,16,128]{2,1,0:T(8,128)S(...) custom-call(bf16[192,256]{1,0:T(8,128)(2,1)S(1)} %copy-done, ...), custom_call_target="tpu_custom_call" | custom-call | tf_op jit(solution)/shard_map/pallas_call | solution.py:715
  24.4 0.2 collective-permute-start.11
  24.6 2.3 %collective-permute-start.12 = (f32[336,128]{1,0:T(8,128)S(1)}, f32[336,128]{1,0:T(8,128)S(1)}, u32[]{:S(2)}, u32[]{:S(2)}) collective-permute-start(f32[336,128]{1,0:T(8,128)S(1)} %get-tuple-element.69), channel_id=1, source_target_pairs={{0,1},{1,0},{2,3},{3,2},{4,8},{5,9},{6,10},{7,11},{8,4},{9,5},{10,... | collective-permute-start | bytes 516104 | tf_op jit(solution)/shard_map/ppermute | solution.py:747
  26.9 0.0 collective-permute-start.8
  27.0 2.0 %collective-permute-start.9 = (f32[312,128]{1,0:T(8,128)S(1)}, f32[312,128]{1,0:T(8,128)S(1)}, u32[]{:S(2)}, u32[]{:S(2)}) collective-permute-start(f32[312,128]{1,0:T(8,128)S(1)} %get-tuple-element.63), channel_id=1, source_target_pairs={{0,1},{1,0},{2,3},{3,2},{4,9},{5,8},{6,11},{7,10},{8,5},{9,4},{10,... | collective-permute-start | bytes 479240 | tf_op jit(solution)/shard_map/ppermute | solution.py:747
  29.0 0.0 collective-permute-start.10
  29.0 8.5 %collective-permute-done.9.rest_2_ = f32[312,128]{1,0:T(8,128)S(1)} collective-permute-done((f32[312,128]{1,0:T(8,128)S(1)}, f32[312,128]{1,0:T(8,128)S(1)}, u32[]{:S(2)}, u32[]{:S(2)}) %collective-permute-start.9) | collective-permute-done | bytes 159776 | tf_op jit(solution)/shard_map/ppermute | solution.py:747
  37.5 0.5 collective-permute-start.14
  38.0 0.1 collective-permute-start.13
  38.0 1.0 %collective-permute-done.14.rest_6_ = f32[336,128]{1,0:T(8,128)S(1)} collective-permute-done((f32[336,128]{1,0:T(8,128)S(1)}, f32[336,128]{1,0:T(8,128)S(1)}, u32[]{:S(2)}, u32[]{:S(2)}) %collective-permute-start.14) | collective-permute-done | bytes 172064 | tf_op jit(solution)/shard_map/ppermute | solution.py:747
  39.1 0.3 collective-permute-done.13.rest_5_
  39.4 4.5 %shard_map.114 = (f32[13,104,128]{2,1,0:T(8,128)S(1)}, f32[13,104,128]{2,1,0:T(8,128)S(1)}, f32[13,104,128]{2,1,0:T(8,128)S(1)}, f32[32,128]{1,0:T(8,128)S(1)}) custom-call(bf16[192,256]{1,0:T(8,128)(2,1)S(1)} %copy-done, f32[8,64,128]{2,1,0:T(8,128)S(1)} %get-tuple-element.55.z1_own, f32[17,136,128]{2,1,0:T(8,128)S(1)} %get-tuple-element.56.dinv, ...), custom_call_target="tpu_custom_call" | custom-call | tf_op jit(solution)/shard_map/pallas_call | solution.py:715
  43.9 12.6 %all_to_all.11 = f32[32,1,128]{2,1,0:T(1,128)S(1)} all-to-all(f32[32,1,128]{2,1,0:T(1,128)S(1)} %bitcast.11), channel_id=1, replica_groups=mesh['sx'=8,'sy'=4] {'sx','sy'}, dimensions={0} | all-to-all | bytes 32768 | tf_op jit(solution)/shard_map/all_to_all | solution.py:809
  56.4 2.1 %shard_map.115 = (f32[3,8,8,256]{3,2,1,0:T(8,128)}, f32[4,4,128]{2,1,0:T(4,128)}, f32[1,128]{1,0:T(1,128)}) custom-call(bf16[240,256]{1,0:T(8,128)(2,1)S(1)} %copy-done.1, f32[32,128]{1,0:T(8,128)S(1)} %bitcast.10, f32[13,104,128]{2,1,0:T(8,128)S(1)} %get-tuple-element.61.u_ref, f32[13,104,128]{2,1,0:T(8,128)S(1)} %get-tuple-element.60.z0_ref, ...), custom_call_target="tpu_custom_call" | custom-call | tf_op jit(solution)/shard_map/pallas_call | solution.py:715
  (12 shorter events, 0.0 us)
Async XLA Ops:
  0.6 21.6 %copy-start = (bf16[192,256]{1,0:T(8,128)(2,1)S(1)}, bf16[192,256]{1,0:T(8,128)(2,1)}, u32[]{:S(2)}) copy-start(bf16[192,256]{1,0:T(8,128)(2,1)} %constant.10.clone.matrix) | copy-start | bytes 294916
  0.6 21.6 %copy-start.2 = (f32[4,8,128]{2,1,0:T(8,128)S(1)}, f32[4,8,128]{2,1,0:T(8,128)}, u32[]{:S(2)}) copy-start(f32[4,8,128]{2,1,0:T(8,128)} %constant.12.clone.diag) | copy-start | bytes 49156
  2.3 17.6 %collective-permute-start.3 = (f32[512,128]{1,0:T(8,128)S(1)}, f32[512,128]{1,0:T(8,128)S(1)}, u32[]{:S(2)}, u32[]{:S(2)}) collective-permute-start(f32[512,128]{1,0:T(8,128)S(1)} %get-tuple-element.47), channel_id=1, source_target_pairs={{0,4},{1,2},{2,1},{3,7},{4,0},{5,6},{6,5},{7,3},{8,12},{9,10},{10,... | collective-permute-start | bytes 786440 | tf_op jit(solution)/shard_map/ppermute | solution.py:747
  2.8 17.1 %collective-permute-start.4 = (f32[512,128]{1,0:T(8,128)S(1)}, f32[512,128]{1,0:T(8,128)S(1)}, u32[]{:S(2)}, u32[]{:S(2)}) collective-permute-start(f32[512,128]{1,0:T(8,128)S(1)} %get-tuple-element.51), channel_id=1, source_target_pairs={{0,1},{1,0},{2,3},{3,2},{4,8},{5,9},{6,10},{7,11},{8,4},{9,5},{10,... | collective-permute-start | bytes 786440 | tf_op jit(solution)/shard_map/ppermute | solution.py:747
  7.0 13.0 %collective-permute-start = (f32[512,128]{1,0:T(8,128)S(1)}, f32[512,128]{1,0:T(8,128)S(1)}, u32[]{:S(2)}, u32[]{:S(2)}) collective-permute-start(f32[512,128]{1,0:T(8,128)S(1)} %get-tuple-element.44), channel_id=1, source_target_pairs={{0,1},{1,0},{2,3},{3,2},{4,5},{5,4},{6,7},{7,6},{8,9},{9,8},{10,11... | collective-permute-start | bytes 786440 | tf_op jit(solution)/shard_map/ppermute | solution.py:747
  7.0 12.9 %collective-permute-start.1 = (f32[272,128]{1,0:T(8,128)S(1)}, f32[272,128]{1,0:T(8,128)S(1)}, u32[]{:S(2)}, u32[]{:S(2)}) collective-permute-start(f32[272,128]{1,0:T(8,128)S(1)} %get-tuple-element.45), channel_id=1, source_target_pairs={{0,1},{1,0},{2,3},{3,2},{4,9},{5,8},{6,11},{7,10},{8,5},{9,4},{10,... | collective-permute-start | bytes 417800 | tf_op jit(solution)/shard_map/ppermute | solution.py:747
  9.0 10.9 %collective-permute-start.2 = (f32[272,128]{1,0:T(8,128)S(1)}, f32[272,128]{1,0:T(8,128)S(1)}, u32[]{:S(2)}, u32[]{:S(2)}) collective-permute-start(f32[272,128]{1,0:T(8,128)S(1)} %get-tuple-element.46), channel_id=1, source_target_pairs={{0,28},{1,2},{2,1},{3,31},{4,8},{5,10},{6,9},{7,11},{8,4},{9,6},{1... | collective-permute-start | bytes 417800 | tf_op jit(solution)/shard_map/ppermute | solution.py:747
  19.9 1.9 %collective-permute-start.7 = (f32[512,128]{1,0:T(8,128)S(1)}, f32[512,128]{1,0:T(8,128)S(1)}, u32[]{:S(2)}, u32[]{:S(2)}) collective-permute-start(f32[512,128]{1,0:T(8,128)S(1)} %collective-permute-done.3.rest_1_), channel_id=1, source_target_pairs={{0,4},{1,5},{2,6},{3,7},{4,0},{5,1},{6,2},{7,3},{8,12},{9,13},{10,... | collective-permute-start | bytes 786440 | tf_op jit(solution)/shard_map/ppermute | solution.py:747
  20.0 1.9 %collective-permute-start.6 = (f32[512,128]{1,0:T(8,128)S(1)}, f32[512,128]{1,0:T(8,128)S(1)}, u32[]{:S(2)}, u32[]{:S(2)}) collective-permute-start(f32[512,128]{1,0:T(8,128)S(1)} %collective-permute-done.rest_0_), channel_id=1, source_target_pairs={{0,4},{1,5},{2,6},{3,7},{4,0},{5,1},{6,2},{7,3},{8,12},{9,13},{10,... | collective-permute-start | bytes 786440 | tf_op jit(solution)/shard_map/ppermute | solution.py:747
  20.5 1.8 %collective-permute-start.5 = (f32[512,128]{1,0:T(8,128)S(1)}, f32[512,128]{1,0:T(8,128)S(1)}, u32[]{:S(2)}, u32[]{:S(2)}) collective-permute-start(f32[512,128]{1,0:T(8,128)S(1)} %get-tuple-element.54), channel_id=1, source_target_pairs={{0,4},{1,5},{2,6},{3,7},{4,0},{5,1},{6,2},{7,3},{8,12},{9,13},{10,... | collective-permute-start | bytes 786440 | tf_op jit(solution)/shard_map/ppermute | solution.py:747
  24.4 13.0 %collective-permute-start.11 = (f32[336,128]{1,0:T(8,128)S(1)}, f32[336,128]{1,0:T(8,128)S(1)}, u32[]{:S(2)}, u32[]{:S(2)}) collective-permute-start(f32[336,128]{1,0:T(8,128)S(1)} %get-tuple-element.65), channel_id=1, source_target_pairs={{0,4},{1,2},{2,1},{3,7},{4,0},{5,6},{6,5},{7,3},{8,12},{9,10},{10,... | collective-permute-start | bytes 516104 | tf_op jit(solution)/shard_map/ppermute | solution.py:747
  24.6 12.8 %collective-permute-start.12 = (f32[336,128]{1,0:T(8,128)S(1)}, f32[336,128]{1,0:T(8,128)S(1)}, u32[]{:S(2)}, u32[]{:S(2)}) collective-permute-start(f32[336,128]{1,0:T(8,128)S(1)} %get-tuple-element.69), channel_id=1, source_target_pairs={{0,1},{1,0},{2,3},{3,2},{4,8},{5,9},{6,10},{7,11},{8,4},{9,5},{10,... | collective-permute-start | bytes 516104 | tf_op jit(solution)/shard_map/ppermute | solution.py:747
  26.9 10.5 %collective-permute-start.8 = (f32[336,128]{1,0:T(8,128)S(1)}, f32[336,128]{1,0:T(8,128)S(1)}, u32[]{:S(2)}, u32[]{:S(2)}) collective-permute-start(f32[336,128]{1,0:T(8,128)S(1)} %get-tuple-element.62), channel_id=1, source_target_pairs={{0,1},{1,0},{2,3},{3,2},{4,5},{5,4},{6,7},{7,6},{8,9},{9,8},{10,11... | collective-permute-start | bytes 516104 | tf_op jit(solution)/shard_map/ppermute | solution.py:747
  27.0 10.5 %collective-permute-start.9 = (f32[312,128]{1,0:T(8,128)S(1)}, f32[312,128]{1,0:T(8,128)S(1)}, u32[]{:S(2)}, u32[]{:S(2)}) collective-permute-start(f32[312,128]{1,0:T(8,128)S(1)} %get-tuple-element.63), channel_id=1, source_target_pairs={{0,1},{1,0},{2,3},{3,2},{4,9},{5,8},{6,11},{7,10},{8,5},{9,4},{10,... | collective-permute-start | bytes 479240 | tf_op jit(solution)/shard_map/ppermute | solution.py:747
  29.0 8.5 %collective-permute-start.10 = (f32[312,128]{1,0:T(8,128)S(1)}, f32[312,128]{1,0:T(8,128)S(1)}, u32[]{:S(2)}, u32[]{:S(2)}) collective-permute-start(f32[312,128]{1,0:T(8,128)S(1)} %get-tuple-element.64), channel_id=1, source_target_pairs={{0,28},{1,2},{2,1},{3,31},{4,8},{5,10},{6,9},{7,11},{8,4},{9,6},{1... | collective-permute-start | bytes 479240 | tf_op jit(solution)/shard_map/ppermute | solution.py:747
  37.4 1.7 %collective-permute-start.15 = (f32[336,128]{1,0:T(8,128)S(1)}, f32[336,128]{1,0:T(8,128)S(1)}, u32[]{:S(2)}, u32[]{:S(2)}) collective-permute-start(f32[336,128]{1,0:T(8,128)S(1)} %collective-permute-done.11.rest_1_), channel_id=1, source_target_pairs={{0,4},{1,5},{2,6},{3,7},{4,0},{5,1},{6,2},{7,3},{8,12},{9,13},{10,... | collective-permute-start | bytes 516104 | tf_op jit(solution)/shard_map/ppermute | solution.py:747
  37.5 1.6 %collective-permute-start.14 = (f32[336,128]{1,0:T(8,128)S(1)}, f32[336,128]{1,0:T(8,128)S(1)}, u32[]{:S(2)}, u32[]{:S(2)}) collective-permute-start(f32[336,128]{1,0:T(8,128)S(1)} %collective-permute-done.8.rest_0_), channel_id=1, source_target_pairs={{0,4},{1,5},{2,6},{3,7},{4,0},{5,1},{6,2},{7,3},{8,12},{9,13},{10,... | collective-permute-start | bytes 516104 | tf_op jit(solution)/shard_map/ppermute | solution.py:747
  38.0 1.4 %collective-permute-start.13 = (f32[336,128]{1,0:T(8,128)S(1)}, f32[336,128]{1,0:T(8,128)S(1)}, u32[]{:S(2)}, u32[]{:S(2)}) collective-permute-start(f32[336,128]{1,0:T(8,128)S(1)} %get-tuple-element.72), channel_id=1, source_target_pairs={{0,4},{1,5},{2,6},{3,7},{4,0},{5,1},{6,2},{7,3},{8,12},{9,13},{10,... | collective-permute-start | bytes 516104 | tf_op jit(solution)/shard_map/ppermute | solution.py:747
  39.4 17.1 %copy-start.1 = (bf16[240,256]{1,0:T(8,128)(2,1)S(1)}, bf16[240,256]{1,0:T(8,128)(2,1)}, u32[]{:S(2)}) copy-start(bf16[240,256]{1,0:T(8,128)(2,1)} %constant.11.clone.matrix) | copy-start | bytes 368644
